TPU v7x, 32 devices: a whole 2x2x4 slice. The times are simulated.
32 devices in a mesh: seq: 8 (over y, x, core), rows: 4 (over z).
Axes of the slice: x: 2, y: 2, z: 4, core: 2. Of those that a mesh axis runs over, the one named last changes fastest.
Arguments:
- hidden: bfloat16 [16, 1024, 768], P('rows', 'seq'), may hold values from -6 to 6
- lengths: int32 [16, 4], P('rows'), may hold values from 1 to 1021, as said below
- cotangent: bfloat16 [16, 1024, 768], P('rows', 'seq'), may hold values from -6 to 6
- first_gain: float32 [768], replicated, may hold values from 0.1 to 1.9
- first_shift: float32 [768], replicated, may hold values from -1.75 to 1.75
- second_gain: float32 [768], replicated, may hold values from 0.1 to 1.9
- second_shift: float32 [768], replicated, may hold values from -1.75 to 1.75
- query_weight: bfloat16 [768, 768], replicated, may hold values from -0.21875 to 0.21875
- query_bias: float32 [768], replicated, may hold values from -3 to 3
- keyvalue_weight: bfloat16 [768, 128], replicated, may hold values from -0.21875 to 0.21875
- keyvalue_bias: float32 [128], replicated, may hold values from -3 to 3
- output_weight: bfloat16 [768, 768], replicated, may hold values from -0.875 to 0.875
- output_bias: float32 [768], replicated, may hold values from -3 to 3
- up_weight: bfloat16 [768, 3072], replicated, may hold values from -0.21875 to 0.21875
- up_bias: float32 [3072], replicated, may hold values from -3 to 3
- down_weight: bfloat16 [3072, 768], replicated, may hold values from -0.109375 to 0.109375
- down_bias: float32 [768], replicated, may hold values from -3 to 3
Outputs:
- layer_output: bfloat16 [16, 1024, 768], P('rows', 'seq')
- input_grad: bfloat16 [16, 1024, 768], P('rows', 'seq')
- grad_first_gain: float32 [768], replicated
- grad_first_shift: float32 [768], replicated
- grad_second_gain: float32 [768], replicated
- grad_second_shift: float32 [768], replicated
- grad_query_weight: float32 [768, 768], P('seq')
- grad_query_bias: float32 [768], replicated
- grad_keyvalue_weight: float32 [768, 128], P('seq')
- grad_keyvalue_bias: float32 [128], replicated
- grad_output_weight: float32 [768, 768], P('seq')
- grad_output_bias: float32 [768], replicated
- grad_up_weight: float32 [768, 3072], P('seq')
- grad_up_bias: float32 [3072], replicated
- grad_down_weight: float32 [3072, 768], P('seq')
- grad_down_bias: float32 [768], replicated
Inputs may be any that keep to these rules, and one draw needn't show every extreme that they name: `lengths`: each row has 4 documents of 1 or more positions that together fill its 1024 positions.
All inputs are finite; a program needn't handle non-finite values.
Results may differ from a plain program's by a relative error of at most 0.015.
Values may be sent and summed in bfloat16 or wider, within the bound.
A program may use at most 192 MiB of HBM per device.

v0:
```python
import jax
import jax.numpy as jnp
from jax import lax
from jax.sharding import PartitionSpec as P

HD = 64
ROT = 16


norm_eps = 1e-05


def layer_norm(values, gain, shift):
    centred = values - jnp.mean(values, axis=-1, keepdims=True)
    factor = lax.rsqrt(jnp.mean(centred * centred, axis=-1, keepdims=True) + norm_eps)
    return centred * factor * gain + shift


def both_norms(values, gain_one, shift_one, gain_two, shift_two):
    return (layer_norm(values, gain_one, shift_one), layer_norm(values, gain_two, shift_two))


def doc_layout(doc_lengths, row_len):
    ends = jnp.cumsum(doc_lengths, axis=-1)
    starts = ends - doc_lengths
    places = jnp.arange(row_len, dtype=jnp.int32)
    segment = jnp.sum((places[None, :, None] >= ends[:, None, :]).astype(jnp.int32), axis=-1)
    owners = (
        segment[:, :, None] == jnp.arange(doc_lengths.shape[-1], dtype=jnp.int32)[None, None, :]
    )
    begin = jnp.sum(jnp.where(owners, starts[:, None, :], 0), axis=-1)
    return (segment, places[None, :] - begin)


def rotary_tables(positions, rot_dims):
    half_dims = rot_dims // 2
    freqs = jnp.power(10000.0, -2.0 * jnp.arange(half_dims, dtype=jnp.float32) / rot_dims)
    angles = positions.astype(jnp.float32)[..., None] * freqs
    return (jnp.cos(angles), jnp.sin(angles))


def rotate(values, cosine, sine):
    half_dims = cosine.shape[-1]
    front = values[..., :half_dims]
    behind = values[..., half_dims : 2 * half_dims]
    remain = values[..., 2 * half_dims :]
    return jnp.concatenate(
        [front * cosine - behind * sine, behind * cosine + front * sine, remain], axis=-1
    )


def gelu_exact(values):
    return 0.5 * values * (1.0 + lax.erf(values * 0.7071067811865476))


def masked_scores(query_rot, row_kv, visible):
    block_len, head_count, head_size = query_rot.shape
    flat_queries = query_rot.reshape(block_len * head_count, head_size)
    scores = jnp.dot(flat_queries, row_kv[:, :head_size].T, preferred_element_type=jnp.float32)
    scores = scores.reshape(block_len, head_count, row_kv.shape[0]) * 0.125
    return jnp.where(visible[:, None, :], scores, -1e30)


def attend(operands):
    query_rot, row_kv, visible = operands
    block_len, head_count, head_size = query_rot.shape
    scores = masked_scores(query_rot, row_kv, visible)
    row_max = jnp.max(scores, axis=-1)
    expo = jnp.exp(scores - row_max[..., None])
    totals = jnp.sum(expo, axis=-1)
    probs_low = (expo / totals[..., None]).astype(jnp.bfloat16)
    mixed = jnp.dot(
        probs_low.reshape(block_len * head_count, -1),
        row_kv[:, head_size:],
        preferred_element_type=jnp.float32,
    )
    return (mixed.reshape(block_len, head_count * head_size), row_max + jnp.log(totals))


def attend_back(operands):
    query_rot, row_kv, visible, log_total, d_mixed = operands
    block_len, head_count, head_size = query_rot.shape
    scores = masked_scores(query_rot, row_kv, visible)
    probs = jnp.exp(scores - log_total[..., None])
    flat_grad = d_mixed.reshape(block_len * head_count, head_size)
    d_probs = jnp.dot(flat_grad, row_kv[:, head_size:].T, preferred_element_type=jnp.float32)
    d_probs = d_probs.reshape(probs.shape)
    d_scores = probs * (d_probs - jnp.sum(probs * d_probs, axis=-1, keepdims=True))
    d_scores = d_scores.astype(jnp.bfloat16).reshape(block_len * head_count, -1)
    probs_low = probs.astype(jnp.bfloat16).reshape(block_len * head_count, -1)
    d_query = jnp.dot(d_scores, row_kv[:, :head_size], preferred_element_type=jnp.float32) * 0.125
    d_key = (
        jnp.dot(
            d_scores.T,
            query_rot.reshape(block_len * head_count, head_size),
            preferred_element_type=jnp.float32,
        )
        * 0.125
    )
    d_value = jnp.dot(probs_low.T, flat_grad, preferred_element_type=jnp.float32)
    return (
        d_query.reshape(block_len, head_count, head_size),
        jnp.concatenate([d_key, d_value], axis=-1),
    )


def shards(
    hidden,
    lengths,
    cotangent,
    first_gain,
    first_shift,
    second_gain,
    second_shift,
    query_weight,
    query_bias,
    keyvalue_weight,
    keyvalue_bias,
    output_weight,
    output_bias,
    up_weight,
    up_bias,
    down_weight,
    down_bias,
):
    row_count, block_len, features = hidden.shape
    head_count = features // HD
    row_len = block_len * lax.axis_size("seq")
    tok_count = row_count * block_len
    block_start = lax.axis_index("seq") * block_len
    segment_all, positions_all = doc_layout(lengths, row_len)
    segment_own = lax.dynamic_slice_in_dim(segment_all, block_start, block_len, 1)
    positions_own = lax.dynamic_slice_in_dim(positions_all, block_start, block_len, 1)
    cosine, sine = rotary_tables(positions_own, ROT)
    query_places = block_start + jnp.arange(block_len, dtype=jnp.int32)
    key_places = jnp.arange(row_len, dtype=jnp.int32)
    visible = (key_places[None, None, :] <= query_places[None, :, None]) & (
        segment_all[:, None, :] == segment_own[:, :, None]
    )
    inputs = hidden.astype(jnp.float32).reshape(tok_count, features)
    (first_norm, second_norm), norm_back = jax.vjp(
        both_norms, inputs, first_gain, first_shift, second_gain, second_shift
    )
    first_low = first_norm.astype(jnp.bfloat16)
    second_low = second_norm.astype(jnp.bfloat16)
    queries = jnp.dot(first_low, query_weight, preferred_element_type=jnp.float32) + query_bias
    key_vals = (
        jnp.dot(first_low, keyvalue_weight, preferred_element_type=jnp.float32) + keyvalue_bias
    )
    query_rot = rotate(
        queries.reshape(row_count, block_len, head_count, HD),
        cosine[:, :, None, :],
        sine[:, :, None, :],
    ).astype(jnp.bfloat16)
    key_vals = key_vals.reshape(row_count, block_len, 2 * HD)
    key_rot = rotate(key_vals[..., :HD], cosine, sine)
    kv_low = jnp.concatenate([key_rot, key_vals[..., HD:]], axis=-1).astype(jnp.bfloat16)
    kv_full = lax.all_gather(kv_low, "seq", axis=1, tiled=True)
    mixed, log_total = lax.map(attend, (query_rot, kv_full, visible))
    mixed_low = mixed.reshape(tok_count, features).astype(jnp.bfloat16)
    attn_out = jnp.dot(mixed_low, output_weight, preferred_element_type=jnp.float32) + output_bias
    up_pre = jnp.dot(second_low, up_weight, preferred_element_type=jnp.float32) + up_bias
    act_full, gelu_back = jax.vjp(gelu_exact, up_pre)
    act_low = act_full.astype(jnp.bfloat16)
    ffn_out = jnp.dot(act_low, down_weight, preferred_element_type=jnp.float32) + down_bias
    layer_output = (
        (inputs + attn_out + ffn_out).astype(jnp.bfloat16).reshape(row_count, block_len, features)
    )
    grad_low = cotangent.reshape(tok_count, features)
    grad_full = grad_low.astype(jnp.float32)
    g_output_weight = jnp.dot(mixed_low.T, grad_low, preferred_element_type=jnp.float32)
    g_output_bias = jnp.sum(grad_full, axis=0)
    g_down_weight = jnp.dot(act_low.T, grad_low, preferred_element_type=jnp.float32)
    d_up = gelu_back(jnp.dot(grad_low, down_weight.T, preferred_element_type=jnp.float32))[
        0
    ].astype(jnp.bfloat16)
    g_up_weight = jnp.dot(second_low.T, d_up, preferred_element_type=jnp.float32)
    g_up_bias = jnp.sum(d_up.astype(jnp.float32), axis=0)
    second_grad = jnp.dot(d_up, up_weight.T, preferred_element_type=jnp.float32)
    d_mixed = jnp.dot(grad_low, output_weight.T, preferred_element_type=jnp.float32).astype(
        jnp.bfloat16
    )
    d_mixed = d_mixed.reshape(row_count, block_len, head_count, HD)
    d_query_rot, kv_terms = lax.map(attend_back, (query_rot, kv_full, visible, log_total, d_mixed))
    kv_own = lax.psum_scatter(kv_terms, "seq", scatter_dimension=1, tiled=True)
    d_key = rotate(kv_own[..., :HD], cosine, -sine)
    d_kv = (
        jnp.concatenate([d_key, kv_own[..., HD:]], axis=-1)
        .astype(jnp.bfloat16)
        .reshape(tok_count, 2 * HD)
    )
    d_query = (
        rotate(d_query_rot, cosine[:, :, None, :], -sine[:, :, None, :])
        .astype(jnp.bfloat16)
        .reshape(tok_count, features)
    )
    g_query_weight = jnp.dot(first_low.T, d_query, preferred_element_type=jnp.float32)
    g_query_bias = jnp.sum(d_query.astype(jnp.float32), axis=0)
    g_kv_weight = jnp.dot(first_low.T, d_kv, preferred_element_type=jnp.float32)
    g_kv_bias = jnp.sum(d_kv.astype(jnp.float32), axis=0)
    first_grad = jnp.dot(d_query, query_weight.T, preferred_element_type=jnp.float32)
    first_grad = first_grad + jnp.dot(d_kv, keyvalue_weight.T, preferred_element_type=jnp.float32)
    d_inputs, g_first_gain, g_first_shift, g_second_gain, g_second_shift = norm_back(
        (first_grad, second_grad)
    )
    input_grad = (grad_full + d_inputs).astype(jnp.bfloat16).reshape(row_count, block_len, features)
    part_query, part_kv, part_out, part_up, part_down = (
        lax.psum_scatter(
            g_query_weight.astype(jnp.bfloat16), "seq", scatter_dimension=0, tiled=True
        ).astype(jnp.float32),
        lax.psum_scatter(
            g_kv_weight.astype(jnp.bfloat16), "seq", scatter_dimension=0, tiled=True
        ).astype(jnp.float32),
        lax.psum_scatter(
            g_output_weight.astype(jnp.bfloat16), "seq", scatter_dimension=0, tiled=True
        ).astype(jnp.float32),
        lax.psum_scatter(
            g_up_weight.astype(jnp.bfloat16), "seq", scatter_dimension=0, tiled=True
        ).astype(jnp.float32),
        lax.psum_scatter(
            g_down_weight.astype(jnp.bfloat16), "seq", scatter_dimension=0, tiled=True
        ).astype(jnp.float32),
    )
    sum_query, sum_kv, sum_out, sum_up, sum_down = (
        lax.psum(part_query.astype(jnp.bfloat16), "rows").astype(jnp.float32),
        lax.psum(part_kv.astype(jnp.bfloat16), "rows").astype(jnp.float32),
        lax.psum(part_out.astype(jnp.bfloat16), "rows").astype(jnp.float32),
        lax.psum(part_up.astype(jnp.bfloat16), "rows").astype(jnp.float32),
        lax.psum(part_down.astype(jnp.bfloat16), "rows").astype(jnp.float32),
    )
    (
        s_first_gain,
        s_first_shift,
        s_second_gain,
        s_second_shift,
        s_query_bias,
        s_kv_bias,
        s_output_bias,
        s_up_bias,
    ) = lax.psum(
        (
            g_first_gain,
            g_first_shift,
            g_second_gain,
            g_second_shift,
            g_query_bias,
            g_kv_bias,
            g_output_bias,
            g_up_bias,
        ),
        ("seq", "rows"),
    )
    return (
        layer_output,
        input_grad,
        s_first_gain,
        s_first_shift,
        s_second_gain,
        s_second_shift,
        sum_query,
        s_query_bias,
        sum_kv,
        s_kv_bias,
        sum_out,
        s_output_bias,
        sum_up,
        s_up_bias,
        sum_down,
        s_output_bias,
    )


def solution(mesh):
    placed = (
        P("rows", "seq", None),
        P("rows", None),
        P("rows", "seq", None),
        P(),
        P(),
        P(),
        P(),
        P(),
        P(),
        P(),
        P(),
        P(),
        P(),
        P(),
        P(),
        P(),
        P(),
    )
    return jax.shard_map(
        shards,
        mesh=mesh,
        in_specs=placed,
        out_specs=(
            P("rows", "seq", None),
            P("rows", "seq", None),
            P(),
            P(),
            P(),
            P(),
            P("seq", None),
            P(),
            P("seq", None),
            P(),
            P("seq", None),
            P(),
            P("seq", None),
            P(),
            P("seq", None),
            P(),
        ),
        check_vma=False,
    )
```

profile of v0, /device:TPU:0, one launch (start us, length us, event | category | flops | bytes accessed | tf_op | source)
XLA Modules:
  0.0 686.1 jit_solution(5163011281018819129)
XLA Ops:
  31.0 12.7 %all-gather.2.cloned.1.call-done = bf16[4,1024,128]{1,2,0:T(8,128)(2,1)} async-done(((bf16[4,128,128]{1,2,0:T(8,128)(2,1)}), bf16[4,1024,128]{1,2,0:T(8,128)(2,1)}) %all-gather.2.cloned.1.call-update) | async-done | bytes 1048592 | tf_op jit(solution)/shard_map/all_gather | solution.py:158
  43.7 79.0 %while.24 = (s32[]{:T(128)}, bf16[4,128,768]{2,1,0:T(8,128)(2,1)}, f32[4,128,12]{1,2,0:T(8,128)}, pred[4,128,1024]{2,1,0:T(8,128)(4,1)S(1)}, bf16[4,128,12,64]{1...) while((s32[]{:T(128)}, bf16[4,128,768]{2,1,0:T(8,128)(2,1)}, f32[4,128,12]{1,2,0:T(8,128)}, ...), condition=%wide.region_8.9_spmd, body=%wide.region_5.8_spmd.sunk | while | flops 421526016 | bytes 40422488 | solution.py:159
  52.9 6.1 reshape.285
  92.4 6.1 reshape.285
  112.1 6.1 reshape.285
  122.7 204.8 %while.25 = (s32[]{:T(128)}, f32[4,128,12,64]{3,2,1,0:T(8,128)}, f32[4,1024,128]{1,2,0:T(8,128)}, pred[4,128,1024]{2,1,0:T(8,128)(4,1)S(1)}, bf16[4,128,12,64]{1...) while((s32[]{:T(128)}, f32[4,128,12,64]{3,2,1,0:T(8,128)}, ...), condition=%wide.region_13.14_spmd, body=%wide.region_11.13_spmd.sunk | while | flops 1230277120 | bytes 95196328 | solution.py:184
  132.1 10.1 %multiply_convert_fusion.3 = bf16[128,12,1024]{2,0,1:T(8,128)(2,1)} fusion(f32[128,12,1024]{2,0,1:T(8,128)} %get-tuple-element.323, f32[128,12]{0,1:T(8,128)S(1)} %dynamic-slice_bitcast_fusion.12, pred[128,1024]{1,0:T(8,128)(4,1)S(1)} %dynamic-slice_bitcast_fusion.13, bf16[1,128,12,64]{1,3,2,0:T(8,128)(2,1)S(1)} %copy.153, ...), kind=kOutput, calls=%fused_computation.17.clone.1 | convolution fusion | flops 418384384 | bytes 16662528 | tf_op jit(solution)/shard_map/while/body/eval_jaxpr/sub | solution.py:88
  183.3 10.2 %multiply_convert_fusion.3 = bf16[128,12,1024]{2,0,1:T(8,128)(2,1)} fusion(f32[128,12,1024]{2,0,1:T(8,128)} %get-tuple-element.323, f32[128,12]{0,1:T(8,128)S(1)} %dynamic-slice_bitcast_fusion.12, pred[128,1024]{1,0:T(8,128)(4,1)S(1)} %dynamic-slice_bitcast_fusion.13, bf16[1,128,12,64]{1,3,2,0:T(8,128)(2,1)S(1)} %copy.153, ...), kind=kOutput, calls=%fused_computation.17.clone.1 | convolution fusion | flops 418384384 | bytes 16662528 | tf_op jit(solution)/shard_map/while/body/eval_jaxpr/sub | solution.py:88
  199.1 6.1 reshape.286
  234.5 10.1 %multiply_convert_fusion.3 = bf16[128,12,1024]{2,0,1:T(8,128)(2,1)} fusion(f32[128,12,1024]{2,0,1:T(8,128)} %get-tuple-element.323, f32[128,12]{0,1:T(8,128)S(1)} %dynamic-slice_bitcast_fusion.12, pred[128,1024]{1,0:T(8,128)(4,1)S(1)} %dynamic-slice_bitcast_fusion.13, bf16[1,128,12,64]{1,3,2,0:T(8,128)(2,1)S(1)} %copy.153, ...), kind=kOutput, calls=%fused_computation.17.clone.1 | convolution fusion | flops 418384384 | bytes 16662528 | tf_op jit(solution)/shard_map/while/body/eval_jaxpr/sub | solution.py:88
  250.2 6.1 reshape.286
  285.7 10.2 %multiply_convert_fusion.3 = bf16[128,12,1024]{2,0,1:T(8,128)(2,1)} fusion(f32[128,12,1024]{2,0,1:T(8,128)} %get-tuple-element.323, f32[128,12]{0,1:T(8,128)S(1)} %dynamic-slice_bitcast_fusion.12, pred[128,1024]{1,0:T(8,128)(4,1)S(1)} %dynamic-slice_bitcast_fusion.13, bf16[1,128,12,64]{1,3,2,0:T(8,128)(2,1)S(1)} %copy.153, ...), kind=kOutput, calls=%fused_computation.17.clone.1 | convolution fusion | flops 418384384 | bytes 16662528 | tf_op jit(solution)/shard_map/while/body/eval_jaxpr/sub | solution.py:88
  301.5 6.1 reshape.286
  341.8 6.9 %fusion.91 = f32[512,3072]{1,0:T(8,128)} fusion(bf16[512,768]{1,0:T(8,128)(2,1)S(1)} %copy-done.9, bf16[768,3072]{1,0:T(8,128)(2,1)} %param.34), kind=kOutput, calls=%fused_computation.160 | convolution fusion | flops 2415919104 | bytes 11796480 | tf_op jit(solution)/shard_map/dot_general | solution.py:162
  350.7 9.8 %convert_reduce_fusion = (f32[3072]{0:T(1024)}, bf16[512,3072]{1,0:T(8,128)(2,1)S(1)}, bf16[512,3072]{1,0:T(8,128)(2,1)}) fusion(f32[512,3072]{1,0:T(8,128)} %fusion.91, f32[3072]{0:T(1024)S(1)} %copy-done.49, bf16[512,768]{1,0:T(8,128)(2,1)S(1)} %bitcast.225, bf16[3072,768]{1,0:T(8,128)(2,1)} %param.36), kind=kOutput, calls=%fused_computation.48 | convolution fusion | flops 2444227584 | bytes 18112512 | tf_op jit(solution)/shard_map/dot_general | solution.py:174
  366.6 6.8 convolution_convert_fusion
  380.6 6.2 fusion.92
  399.3 10.6 %reduce-scatter.9.cloned.1.call-done = bf16[96,768]{1,0:T(8,128)(2,1)} async-done(((bf16[768,768]{1,0:T(8,128)(2,1)}), bf16[96,768]{1,0:T(8,128)(2,1)}) %reduce-scatter.9.cloned.1.call-update) | async-done | bytes 147472 | tf_op jit(solution)/shard_map/reduce_scatter | solution.py:208
  410.0 40.5 %reduce-scatter.13.cloned.1.call-done = bf16[96,768]{1,0:T(8,128)(2,1)} async-done(((bf16[768,768]{1,0:T(8,128)(2,1)}), bf16[96,768]{1,0:T(8,128)(2,1)}) %reduce-scatter.13.cloned.1.call-update) | async-done | bytes 147472 | tf_op jit(solution)/shard_map/reduce_scatter | solution.py:214
  450.4 57.6 %reduce-scatter.15.cloned.1.call-done = bf16[96,3072]{1,0:T(8,128)(2,1)} async-done(((bf16[768,3072]{1,0:T(8,128)(2,1)}), bf16[96,3072]{1,0:T(8,128)(2,1)}) %reduce-scatter.15.cloned.1.call-update) | async-done | bytes 589840 | tf_op jit(solution)/shard_map/reduce_scatter | solution.py:217
  508.1 57.2 %reduce-scatter.17.cloned.1.call-done = bf16[384,768]{1,0:T(8,128)(2,1)} async-done(((bf16[3072,768]{1,0:T(8,128)(2,1)}), bf16[384,768]{1,0:T(8,128)(2,1)}) %reduce-scatter.17.cloned.1.call-update) | async-done | bytes 589840 | tf_op jit(solution)/shard_map/reduce_scatter | solution.py:220
  572.2 41.3 %all-reduce = (f32[768]{0:T(1024)}, f32[768]{0:T(1024)}, f32[768]{0:T(1024)}, f32[768]{0:T(1024)}, f32[768]{0:T(1024)}, /*index=5*/f32[128]{0:T(128)}, f32[768]{0:T(1024)}, f32[3072]{0:T(1024)}) all-reduce(f32[768]{0:T(1024)} %get-tuple-element.155, f32[768]{0:T(1024)} %get-tuple-element.152, ...), channel_id=1, replica_groups=mesh['seq'=8,'rows'=4] {'seq','rows'}, use_global_device_ids=true, to_apply=%region_18.19 | all-reduce | flops 7808 | bytes 62464 | tf_op jit(solution)/shard_map/psum | solution.py:240
  617.4 20.2 %psum.97 = bf16[96,128]{1,0:T(8,128)(2,1)S(1)} all-reduce(bf16[96,128]{1,0:T(8,128)(2,1)} %reduce-scatter.11.cloned.1.call-done), channel_id=1, replica_groups=mesh['seq'=8,'rows'=4] {'rows'}, use_global_device_ids=true, to_apply=%region_30.31 | all-reduce | flops 12288 | bytes 49152 | tf_op jit(solution)/shard_map/psum | solution.py:226
  638.2 35.2 %all-reduce.4.cloned.1.call-done = (bf16[96,768]{1,0:T(8,128)(2,1)}, bf16[96,768]{1,0:T(8,128)(2,1)}, bf16[96,3072]{1,0:T(8,128)(2,1)}, bf16[384,768]{1,0:T(8,128)(2,1)}) async-done(((bf16[96,768]{1,0:T(8,128)(2,1)}, bf16[96,768]{1,0:T(8,128)(2,1)}, bf16[96,3072]{1,0:T(8,128)(2,1)}, bf16[384,768]{1,0:T(8,128)(2,1)}), (bf16[96,768]{1,0:T(8,128)(2,1)}, bf16[96,768]{1,0:T(8,128)(2,1)}, ...) | async-done | bytes 1474576 | tf_op jit(solution)/shard_map/psum | solution.py:225
  (331 shorter events, 287.7 us)
Async XLA Ops:
  7.2 10.2 %copy-start = (bf16[768,768]{1,0:T(8,128)(2,1)S(1)}, bf16[768,768]{1,0:T(8,128)(2,1)}, u32[]{:S(2)}) copy-start(bf16[768,768]{1,0:T(8,128)(2,1)} %param.28) | copy-start | bytes 3538948
  7.2 5.3 copy-start.3
  7.2 7.4 %copy-start.14 = (bf16[768,128]{1,0:T(8,128)(2,1)S(1)}, bf16[768,128]{1,0:T(8,128)(2,1)}, u32[]{:S(2)}) copy-start(bf16[768,128]{1,0:T(8,128)(2,1)} %param.30) | copy-start | bytes 589828
  7.2 7.4 %copy-start.46 = (f32[128]{0:T(128)S(1)}, f32[128]{0:T(128)}, u32[]{:S(2)}) copy-start(f32[128]{0:T(128)} %param.31) | copy-start | bytes 1540
  7.2 36.5 %all-gather.2.cloned.1.call-start = ((), (), s32[]{:S(2)}) async-start(), calls=%async_computation.6 | async-start | bytes 1179648 | tf_op jit(solution)/shard_map/all_gather | solution.py:158
  9.1 6.7 copy-start.44
  17.3 369.6 %reduce-scatter.7.cloned.1.call-start = ((), (), s32[]{:S(2)}) async-start(), calls=%async_computation.7 | async-start | bytes 2359296 | tf_op jit(solution)/shard_map/reduce_scatter | solution.py:185
  17.4 7.1 %copy-start.19 = (f32[4,128,8]{1,0,2:T(4,128)}, f32[4,128,8]{1,0,2:T(4,128)S(1)}, u32[]{:S(2)}) copy-start(f32[4,128,8]{1,0,2:T(4,128)S(1)} %copy.102) | copy-start | bytes 49156
  327.6 82.4 %reduce-scatter.9.cloned.1.call-start = ((), (), s32[]{:S(2)}) async-start(), calls=%async_computation.8 | async-start | bytes 1327104 | tf_op jit(solution)/shard_map/reduce_scatter | solution.py:208
  341.8 108.7 %reduce-scatter.13.cloned.1.call-start = ((), (), s32[]{:S(2)}) async-start(), calls=%async_computation.10 | async-start | bytes 1327104 | tf_op jit(solution)/shard_map/reduce_scatter | solution.py:214
  341.8 7.0 %copy-start.8 = (bf16[4,128,768]{2,1,0:T(8,128)(2,1)S(1)}, bf16[4,128,768]{2,1,0:T(8,128)(2,1)}, u32[]{:S(2)}) copy-start(bf16[4,128,768]{2,1,0:T(8,128)(2,1)} %param.23) | copy-start | bytes 2359300
  341.8 6.9 %copy-start.48 = (bf16[4,128,768]{2,1,0:T(8,128)(2,1)S(1)}, bf16[4,128,768]{2,1,0:T(8,128)(2,1)}, u32[]{:S(2)}) copy-start(bf16[4,128,768]{2,1,0:T(8,128)(2,1)} %get-tuple-element.92) | copy-start | bytes 2359300
  350.6 157.4 %reduce-scatter.15.cloned.1.call-start = ((), (), s32[]{:S(2)}) async-start(), calls=%async_computation.11 | async-start | bytes 5308416 | tf_op jit(solution)/shard_map/reduce_scatter | solution.py:217
  366.6 198.7 %reduce-scatter.17.cloned.1.call-start = ((), (), s32[]{:S(2)}) async-start(), calls=%async_computation.12 | async-start | bytes 5308416 | tf_op jit(solution)/shard_map/reduce_scatter | solution.py:220
  373.4 243.9 %reduce-scatter.11.cloned.1.call-start = ((), (), s32[]{:S(2)}) async-start(), calls=%async_computation.9 | async-start | bytes 221184 | tf_op jit(solution)/shard_map/reduce_scatter | solution.py:211
  374.5 6.1 copy-start.52
  380.6 6.3 copy-start.41
  380.6 6.3 copy-start.45
  391.6 281.8 %all-reduce.4.cloned.1.call-start = ((), (), s32[]{:S(2)}) async-start(), calls=%async_computation.13 | async-start | bytes 2949120 | tf_op jit(solution)/shard_map/psum | solution.py:225
  395.4 169.9 %copy-start.22 = (f32[768]{0:T(1024)S(1)}, f32[768]{0:T(1024)}, u32[]{:S(2)}) copy-start(f32[768]{0:T(1024)} %param.24) | copy-start | bytes 9220
  395.4 169.9 %copy-start.25 = (f32[768]{0:T(1024)S(1)}, f32[768]{0:T(1024)}, u32[]{:S(2)}) copy-start(f32[768]{0:T(1024)} %param.26) | copy-start | bytes 9220
  565.3 4.8 copy-start.28
  569.8 44.4 %copy-start.29 = (f32[512]{0:T(512)S(1)}, f32[512]{0:T(512)}, u32[]{:S(2)}) copy-start(f32[512]{0:T(512)} %copy-done.27) | copy-start | bytes 6148
  569.8 44.4 %copy-start.32 = (f32[512]{0:T(512)S(1)}, f32[512]{0:T(512)}, u32[]{:S(2)}) copy-start(f32[512]{0:T(512)} %copy-done.30) | copy-start | bytes 6148
  (44 other events, 110.3 us)
Sparse Core Ops, SparseCore 0:
  17.4 26.2 all-gather.1
  327.7 41.2 reduce-scatter.6
  373.2 36.7 reduce-scatter.8
  413.6 36.7 reduce-scatter.12
  454.1 53.8 reduce-scatter.14
  511.4 53.8 reduce-scatter.16
  569.1 33.4 reduce-scatter.10
  605.3 68.0 all-reduce.3
where the time goes:
time: 698 us; the launch traced here: 686 us
  waiting for transfers between devices  214 us (31%)
  local copies, waits for them, and re-layouts  188 us (27%)
  matrix products  160 us (23%)
  blocking collectives  61.5 us (9%)
  other arithmetic  46.1 us (7%)
  between operations  15.3 us (2%)
    reduce_scatter x1, waiting for transfers between devices, shards(): lax.psum_scatter(g_up_weight.astype(jnp.bfloat16), 'seq', scatter_dimensi...  57.6 us
    reduce_scatter x1, waiting for transfers between devices, shards(): lax.psum_scatter(g_down_weight.astype(jnp.bfloat16), 'seq', scatter_dimen...  57.2 us
    psum x1, blocking collectives, shards(): lax.psum((g_first_gain, g_first_shift, g_second_gain, g_second_shift, g_q...  41.3 us
    sub x4, matrix products, attend_back(): d_probs - jnp.sum(probs * d_probs, axis=-1, keepdims=True)  40.6 us
    reduce_scatter x1, waiting for transfers between devices, shards(): lax.psum_scatter(g_output_weight.astype(jnp.bfloat16), 'seq', scatter_dim...  40.5 us
    psum x1, waiting for transfers between devices, shards(): lax.psum(part_query.astype(jnp.bfloat16), 'rows').astype(jnp.float32)  35.2 us
    reshape x4, local copies, waits for them, and re-layouts, attend(): probs_low.reshape(block_len * head_count, -1)  24.6 us
    reshape x4, local copies, waits for them, and re-layouts, attend_back(): d_scores = d_scores.astype(jnp.bfloat16).reshape(block_len * head_count, -1)  24.6 us
  transfers between devices with their start and end apart: 8, of which 6 were waited for; matrix products, arithmetic and copies ran while one was open for 13% of the time, Pallas kernels for 0%

commit v1 on v0

v1 whole, which is shorter than its diff:
```python
import functools

import jax
import jax.numpy as jnp
from jax import lax
from jax.experimental import pallas as pl
from jax.experimental.pallas import tpu as pltpu
from jax.sharding import PartitionSpec as P

HD = 64
ROT = 16
BLK = 128
NEG = -1e30
EPS = 1e-05
F32 = jnp.float32
BF = jnp.bfloat16


def dot(a, b):
    return jnp.dot(a, b, preferred_element_type=F32)


def dot_nt(a, b):
    return lax.dot_general(a, b, (((1,), (1,)), ((), ())), preferred_element_type=F32)


def dot_tn(a, b):
    return lax.dot_general(a, b, (((0,), (0,)), ((), ())), preferred_element_type=F32)


def doc_start(place, cuts):
    begin = jnp.where(place >= cuts[0], cuts[0], 0)
    for cut in cuts[1:]:
        begin = jnp.where(place >= cut, cut, begin)
    return begin


def attn_kernel(
    own_ref, len_ref, q_ref, do_ref, kv_ref, cos_ref, sin_ref,
    mt_ref, mx_ref, dq_ref, dkv_ref,
    s_ref, e_ref, qz, dz, m_ref, l_ref, o_ref, dqa,
):
    row = pl.program_id(0)
    own = own_ref[0]
    lanes = q_ref.shape[-1]
    heads = lanes // BLK
    cuts = []
    for i in range(len_ref.shape[1] - 1):
        cuts.append(len_ref[row, i] + (cuts[-1] if cuts else 0))
    t0 = own * BLK
    low = doc_start(t0, cuts) // BLK
    place = t0 + lax.broadcasted_iota(jnp.int32, (BLK, BLK), 1)
    begin = doc_start(place, cuts)
    key_iota = lax.broadcasted_iota(jnp.int32, (BLK, BLK), 0)
    qz[:HD, :] = q_ref[0]
    qz[HD:, :] = jnp.zeros((HD, lanes), BF)
    dz[HD:, :] = do_ref[0]
    dz[:HD, :] = jnp.zeros((HD, lanes), BF)
    m_ref[...] = jnp.full(m_ref.shape, NEG, F32)
    l_ref[...] = jnp.zeros(l_ref.shape, F32)
    o_ref[...] = jnp.zeros(o_ref.shape, F32)
    dqa[...] = jnp.zeros(dqa.shape, F32)
    dkv_ref[...] = jnp.zeros(dkv_ref.shape, dkv_ref.dtype)

    def scores(j, _):
        kv = kv_ref[0, pl.ds(pl.multiple_of(j * BLK, BLK), BLK), :]
        keys = j * BLK + key_iota
        bias = jnp.where((keys <= place) & (keys >= begin), 0.0, NEG)
        s = dot(kv, qz[...]) + jnp.concatenate([bias] * heads, axis=1)
        s_ref[j] = s
        m_ref[...] = jnp.maximum(m_ref[...], jnp.max(s.reshape(BLK // 8, 8, lanes), axis=0))
        return 0

    lax.fori_loop(low, own + 1, scores, 0)
    m_ref[0:1, :] = jnp.max(m_ref[...], axis=0, keepdims=True)

    def mix(j, _):
        v_t = kv_ref[0, pl.ds(pl.multiple_of(j * BLK, BLK), BLK), :].T[HD:]
        e = jnp.exp(s_ref[j] - m_ref[0:1, :])
        l_ref[...] += jnp.sum(e.reshape(BLK // 8, 8, lanes), axis=0)
        e_low = e.astype(BF)
        e_ref[j] = e_low
        o_ref[...] += dot(v_t, e_low)
        return 0

    lax.fori_loop(low, own + 1, mix, 0)
    inv = 1.0 / jnp.sum(l_ref[...], axis=0, keepdims=True)
    o = o_ref[...] * inv
    l_ref[0:1, :] = inv
    m_ref[0:1, :] = jnp.sum(o * dz[HD:, :].astype(F32), axis=0, keepdims=True)
    for h in range(0, heads, 2):
        pair = jnp.concatenate(
            [o[:, h * BLK : (h + 1) * BLK], o[:, (h + 1) * BLK : (h + 2) * BLK]], axis=0
        )
        mt_ref[0, h * HD : (h + 2) * HD, :] = pair.astype(BF)
        mx_ref[0, :, h * HD : (h + 2) * HD] = pair.T.astype(BF)

    def back(j, _):
        rows = pl.ds(pl.multiple_of(j * BLK, BLK), BLK)
        kv = kv_ref[0, rows, :]
        k_t = kv.T[:HD]
        dp = dot(kv, dz[...])
        p = e_ref[j].astype(F32) * l_ref[0:1, :]
        ds = (p * (dp - m_ref[0:1, :])).astype(BF)
        acc = dot_nt(ds, qz[...]) + dot_nt(p.astype(BF), dz[...])
        dqa[...] += dot(k_t, ds)
        dkv_ref[0, rows, :] = acc.astype(dkv_ref.dtype)
        return 0

    lax.fori_loop(low, own + 1, back, 0)
    cosine, sine = cos_ref[0], sin_ref[0]
    for h in range(0, heads, 2):
        parts = []
        for g in (h, h + 1):
            d = dqa[:, g * BLK : (g + 1) * BLK]
            front, behind = d[0:8], d[8:16]
            parts += [front * cosine + behind * sine, behind * cosine - front * sine, d[16:]]
        dq_ref[0, :, h * HD : (h + 2) * HD] = (jnp.concatenate(parts, axis=0) * 0.125).T.astype(BF)


def attention(own, lengths, q, do, kv, cosine, sine):
    rows, length, _ = kv.shape
    lanes = q.shape[-1]
    width = lanes // BLK * HD
    blocks = length // BLK

    def per_row(*shape):
        return pl.BlockSpec((1,) + shape, lambda r, *_: (r,) + (0,) * len(shape))

    return pl.pallas_call(
        attn_kernel,
        grid_spec=pltpu.PrefetchScalarGridSpec(
            num_scalar_prefetch=2,
            grid=(rows,),
            in_specs=[
                per_row(HD, lanes), per_row(HD, lanes), per_row(length, 2 * HD),
                per_row(8, BLK), per_row(8, BLK),
            ],
            out_specs=[
                per_row(width, BLK), per_row(BLK, width), per_row(BLK, width),
                per_row(length, 2 * HD),
            ],
            scratch_shapes=[
                pltpu.VMEM((blocks, BLK, lanes), F32),
                pltpu.VMEM((blocks, BLK, lanes), BF),
                pltpu.VMEM((2 * HD, lanes), BF),
                pltpu.VMEM((2 * HD, lanes), BF),
                pltpu.VMEM((8, lanes), F32),
                pltpu.VMEM((8, lanes), F32),
                pltpu.VMEM((HD, lanes), F32),
                pltpu.VMEM((HD, lanes), F32),
            ],
        ),
        out_shape=[
            jax.ShapeDtypeStruct((rows, width, BLK), BF),
            jax.ShapeDtypeStruct((rows, BLK, width), BF),
            jax.ShapeDtypeStruct((rows, BLK, width), BF),
            jax.ShapeDtypeStruct((rows, length, 2 * HD), BF),
        ],
        compiler_params=pltpu.CompilerParams(
            vmem_limit_bytes=50 * 2**20, dimension_semantics=("arbitrary",)
        ),
        cost_estimate=pl.CostEstimate(
            flops=10 * rows * length * lanes * HD, bytes_accessed=8 * 2**20,
            transcendentals=rows * length * lanes,
        ),
        name="attention",
    )(own, lengths, q, do, kv, cosine, sine)


def ffn_kernel(h_ref, ht_ref, dy_ref, wu_ref, wd_ref, bu_ref, fo_ref, dh_ref, gu_ref, gd_ref, gb_ref):
    step = pl.program_id(0)
    h, dy, wu, wd = h_ref[...], dy_ref[...], wu_ref[...], wd_ref[...]
    up = dot(h, wu) + bu_ref[...]
    d_act = dot_nt(dy, wd)
    cdf = 0.5 + 0.5 * lax.erf(up * 0.7071067811865476)
    act = (up * cdf).astype(BF)
    pdf = jnp.exp(-0.5 * up * up) * 0.3989422804014327
    d_up = (d_act * (cdf + up * pdf)).astype(BF)
    gb_ref[...] = jnp.sum(d_up.astype(F32), axis=0, keepdims=True)

    @pl.when(step == 0)
    def _():
        fo_ref[...] = jnp.zeros_like(fo_ref)
        dh_ref[...] = jnp.zeros_like(dh_ref)

    fo_ref[...] += dot(act, wd)
    dh_ref[...] += dot_nt(d_up, wu)
    gu_ref[...] = dot(ht_ref[...], d_up).astype(BF)
    gd_ref[...] = dot_tn(act, dy).astype(BF)


def ffn(h, dy, wu, wd, bu, cols=768):
    toks, width = h.shape
    hidden = wu.shape[1]

    def full(*shape):
        return pl.BlockSpec(shape, lambda i: (0,) * len(shape))

    up_spec = pl.BlockSpec((width, cols), lambda i: (0, i))
    down_spec = pl.BlockSpec((cols, width), lambda i: (i, 0))
    bias_spec = pl.BlockSpec((1, cols), lambda i: (0, i))
    return pl.pallas_call(
        ffn_kernel,
        grid=(hidden // cols,),
        in_specs=[full(toks, width), full(width, toks), full(toks, width), up_spec, down_spec, bias_spec],
        out_specs=[full(toks, width), full(toks, width), up_spec, down_spec, bias_spec],
        out_shape=[
            jax.ShapeDtypeStruct((toks, width), F32),
            jax.ShapeDtypeStruct((toks, width), F32),
            jax.ShapeDtypeStruct((width, hidden), BF),
            jax.ShapeDtypeStruct((hidden, width), BF),
            jax.ShapeDtypeStruct((1, hidden), F32),
        ],
        compiler_params=pltpu.CompilerParams(
            vmem_limit_bytes=50 * 2**20, dimension_semantics=("arbitrary",)
        ),
        cost_estimate=pl.CostEstimate(
            flops=12 * toks * width * hidden, bytes_accessed=8 * width * hidden, transcendentals=2 * toks * hidden
        ),
        name="feed_forward",
    )(h, h.T, dy, wu, wd, bu[None, :])


def rotate_t(values, cosine, sine):
    front, behind = values[:, :, :8], values[:, :, 8:16]
    return jnp.concatenate(
        [front * cosine - behind * sine, behind * cosine + front * sine, values[:, :, 16:]], axis=2
    )


def shards(
    hidden, lengths, cotangent, first_gain, first_shift, second_gain, second_shift,
    query_weight, query_bias, keyvalue_weight, keyvalue_bias, output_weight, output_bias,
    up_weight, up_bias, down_weight, down_bias,
):
    rows, block, width = hidden.shape
    heads = width // HD
    toks = rows * block
    own = lax.axis_index("seq")
    cuts = [jnp.sum(lengths[:, : i + 1], axis=1)[:, None] for i in range(lengths.shape[1] - 1)]
    place = own * block + jnp.arange(block, dtype=jnp.int32)[None, :]
    positions = place - doc_start(place, cuts)
    freqs = jnp.power(10000.0, -2.0 * jnp.arange(ROT // 2, dtype=F32) / ROT)
    angles = positions.astype(F32)[:, None, :] * freqs[None, :, None]
    cosine, sine = jnp.cos(angles), jnp.sin(angles)

    x = hidden.astype(F32).reshape(toks, width)
    dy = cotangent.reshape(toks, width)
    dy32 = dy.astype(F32)
    centred = x - jnp.mean(x, axis=-1, keepdims=True)
    factor = lax.rsqrt(jnp.mean(centred * centred, axis=-1, keepdims=True) + EPS)
    xhat = centred * factor
    h1 = (xhat * first_gain + first_shift).astype(BF)
    h2 = (xhat * second_gain + second_shift).astype(BF)

    kv = (dot(h1, keyvalue_weight) + keyvalue_bias).reshape(rows, block, 2 * HD)
    cos_k, sin_k = cosine.swapaxes(1, 2), sine.swapaxes(1, 2)
    front, behind = kv[..., :8], kv[..., 8:16]
    kv_low = jnp.concatenate(
        [front * cos_k - behind * sin_k, behind * cos_k + front * sin_k, kv[..., 16:]], axis=-1
    ).astype(BF)
    kv_full = lax.all_gather(kv_low, "seq", axis=1, tiled=True)

    ffn_out, second_grad, g_up, g_down, g_up_bias = ffn(h2, dy, up_weight, down_weight, up_bias)

    q = jnp.einsum("rtd,de->ret", h1.reshape(rows, block, width), query_weight, preferred_element_type=F32)
    q = (q + query_bias[None, :, None]).reshape(rows, heads, HD, block)
    q = (rotate_t(q, cosine[:, None], sine[:, None]).astype(BF) * 0.125).astype(BF)
    q = q.transpose(0, 2, 1, 3).reshape(rows, HD, heads * block)
    do = jnp.einsum("rtd,ed->ret", dy.reshape(rows, block, width), output_weight, preferred_element_type=F32)
    do = do.astype(BF).reshape(rows, heads, HD, block).transpose(0, 2, 1, 3).reshape(rows, HD, heads * block)

    mixed_t, mixed, dq, dkv = attention(own[None], lengths, q, do, kv_full, cosine, sine)
    mixed = mixed.reshape(toks, width)
    dq = dq.reshape(toks, width)
    layer_output = x + dot(mixed, output_weight) + output_bias + ffn_out + down_bias
    layer_output = layer_output.astype(BF).reshape(rows, block, width)
    g_out = jnp.einsum("ret,rtd->ed", mixed_t, cotangent, preferred_element_type=F32)
    g_query = dot_tn(h1, dq)

    dkv = lax.psum_scatter(dkv, "seq", scatter_dimension=1, tiled=True).astype(F32)
    front, behind = dkv[..., :8], dkv[..., 8:16]
    d_kv = jnp.concatenate(
        [front * cos_k + behind * sin_k, behind * cos_k - front * sin_k, dkv[..., 16:]], axis=-1
    ).astype(BF).reshape(toks, 2 * HD)
    g_kv = dot_tn(h1, d_kv)
    first_grad = dot_nt(dq, query_weight) + dot_nt(d_kv, keyvalue_weight)

    def norm_back(grad, gain):
        g = grad * gain
        return factor * (
            g - jnp.mean(g, axis=-1, keepdims=True) - xhat * jnp.mean(g * xhat, axis=-1, keepdims=True)
        )

    input_grad = dy32 + norm_back(first_grad, first_gain) + norm_back(second_grad, second_gain)
    input_grad = input_grad.astype(BF).reshape(rows, block, width)

    seq_size = lax.axis_size("seq")

    def by_owner(g):
        return g.astype(BF).reshape(seq_size, -1, 512)

    def summed(parts):
        joined = jnp.concatenate([by_owner(g) for g in parts], axis=1)
        part = lax.psum_scatter(joined, "seq", scatter_dimension=0, tiled=True)[0]
        return lax.psum(part, "rows").astype(F32)

    first = summed([g_up, g_down])
    second = summed([g_out, g_query, g_kv])

    def split(part, shapes):
        outs, at = [], 0
        for shape in shapes:
            n = shape[0] * shape[1] // 512
            outs.append(part[at : at + n].reshape(shape))
            at += n
        return outs

    sub = width // seq_size
    hid = up_weight.shape[1]
    s_up, s_down = split(first, [(sub, hid), (hid // seq_size, width)])
    s_out, s_query, s_kv = split(second, [(sub, width), (sub, width), (sub, 2 * HD)])

    small = lax.psum(
        jnp.concatenate([
            jnp.sum(first_grad * xhat, axis=0), jnp.sum(first_grad, axis=0),
            jnp.sum(second_grad * xhat, axis=0), jnp.sum(second_grad, axis=0),
            jnp.sum(dq.astype(F32), axis=0), jnp.sum(d_kv.astype(F32), axis=0),
            jnp.sum(dy32, axis=0), g_up_bias[0],
        ]),
        ("seq", "rows"),
    )
    sizes = [width] * 5 + [2 * HD, width, hid]
    pieces, at = [], 0
    for size in sizes:
        pieces.append(small[at : at + size])
        at += size
    s_fg, s_fs, s_sg, s_ss, s_qb, s_kb, s_ob, s_ub = pieces
    return (
        layer_output, input_grad, s_fg, s_fs, s_sg, s_ss, s_query, s_qb, s_kv, s_kb,
        s_out, s_ob, s_up, s_ub, s_down, s_ob,
    )


def solution(mesh):
    tokens = P("rows", "seq", None)
    weight = P("seq", None)
    return jax.shard_map(
        shards,
        mesh=mesh,
        in_specs=(tokens, P("rows", None), tokens) + (P(),) * 14,
        out_specs=(
            tokens, tokens, P(), P(), P(), P(), weight, P(), weight, P(), weight, P(), weight, P(), weight, P(),
        ),
        check_vma=False,
    )
```

time: 698 us -> 336 us (0.48); the launches traced: 686 us -> 332 us
  matrix products: 160 us -> 18.4 us
  local copies, waits for them, and re-layouts: 188 us -> 58.5 us
  waiting for transfers between devices: 214 us -> 143 us
  Pallas kernels: 0 us -> 27.8 us
  blocking collectives: 61.5 us -> 42.4 us
  other arithmetic: 46.1 us -> 27.9 us
    dot_general x39 -> x9, matrix products: 120 us -> 18.4 us  [the longest x2 4.55 us: dot_tn(): lax.dot_general(a, b, (((0,), (0,)), ((), ())), preferred_element_type=F32)]
    reduce_scatter x6 -> x3, waiting for transfers between devices: 166 us -> 109 us  [the longest x2 67.1 us: summed(): part = lax.psum_scatter(joined, 'seq', scatter_dimension=0, tiled=True)[0]]
    convert_element_type x13 -> x0, local copies, waits for them, and re-layouts: 53.4 us -> none  [the longest x4 22.6 us: attend_back(): d_scores = d_scores.astype(jnp.bfloat16).reshape(block_len * head_count, -1)]
    reshape x21 -> x12, local copies, waits for them, and re-layouts: 76.9 us -> 34.5 us  [the longest x5 25 us: by_owner(): return g.astype(BF).reshape(seq_size, -1, 512)]
    sub x4 -> x0, matrix products: 40.6 us -> none  [attend_back(): d_probs - jnp.sum(probs * d_probs, axis=-1, keepdims=True)]
    pallas_call x0 -> x2, Pallas kernels: none -> 27.8 us  [the longest x1 19.4 us: ffn(): pl.pallas_call(ffn_kernel, grid=(hidden // cols,), in_specs=[full(toks, w...]
    psum x2 -> x1, blocking collectives: 61.5 us -> 42.4 us  [shards(): lax.psum(jnp.concatenate([jnp.sum(first_grad * xhat, axis=0), jnp.sum(fir...]
    dynamic_slice x17 -> x0, local copies, waits for them, and re-layouts: 15.2 us -> none  [the longest x16 15.2 us: shards(): mixed, log_total = lax.map(attend, (query_rot, kv_full, visible))]
  transfers between devices with their start and end apart: 8 -> 5, of which waited for: 6 -> 4; matrix products, arithmetic and copies ran while one was open for 13% -> 20% of each run, Pallas kernels for 0% -> 6%
where the time goes in v1:
time: 336 us; the launch traced here: 332 us
  waiting for transfers between devices  143 us (43%)
  local copies, waits for them, and re-layouts  58.5 us (17%)
  blocking collectives  42.4 us (13%)
  other arithmetic  27.9 us (8%)
  Pallas kernels  27.8 us (8%)
  matrix products  18.4 us (5%)
  between operations  14.4 us (4%)
    reduce_scatter x2, waiting for transfers between devices, summed(): part = lax.psum_scatter(joined, 'seq', scatter_dimension=0, tiled=True)[0]  67.1 us
    psum x1, blocking collectives, shards(): lax.psum(jnp.concatenate([jnp.sum(first_grad * xhat, axis=0), jnp.sum(fir...  42.4 us
    reduce_scatter x1, waiting for transfers between devices, shards(): lax.psum_scatter(dkv, 'seq', scatter_dimension=1, tiled=True).astype(F32)  42.3 us
    reshape x5, local copies, waits for them, and re-layouts, by_owner(): return g.astype(BF).reshape(seq_size, -1, 512)  25 us
    psum x1, waiting for transfers between devices, summed(): return lax.psum(part, 'rows').astype(F32)  23.3 us
    pallas_call x1, Pallas kernels, ffn(): pl.pallas_call(ffn_kernel, grid=(hidden // cols,), in_specs=[full(toks, w...  19.4 us
    unnamed x102, local copies, waits for them, and re-layouts  12 us
    concatenate x2, other arithmetic, summed(): joined = jnp.concatenate([by_owner(g) for g in parts], axis=1)  10.9 us
  transfers between devices with their start and end apart: 5, of which 4 were waited for; matrix products, arithmetic and copies ran while one was open for 20% of the time, Pallas kernels for 6%

profile of v1, /device:TPU:0, one launch (start us, length us, event | category | flops | bytes accessed | tf_op | source)
XLA Modules:
  0.0 332.5 jit_solution(6124989804943984254)
XLA Ops:
  16.9 2.1 convolution_convert_fusion
  20.5 1.7 reshape.333.do_ref
  22.2 3.2 add_bitcast_fusion
  25.4 3.1 copy.44
  33.4 9.9 %all-gather.2.cloned.1.call-done.kv_ref = bf16[4,1024,128]{2,1,0:T(8,128)(2,1)} async-done(((bf16[4,128,128]{2,1,0:T(8,128)(2,1)}), bf16[4,1024,128]{2,1,0:T(8,128)(2,1)}) %all-gather.2.cloned.1.call-update) | async-done | bytes 1048592 | tf_op jit(solution)/shard_map/all_gather | solution.py:263
  45.8 8.4 %attention.1 = (bf16[4,768,128]{2,1,0:T(8,128)(2,1)S(1)}, bf16[4,128,768]{2,1,0:T(8,128)(2,1)S(1)}, bf16[4,128,768]{2,1,0:T(8,128)(2,1)S(1)}, bf16[4,1024,128]{2,1,0:T(8,128)(2,1)}) custom-call(s32[1]{0:T(128)} %bitcast.1.own_ref, s32[4,4]{1,0:T(4,128)S(1)} %copy-done.7, bf16[4,64,1536]{2,1,0:T(8,128)(2,1)S(1)} %copy-done.4, ...), custom_call_target="tpu_custom_call" | custom-call | flops 4026531840 | bytes 8388608 | tf_op jit(solution)/shard_map/attention/pallas_call | solution.py:130
  56.9 3.5 %bitcast_convert_fusion = bf16[768,768]{1,0:T(8,128)(2,1)} fusion(bf16[4,128,768]{2,1,0:T(8,128)(2,1)} %copy-done.2, bf16[4,128,768]{2,1,0:T(8,128)(2,1)} %param.17, f32[768]{0:T(1024)} %param.21, f32[768]{0:T(1024)} %param.20, f32[4,128]{1,0:T(4,128)} %copy-done.44, f32[4,128]{1,0:T(4,128)} %copy-done.39), kind=kOutput, calls=%fused_computation.2 | convolution fusion | flops 606928896 | bytes 2762752 | tf_op jit(solution)/shard_map/dot_general | solution.py:28
  60.4 3.2 reshape.341
  63.6 1.8 bitcast_convert_fusion.1
  65.4 3.1 reshape.340
  68.5 42.3 %reduce-scatter.4.cloned.1.call-done = bf16[4,128,128]{2,1,0:T(8,128)(2,1)} async-done(((bf16[4,1024,128]{2,1,0:T(8,128)(2,1)}), bf16[4,128,128]{2,1,0:T(8,128)(2,1)}) %reduce-scatter.4.cloned.1.call-update) | async-done | bytes 131088 | tf_op jit(solution)/shard_map/reduce_scatter | solution.py:282
  117.4 3.3 %pad_maximum_fusion.1 = bf16[8,312,512]{2,1,0:T(8,128)(2,1)} fusion(bf16[8,24,512]{2,1,0:T(8,128)(2,1)S(1)} %reshape.342, bf16[8,144,512]{2,1,0:T(8,128)(2,1)} %reshape.341, bf16[8,144,512]{2,1,0:T(8,128)(2,1)} %reshape.340), kind=kLoop, calls=%fused_computation.1 | loop fusion | flops 7667712 | bytes 5111808 | tf_op jit(solution)/shard_map/concatenate | solution.py:305
  122.0 19.4 %feed_forward.1 = (f32[512,768]{1,0:T(8,128)S(1)}, f32[512,768]{1,0:T(8,128)}, bf16[768,3072]{1,0:T(8,128)(2,1)}, bf16[3072,768]{1,0:T(8,128)(2,1)}, f32[1,3072]{1,0:T(1,128)S(1)}) custom-call(bf16[512,768]{1,0:T(8,128)(2,1)S(1)} %get-tuple-element.55.h_ref, bf16[768,512]{1,0:T(8,128)(2,1)S(1)} %copy.48.ht_ref, bf16[512,768]{1,0:T(8,128)(2,1)S(1)} %bitcast.120, ...), custom_call_target="tpu_custom_call" | custom-call | flops 14495514624 | bytes 18874368 | tf_op jit(solution)/shard_map/feed_forward/pallas_call | solution.py:203
  142.6 9.1 %reshape.346 = bf16[8,576,512]{2,1,0:T(8,128)(2,1)} reshape(bf16[768,3072]{1,0:T(8,128)(2,1)} %get-tuple-element.32) | data formatting | bytes 9437184 | tf_op jit(solution)/shard_map/reshape | solution.py:302
  151.7 8.5 %reshape.347 = bf16[8,576,512]{2,1,0:T(8,128)(2,1)} reshape(bf16[3072,768]{1,0:T(8,128)(2,1)} %get-tuple-element.33) | data formatting | bytes 9437184 | tf_op jit(solution)/shard_map/reshape | solution.py:302
  160.2 7.6 %pad_maximum_fusion = bf16[8,1152,512]{2,1,0:T(8,128)(2,1)} fusion(bf16[8,576,512]{2,1,0:T(8,128)(2,1)} %reshape.347, bf16[8,576,512]{2,1,0:T(8,128)(2,1)} %reshape.346), kind=kLoop, calls=%fused_computation | loop fusion | flops 18874368 | bytes 18874368 | tf_op jit(solution)/shard_map/concatenate | solution.py:305
  169.7 3.5 %fusion.33 = bf16[512,768]{1,0:T(8,128)(2,1)} fusion(f32[512,768]{1,0:T(8,128)} %copy-done.13, bf16[4,128,768]{2,1,0:T(8,128)(2,1)S(1)} %copy-done.15, bf16[512,768]{1,0:T(8,128)(2,1)S(1)} %bitcast.125, bf16[768,768]{1,0:T(8,128)(2,1)} %param.28, f32[768]{0:T(1024)} %param.33, f32[768]{0:T(1024)} %param.29), kind=kOutput, calls=%fused_computation.41 | convolution fusion | flops 606339072 | bytes 5117952 | tf_op jit(solution)/shard_map/dot_general | solution.py:20
  174.8 2.5 fusion.28
  177.4 67.1 %reduce-scatter.8.cloned.1.call-done = bf16[1,1152,512]{2,1,0:T(8,128)(2,1)} async-done(((bf16[8,1152,512]{2,1,0:T(8,128)(2,1)}), bf16[1,1152,512]{2,1,0:T(8,128)(2,1)}) %reduce-scatter.8.cloned.1.call-update) | async-done | bytes 1179664 | tf_op jit(solution)/shard_map/reduce_scatter | solution.py:306
  244.7 42.4 %psum.21 = f32[7808]{0:T(1024)S(1)} all-reduce(f32[7808]{0:T(1024)S(1)} %constant_dynamic-update-slice_fusion), channel_id=1, replica_groups=mesh['seq'=8,'rows'=4] {'seq','rows'}, use_global_device_ids=true, to_apply=%region_16.17 | all-reduce | flops 7808 | bytes 62464 | tf_op jit(solution)/shard_map/psum | solution.py:325
  288.8 3.2 fusion.24
  292.0 23.3 %all-reduce.3.cloned.1.call-done = (bf16[312,512]{1,0:T(8,128)(2,1)}, bf16[1152,512]{1,0:T(8,128)(2,1)}) async-done(((bf16[312,512]{1,0:T(8,128)(2,1)}, bf16[1152,512]{1,0:T(8,128)(2,1)}), (bf16[312,512]{1,0:T(8,128)(2,1)}, bf16[1152,512]{1,0:T(8,128)(2,1)})) %all-reduce.3.cloned.1.call-update) | async-done | bytes 1499152 | tf_op jit(solution)/shard_map/psum | solution.py:307
  319.4 1.8 fusion.57
  321.2 2.6 reshape.349
  (156 shorter events, 41.5 us)
Async XLA Ops:
  7.2 15.0 %copy-start = (bf16[768,768]{1,0:T(8,128)(2,1)S(1)}, bf16[768,768]{1,0:T(8,128)(2,1)}, u32[]{:S(2)}) copy-start(bf16[768,768]{1,0:T(8,128)(2,1)} %param.24) | copy-start | bytes 3538948
  7.2 5.6 %copy-start.14 = (bf16[4,128,768]{2,1,0:T(8,128)(2,1)S(1)}, bf16[4,128,768]{2,1,0:T(8,128)(2,1)}, u32[]{:S(2)}) copy-start(bf16[4,128,768]{2,1,0:T(8,128)(2,1)} %param.17) | copy-start | bytes 2359300
  7.2 5.6 %copy-start.33 = (f32[768]{0:T(1024)S(1)}, f32[768]{0:T(1024)}, u32[]{:S(2)}) copy-start(f32[768]{0:T(1024)} %param.20) | copy-start | bytes 9220
  7.2 5.6 %copy-start.35 = (f32[768]{0:T(1024)S(1)}, f32[768]{0:T(1024)}, u32[]{:S(2)}) copy-start(f32[768]{0:T(1024)} %param.22) | copy-start | bytes 9220
  7.2 5.6 %copy-start.43 = (f32[768]{0:T(1024)S(1)}, f32[768]{0:T(1024)}, u32[]{:S(2)}) copy-start(f32[768]{0:T(1024)} %param.21) | copy-start | bytes 9220
  7.2 5.6 %copy-start.42 = (f32[768]{0:T(1024)S(1)}, f32[768]{0:T(1024)}, u32[]{:S(2)}) copy-start(f32[768]{0:T(1024)} %param.23) | copy-start | bytes 9220
  7.3 36.0 %all-gather.2.cloned.1.call-start = ((), (), s32[]{:S(2)}) async-start(), calls=%async_computation.3 | async-start | bytes 1179648 | tf_op jit(solution)/shard_map/all_gather | solution.py:263
  7.3 7.5 %copy-start.40 = (f32[8]{0:T(128)}, f32[8]{0:T(128)S(1)}, u32[]{:S(2)}) copy-start(f32[8]{0:T(128)S(1)} %multiply_power_fusion) | copy-start | bytes 100
  11.2 11.0 %copy-start.39 = (f32[4,128]{1,0:T(4,128)}, f32[4,128]{1,0:T(4,128)S(1)}, u32[]{:S(2)}) copy-start(f32[4,128]{1,0:T(4,128)S(1)} %get-tuple-element.73) | copy-start | bytes 6148
  12.8 9.4 %copy-start.44 = (f32[4,128]{1,0:T(4,128)}, f32[4,128]{1,0:T(4,128)S(1)}, u32[]{:S(2)}) copy-start(f32[4,128]{1,0:T(4,128)S(1)} %get-tuple-element.70) | copy-start | bytes 6148
  13.4 3.6 %copy-start.1 = (bf16[4,128,768]{2,1,0:T(8,128)(2,1)S(1)}, bf16[4,128,768]{2,1,0:T(8,128)(2,1)}, u32[]{:S(2)}) copy-start(bf16[4,128,768]{2,1,0:T(8,128)(2,1)} %param.19) | copy-start | bytes 2359300
  16.9 93.9 %reduce-scatter.4.cloned.1.call-start = ((), (), s32[]{:S(2)}) async-start(), calls=%async_computation.4 | async-start | bytes 1179648 | tf_op jit(solution)/shard_map/reduce_scatter | solution.py:282
  56.9 120.6 %reduce-scatter.6.cloned.1.call-start = ((), (), s32[]{:S(2)}) async-start(), calls=%async_computation.5 | async-start | bytes 2875392 | tf_op jit(solution)/shard_map/reduce_scatter | solution.py:306
  65.4 46.3 %copy-start.27 = (f32[4,128]{1,0:T(4,128)S(1)}, f32[4,128]{1,0:T(4,128)}, u32[]{:S(2)}) copy-start(f32[4,128]{1,0:T(4,128)} %copy-done.26) | copy-start | bytes 6148
  65.4 46.3 %copy-start.41 = (f32[8]{0:T(128)S(1)}, f32[8]{0:T(128)}, u32[]{:S(2)}) copy-start(f32[8]{0:T(128)} %copy-done.40) | copy-start | bytes 100
  68.5 46.8 %copy-start.18 = (bf16[512,768]{1,0:T(8,128)(2,1)S(1)}, bf16[512,768]{1,0:T(8,128)(2,1)}, u32[]{:S(2)}) copy-start(bf16[512,768]{1,0:T(8,128)(2,1)} %copy-done.17) | copy-start | bytes 2359300
  120.8 123.8 %reduce-scatter.8.cloned.1.call-start = ((), (), s32[]{:S(2)}) async-start(), calls=%async_computation.6 | async-start | bytes 10616832 | tf_op jit(solution)/shard_map/reduce_scatter | solution.py:306
  167.8 147.5 %all-reduce.3.cloned.1.call-start = ((), (), s32[]{:S(2)}) async-start(), calls=%async_computation.7 | async-start | bytes 2998272 | tf_op jit(solution)/shard_map/psum | solution.py:307
  169.7 3.5 %copy-start.25 = (bf16[768,128]{1,0:T(8,128)(2,1)S(1)}, bf16[768,128]{1,0:T(8,128)(2,1)}, u32[]{:S(2)}) copy-start(bf16[768,128]{1,0:T(8,128)(2,1)} %param.26) | copy-start | bytes 589828
  174.8 69.8 %copy-start.37 = (f32[768]{0:T(1024)S(1)}, f32[768]{0:T(1024)}, u32[]{:S(2)}) copy-start(f32[768]{0:T(1024)} %convert_reduce_fusion.2) | copy-start | bytes 9220
  174.8 69.8 %copy-start.46 = (f32[128]{0:T(128)S(1)}, f32[128]{0:T(128)}, u32[]{:S(2)}) copy-start(f32[128]{0:T(128)} %get-tuple-element.48) | copy-start | bytes 1540
  177.4 111.5 %copy-start.16 = (bf16[4,128,768]{2,1,0:T(8,128)(2,1)S(1)}, bf16[4,128,768]{2,1,0:T(8,128)(2,1)}, u32[]{:S(2)}) copy-start(bf16[4,128,768]{2,1,0:T(8,128)(2,1)} %param.17) | copy-start | bytes 2359300
  288.8 36.5 %copy-start.38 = (f32[768]{0:T(1024)}, f32[768]{0:T(1024)S(1)}, u32[]{:S(2)}) copy-start(f32[768]{0:T(1024)S(1)} %get-tuple-element.110) | copy-start | bytes 9220
  315.4 4.1 %copy-start.19 = (bf16[1152,512]{1,0:T(8,128)(2,1)S(1)}, bf16[1152,512]{1,0:T(8,128)(2,1)}, u32[]{:S(2)}) copy-start(bf16[1152,512]{1,0:T(8,128)(2,1)} %get-tuple-element.47) | copy-start | bytes 3538948
  (28 other events, 44.9 us)
Sparse Core Ops, SparseCore 0:
  17.0 26.2 all-gather.1
  57.0 53.7 reduce-scatter.3
  120.9 43.3 reduce-scatter.5
  168.0 76.5 reduce-scatter.7
  247.0 68.2 all-reduce.2

commit v2 on v1

--- a/solution.py
+++ b/solution.py
@@ -168,58 +168,432 @@
     )(own, lengths, q, do, kv, cosine, sine)
 
 
-def ffn_kernel(h_ref, ht_ref, dy_ref, wu_ref, wd_ref, bu_ref, fo_ref, dh_ref, gu_ref, gd_ref, gb_ref):
-    step = pl.program_id(0)
-    h, dy, wu, wd = h_ref[...], dy_ref[...], wu_ref[...], wd_ref[...]
-    up = dot(h, wu) + bu_ref[...]
-    d_act = dot_nt(dy, wd)
+MESH = pl.DeviceIdType.MESH
+RING = 5
+SLOTS = 3
+
+
+def bits_of(value, count):
+    return [value // 2**i % 2 for i in range(count)]
+
+
+class Net:
+    def __init__(self, seq_bits, row_bits):
+        self.a, self.b = seq_bits, row_bits
+        self.me, self.row = lax.axis_index("seq"), lax.axis_index("rows")
+        self.sb, self.rb = bits_of(self.me, seq_bits), bits_of(self.row, row_bits)
+
+    def seq_xor(self, mask):
+        out = self.me
+        for i in range(self.a):
+            if mask >> i & 1:
+                out = out + (1 - 2 * self.sb[i]) * 2**i
+        return {"seq": out}
+
+    def row_xor(self, mask):
+        out = self.row
+        for i in range(self.b):
+            if mask >> i & 1:
+                out = out + (1 - 2 * self.rb[i]) * 2**i
+        return {"rows": out}
+
+    def greet(self):
+        barrier = pltpu.get_barrier_semaphore()
+        peers = [self.seq_xor(m) for m in range(1, 2**self.a)] + [self.row_xor(m) for m in range(1, 2**self.b)]
+        for peer in peers:
+            pl.semaphore_signal(barrier, inc=1, device_id=peer, device_id_type=MESH)
+        pl.semaphore_wait(barrier, len(peers))
+
+    def pick(self, left, bit, mine):
+        own = self.sb[bit]
+        return tuple((own if mine else 1 - own) if i == bit else slice(None) for i in left)
+
+
+def remote(src, dst, send_sem, recv_sem, peer):
+    return pltpu.make_async_remote_copy(
+        src_ref=src, dst_ref=dst, send_sem=send_sem, recv_sem=recv_sem, device_id=peer, device_id_type=MESH
+    )
+
+
+class Ring:
+    def __init__(self, net, total, grads, recs, recz, fin, send_sem, recv_sem):
+        self.net, self.total = net, total
+        self.grads, self.recs, self.recz, self.fin = grads, recs, recz, fin
+        self.send_sem, self.recv_sem = send_sem, recv_sem
+        a, b = net.a, net.b
+        self.halves = min(b, 2)
+        self.stages = [("first", 0)] + [("seq", k) for k in range(1, a)]
+        self.stages += [("split", i) for i in range(self.halves)]
+        self.stages += [("whole", i) for i in range(2, b)]
+        self.stages += [("back", i) for i in reversed(range(self.halves))]
+        self.sem_at, n = [], 0
+        for kind, _ in self.stages:
+            self.sem_at.append(n)
+            n += 2 if kind == "seq" else 1
+
+    def moves(self, stage, ch):
+        net, a = self.net, self.net.a
+        kind, k = self.stages[stage]
+        if kind == "first":
+            left = range(a - 1, -1, -1)
+            slot, at = (ch % SLOTS,), (ch % RING,)
+            return [(self.grads.at[slot + net.pick(left, 0, False)], self.recs[0].at[at], net.seq_xor(1),
+                     (self.grads, slot + net.pick(left, 0, True)), (self.recs[0], at))]
+        if kind == "seq":
+            out = []
+            prev, here = self.recs[k - 1], self.recs[k]
+            for half in (0, 1):
+                if half == 0:
+                    bit, left = k, range(a - 1, k - 1, -1)
+                else:
+                    bit, left = a - k, range(a - k, 0, -1)
+                if k == 1:
+                    base, tail = (ch % RING,), (half,)
+                else:
+                    base, tail = (ch, half), ()
+                out.append((prev.at[base + net.pick(left, bit, False) + tail], here.at[ch, half], net.seq_xor(1 << bit),
+                            (prev, base + net.pick(left, bit, True) + tail), (here, (ch, half))))
+            return out
+        if kind == "split":
+            prev = self.recs[a - 1] if k == 0 else self.recz[k - 1]
+            return [(prev.at[ch, 1 - net.rb[k]], self.recz[k].at[ch], net.row_xor(1 << k),
+                     (prev, (ch, net.rb[k])), (self.recz[k], (ch,)))]
+        if kind == "whole":
+            prev = self.recz[k - 1]
+            return [(prev.at[ch], self.recz[k].at[ch], net.row_xor(1 << k), (prev, (ch,)), (self.recz[k], (ch,)))]
+        at = (ch,) + tuple(net.rb[: k + 1])
+        return [(self.fin.at[at], self.fin.at[at], net.row_xor(1 << k), None, None)]
+
+    def copies(self, stage, ch):
+        out = []
+        for i, (src, dst, peer, _, _) in enumerate(self.moves(stage, ch)):
+            sem = self.sem_at[stage] + i
+            out.append(remote(src, dst, self.send_sem.at[ch, sem], self.recv_sem.at[ch, sem], peer))
+        return out
+
+    def start(self, stage, ch):
+        for copy in self.copies(stage, ch):
+            copy.start()
+
+    def finish(self, stage, ch):
+        for copy in self.copies(stage, ch):
+            copy.wait()
+        kind, _ = self.stages[stage]
+        if kind != "back":
+            last = self.stages[stage + 1][0] == "back"
+            for _, _, _, (src, src_at), (dst, dst_at) in self.moves(stage, ch):
+                total = src[src_at] + dst[dst_at]
+                if last:
+                    self.fin[(ch,) + tuple(self.net.rb[: self.halves])] = total
+                else:
+                    dst[dst_at] = total
+        if stage + 1 < len(self.stages):
+            self.start(stage + 1, ch)
+
+    def tick(self, t):
+        for stage in reversed(range(len(self.stages))):
+            ch = t - 1 - stage
+            if isinstance(ch, int):
+                if 0 <= ch < self.total:
+                    self.finish(stage, ch)
+            else:
+
+                @pl.when((ch >= 0) & (ch < self.total))
+                def _():
+                    self.finish(stage, ch)
+
+
+CHUNK = 512
+QUARTER = 128
+
+
+def put_chunk(grads, slot, a, owner, sub, value, quarters):
+    at = (slot,) + tuple(reversed(bits_of(owner, a)))
+    for i, q in enumerate(quarters):
+        grads[at + (q // 2, q % 2)] = value[:, i * QUARTER : (i + 1) * QUARTER].astype(BF)
+
+
+def gelu_parts(up):
     cdf = 0.5 + 0.5 * lax.erf(up * 0.7071067811865476)
-    act = (up * cdf).astype(BF)
     pdf = jnp.exp(-0.5 * up * up) * 0.3989422804014327
-    d_up = (d_act * (cdf + up * pdf)).astype(BF)
-    gb_ref[...] = jnp.sum(d_up.astype(F32), axis=0, keepdims=True)
-
-    @pl.when(step == 0)
-    def _():
-        fo_ref[...] = jnp.zeros_like(fo_ref)
-        dh_ref[...] = jnp.zeros_like(dh_ref)
-
-    fo_ref[...] += dot(act, wd)
-    dh_ref[...] += dot_nt(d_up, wu)
-    gu_ref[...] = dot(ht_ref[...], d_up).astype(BF)
-    gd_ref[...] = dot_tn(act, dy).astype(BF)
-
-
-def ffn(h, dy, wu, wd, bu, cols=768):
-    toks, width = h.shape
+    return cdf, up * pdf
+
+
+def lanes_mean(v):
+    return jnp.mean(v, axis=-1, keepdims=True)
+
+
+def tail_kernel(
+    seq_bits, row_bits,
+    x_ref, dy_ref, h1_ref, h2_ref, mt_ref, mx_ref, dq_ref, dkv_ref, turn_ref, vec_ref, bu_ref,
+    wq_hbm, wkv_hbm, wo_hbm, wu_hbm, wd_hbm,
+    lo_ref, ig_ref, gup_ref, gdown_ref, gout_ref, gq_ref, gkv_ref, small_ref,
+    wq, wkv, wo, wu, wd, load_sem,
+    h1t, h2t, act, act_t, dup, gub,
+    grads, *rest,
+):
+    a, n = seq_bits, 2**seq_bits
+    recs, rest = rest[:a], rest[a:]
+    recz, rest = rest[:row_bits], rest[row_bits:]
+    fin, send_sem, recv_sem, rest = rest[0], rest[1], rest[2], rest[3:]
+    kvr, rest = rest[:a], rest[a:]
+    kv_send, kv_recv, own_kv, seq_kv, row_kv, own_small, seq_small, row_small, m_send, m_recv = rest
+    net = Net(seq_bits, row_bits)
+    total = 2 * 6 + 3
+    ring = Ring(net, total, grads, recs, recz, fin, send_sem, recv_sem)
+    toks, width = x_ref.shape
     hidden = wu.shape[1]
-
-    def full(*shape):
-        return pl.BlockSpec(shape, lambda i: (0,) * len(shape))
-
-    up_spec = pl.BlockSpec((width, cols), lambda i: (0, i))
-    down_spec = pl.BlockSpec((cols, width), lambda i: (i, 0))
-    bias_spec = pl.BlockSpec((1, cols), lambda i: (0, i))
+    sub = width // n
+    loads = []
+    for i, (src, dst) in enumerate(((wu_hbm, wu), (wd_hbm, wd), (wo_hbm, wo), (wq_hbm, wq), (wkv_hbm, wkv))):
+        loads.append(pltpu.make_async_copy(src, dst, load_sem.at[i]))
+        loads[-1].start()
+    net.greet()
+
+    def kv_moves(k):
+        out = []
+        for half in (0, 1):
+            if k == 0:
+                bit, left = 0, range(a - 1, -1, -1)
+            elif half == 0:
+                bit, left = k, range(a - 1, k - 1, -1)
+            else:
+                bit, left = a - k, range(a - k, 0, -1)
+            prev = dkv_ref if k == 0 else kvr[k - 1]
+            sem = 2 * k + half
+            at = (half, slice(None))
+            out.append((remote(prev.at[at + net.pick(left, bit, False)], kvr[k].at[half],
+                               kv_send.at[sem], kv_recv.at[sem], net.seq_xor(1 << bit)),
+                        prev, at + net.pick(left, bit, True), half))
+        return out
+
+    def kv_start(k):
+        for copy, *_ in kv_moves(k):
+            copy.start()
+
+    def kv_finish(k):
+        for copy, prev, at, half in kv_moves(k):
+            copy.wait()
+            kvr[k][half] = kvr[k][half] + prev[at]
+        if k + 1 < a:
+            kv_start(k + 1)
+
+    kv_start(0)
+
+    h1t[...] = h1_ref[...].T
+    h2t[...] = h2_ref[...].T
+    dy = dy_ref[...]
+
+    def rows_of(ref, owner):
+        return ref[owner * sub : (owner + 1) * sub, :]
+
+    for owner in range(n):
+        put_chunk(grads, 0, a, owner, sub, dot(rows_of(mt_ref, owner), dy[:, :CHUNK]), (0, 1, 2, 3))
+    ring.start(0, 0)
+    ring.tick(0)
+    kv_finish(0)
+    for owner in range(n):
+        put_chunk(grads, 1, a, owner, sub, dot(rows_of(mt_ref, owner), dy[:, CHUNK:]), (0, 1))
+        put_chunk(grads, 1, a, owner, sub, dot(rows_of(h1t, owner), dq_ref[:, :256]), (2, 3))
+    ring.start(0, 1)
+    ring.tick(1)
+    kv_finish(1)
+    for owner in range(n):
+        put_chunk(grads, 2, a, owner, sub, dot(rows_of(h1t, owner), dq_ref[:, 256:]), (0, 1, 2, 3))
+    ring.start(0, 2)
+    ring.tick(2)
+    for k in range(2, a):
+        kv_finish(k)
+    loads[0].wait()
+    loads[1].wait()
+
+    def feed(f, _):
+        cols = pl.ds(pl.multiple_of(f * CHUNK, CHUNK), CHUNK)
+        ch = 3 + f
+        up = dot(h2_ref[...], wu[:, cols]) + bu_ref[:, cols]
+        d_act = dot_nt(dy_ref[...], wd[cols, :])
+        cdf, slope = gelu_parts(up)
+        low = (up * cdf).astype(BF)
+        d_up = (d_act * (cdf + slope)).astype(BF)
+        act[:, cols] = low
+        act_t[cols, :] = low.T
+        dup[:, cols] = d_up
+        gub[:, cols] = jnp.sum(d_up.astype(F32), axis=0, keepdims=True)
+        for owner in range(n):
+            put_chunk(grads, ch % SLOTS, a, owner, sub, dot(rows_of(h2t, owner), d_up), (0, 1, 2, 3))
+        ring.start(0, ch)
+        ring.tick(ch)
+        return 0
+
+    lax.fori_loop(0, hidden // CHUNK, feed, 0)
+
+    def down(i, _):
+        cols = pl.ds(pl.multiple_of(i * 256, 256), 256)
+        part = dy_ref[:, cols]
+        for owner in range(n):
+            g = dot(act_t[owner * 4 * sub : (owner + 1) * 4 * sub, :], part)
+            at = tuple(reversed(bits_of(owner, a)))
+            for u in (0, 1):
+                for q in range(4):
+                    grads[((9 + 2 * i + u) % SLOTS,) + at + (q // 2, q % 2)] = g[
+                        q * sub : (q + 1) * sub, u * 128 : (u + 1) * 128
+                    ].astype(BF)
+        for u in (0, 1):
+            ring.start(0, 9 + 2 * i + u)
+            ring.tick(9 + 2 * i + u)
+        return 0
+
+    lax.fori_loop(0, width // 256, down, 0)
+
+    d_kv = kvr[a - 1][...].reshape(toks, 2 * HD).astype(F32)
+    d_kv = d_kv * turn_ref[0] + pltpu.roll(d_kv, 2 * HD - 8, 1) * turn_ref[1] + pltpu.roll(d_kv, 8, 1) * turn_ref[2]
+    d_kv = d_kv.astype(BF)
+    for owner in range(n):
+        own_kv[owner] = dot(rows_of(h1t, owner), d_kv).astype(BF)
+    ring.tick(total)
+    second_grad = dot_nt(dup[...], wu[...])
+    ring.tick(total + 1)
+    for load in loads[2:]:
+        load.wait()
+    first_grad = dot_nt(dq_ref[...], wq[...]) + dot_nt(d_kv, wkv[...])
+    x = x_ref[...].astype(F32)
+    centred = x - lanes_mean(x)
+    factor = lax.rsqrt(lanes_mean(centred * centred) + EPS)
+    xhat = centred * factor
+    at = 0
+
+    def keep(vector):
+        nonlocal at
+        for i in range(vector.shape[1] // 128):
+            own_small[at : at + 1, :] = vector[:, i * 128 : (i + 1) * 128]
+            at += 1
+
+    def column_sum(v):
+        return jnp.sum(v, axis=0, keepdims=True)
+
+    own_small[...] = jnp.zeros(own_small.shape, F32)
+    dy32 = dy_ref[...].astype(F32)
+    result = dy32
+    for grad, gain in ((first_grad, vec_ref[0:1, :]), (second_grad, vec_ref[1:2, :])):
+        keep(column_sum(grad * xhat))
+        keep(column_sum(grad))
+        g = grad * gain
+        result = result + factor * (g - lanes_mean(g) - xhat * lanes_mean(g * xhat))
+    ig_ref[...] = result.astype(BF)
+    keep(column_sum(dq_ref[...].astype(F32)))
+    keep(column_sum(d_kv.astype(F32)))
+    keep(column_sum(dy32))
+    keep(gub[...])
+
+    def narrow(step):
+        out = []
+        if step == 0:
+            for m in range(1, n):
+                peer = net.seq_xor(m)
+                out.append(remote(own_kv.at[peer["seq"]], seq_kv.at[m - 1], m_send.at[m - 1], m_recv.at[m - 1], peer))
+                out.append(remote(own_small, seq_small.at[net.me], m_send.at[n + m - 2], m_recv.at[n + m - 2], peer))
+            return out
+        base = 2 * (n - 1)
+        count = 2**row_bits
+        for m in range(1, count):
+            peer = net.row_xor(m)
+            k = base + 2 * (m - 1)
+            out.append(remote(row_kv.at[net.row], row_kv.at[net.row], m_send.at[k], m_recv.at[k], peer))
+            out.append(remote(row_small.at[net.row], row_small.at[net.row], m_send.at[k + 1], m_recv.at[k + 1], peer))
+        return out
+
+    for copy in narrow(0):
+        copy.start()
+    ring.tick(total + 2)
+    ffn_out = dot(act[...], wd[...])
+    ring.tick(total + 3)
+    for copy in narrow(0):
+        copy.wait()
+    seq_small[net.me] = own_small[...]
+    sums = own_kv[net.me].astype(F32)
+    for m in range(1, n):
+        sums = sums + seq_kv[m - 1].astype(F32)
+    row_kv[net.row] = sums.astype(BF)
+    sums = seq_small[0]
+    for i in range(1, n):
+        sums = sums + seq_small[i]
+    row_small[net.row] = sums
+    for copy in narrow(1):
+        copy.start()
+    ring.tick(total + 4)
+    lo_ref[...] = (x + dot(mx_ref[...], wo[...]) + ffn_out + vec_ref[2:3, :]).astype(BF)
+    for t in range(total + 5, total + len(ring.stages) + 1):
+        ring.tick(t)
+    for copy in narrow(1):
+        copy.wait()
+    sums, kv_sums = row_small[0], row_kv[0].astype(F32)
+    for i in range(1, 2**row_bits):
+        sums = sums + row_small[i]
+        kv_sums = kv_sums + row_kv[i].astype(F32)
+    small_ref[...] = sums
+    gkv_ref[...] = kv_sums
+    for q in range(4):
+        def piece(ch):
+            return fin[ch, q // 2, q % 2].astype(F32)
+
+        lanes = slice(q * 128, (q + 1) * 128)
+        gout_ref[:, lanes] = piece(0)
+        gq_ref[:, 256 + q * 128 : 384 + q * 128] = piece(2)
+        if q < 2:
+            gout_ref[:, CHUNK + q * 128 : CHUNK + (q + 1) * 128] = piece(1)
+        else:
+            gq_ref[:, (q - 2) * 128 : (q - 1) * 128] = piece(1)
+        for f in range(hidden // CHUNK):
+            gup_ref[:, f * CHUNK + q * 128 : f * CHUNK + (q + 1) * 128] = piece(3 + f)
+        for j in range(width // 128):
+            gdown_ref[q * sub : (q + 1) * sub, j * 128 : (j + 1) * 128] = piece(3 + hidden // CHUNK + j)
+
+
+def tail(net_bits, x, dy, h1, h2, mixed_t, mixed, dq, dkv, turn, vec, bu, wq, wkv, wo, wu, wd):
+    a, b = net_bits
+    n, count = 2**a, 2**b
+    toks, width = x.shape
+    hidden = wu.shape[1]
+    sub = width // n
+    total = 3 + hidden // CHUNK + width // 128
+    rows = dkv.shape[1] * 2
+    two = (2,)
+    vm = pltpu.VMEM
+    dma = pltpu.SemaphoreType.DMA
+    n_sems = 1 + 2 * (a - 1) + b + min(b, 2)
+    scratch = [
+        vm(wq.shape, BF), vm(wkv.shape, BF), vm(wo.shape, BF), vm(wu.shape, BF), vm(wd.shape, BF), dma((5,)),
+        vm((width, toks), BF), vm((width, toks), BF), vm((toks, hidden), BF), vm((hidden, toks), BF), vm((toks, hidden), BF),
+        vm((1, hidden), F32),
+        vm((SLOTS,) + two * a + (2, 2, sub, 128), BF),
+        vm((RING,) + two * (a - 1) + (2, 2, sub, 128), BF),
+    ]
+    scratch += [vm((total, 2) + two * (a - 1 - k) + (2, sub, 128), BF) for k in range(1, a)]
+    scratch += [vm((total, 2, sub, 128), BF)] + [vm((total, sub, 128), BF) for _ in range(1, b)]
+    scratch += [vm((total, 2, 2, sub, 128), BF), dma((total, n_sems)), dma((total, n_sems))]
+    scratch += [vm((2, rows // 2) + two * (a - 1 - k) + (BLK, 2 * HD), BF) for k in range(a)]
+    scratch += [
+        dma((2 * a,)), dma((2 * a,)),
+        vm((n, sub, 128), BF), vm((n - 1, sub, 128), BF), vm((count, sub, 128), BF),
+        vm((64, 128), F32), vm((n, 64, 128), F32), vm((count, 64, 128), F32),
+        dma((2 * (n + count),)), dma((2 * (n + count),)),
+    ]
+    vmem = pl.BlockSpec(memory_space=pltpu.VMEM)
+    hbm = pl.BlockSpec(memory_space=pl.ANY)
+    shape = jax.ShapeDtypeStruct
     return pl.pallas_call(
-        ffn_kernel,
-        grid=(hidden // cols,),
-        in_specs=[full(toks, width), full(width, toks), full(toks, width), up_spec, down_spec, bias_spec],
-        out_specs=[full(toks, width), full(toks, width), up_spec, down_spec, bias_spec],
+        functools.partial(tail_kernel, a, b),
         out_shape=[
-            jax.ShapeDtypeStruct((toks, width), F32),
-            jax.ShapeDtypeStruct((toks, width), F32),
-            jax.ShapeDtypeStruct((width, hidden), BF),
-            jax.ShapeDtypeStruct((hidden, width), BF),
-            jax.ShapeDtypeStruct((1, hidden), F32),
+            shape((toks, width), BF), shape((toks, width), BF),
+            shape((sub, hidden), F32), shape((4 * sub, width), F32), shape((sub, width), F32), shape((sub, width), F32),
+            shape((sub, 2 * HD), F32), shape((64, 128), F32),
         ],
-        compiler_params=pltpu.CompilerParams(
-            vmem_limit_bytes=50 * 2**20, dimension_semantics=("arbitrary",)
-        ),
-        cost_estimate=pl.CostEstimate(
-            flops=12 * toks * width * hidden, bytes_accessed=8 * width * hidden, transcendentals=2 * toks * hidden
-        ),
-        name="feed_forward",
-    )(h, h.T, dy, wu, wd, bu[None, :])
+        in_specs=[vmem] * 11 + [hbm] * 5,
+        out_specs=[vmem] * 8,
+        scratch_shapes=scratch,
+        compiler_params=pltpu.CompilerParams(collective_id=0, has_side_effects=True, vmem_limit_bytes=60 * 2**20),
+        name="tail",
+    )(x, dy, h1, h2, mixed_t, mixed, dq, dkv, turn, vec, bu, wq, wkv, wo, wu, wd)
 
 
 def rotate_t(values, cosine, sine):
@@ -262,8 +636,6 @@
     ).astype(BF)
     kv_full = lax.all_gather(kv_low, "seq", axis=1, tiled=True)
 
-    ffn_out, second_grad, g_up, g_down, g_up_bias = ffn(h2, dy, up_weight, down_weight, up_bias)
-
     q = jnp.einsum("rtd,de->ret", h1.reshape(rows, block, width), query_weight, preferred_element_type=F32)
     q = (q + query_bias[None, :, None]).reshape(rows, heads, HD, block)
     q = (rotate_t(q, cosine[:, None], sine[:, None]).astype(BF) * 0.125).astype(BF)
@@ -272,74 +644,33 @@
     do = do.astype(BF).reshape(rows, heads, HD, block).transpose(0, 2, 1, 3).reshape(rows, HD, heads * block)
 
     mixed_t, mixed, dq, dkv = attention(own[None], lengths, q, do, kv_full, cosine, sine)
-    mixed = mixed.reshape(toks, width)
-    dq = dq.reshape(toks, width)
-    layer_output = x + dot(mixed, output_weight) + output_bias + ffn_out + down_bias
-    layer_output = layer_output.astype(BF).reshape(rows, block, width)
-    g_out = jnp.einsum("ret,rtd->ed", mixed_t, cotangent, preferred_element_type=F32)
-    g_query = dot_tn(h1, dq)
-
-    dkv = lax.psum_scatter(dkv, "seq", scatter_dimension=1, tiled=True).astype(F32)
-    front, behind = dkv[..., :8], dkv[..., 8:16]
-    d_kv = jnp.concatenate(
-        [front * cos_k + behind * sin_k, behind * cos_k - front * sin_k, dkv[..., 16:]], axis=-1
-    ).astype(BF).reshape(toks, 2 * HD)
-    g_kv = dot_tn(h1, d_kv)
-    first_grad = dot_nt(dq, query_weight) + dot_nt(d_kv, keyvalue_weight)
-
-    def norm_back(grad, gain):
-        g = grad * gain
-        return factor * (
-            g - jnp.mean(g, axis=-1, keepdims=True) - xhat * jnp.mean(g * xhat, axis=-1, keepdims=True)
-        )
-
-    input_grad = dy32 + norm_back(first_grad, first_gain) + norm_back(second_grad, second_gain)
-    input_grad = input_grad.astype(BF).reshape(rows, block, width)
-
-    seq_size = lax.axis_size("seq")
-
-    def by_owner(g):
-        return g.astype(BF).reshape(seq_size, -1, 512)
-
-    def summed(parts):
-        joined = jnp.concatenate([by_owner(g) for g in parts], axis=1)
-        part = lax.psum_scatter(joined, "seq", scatter_dimension=0, tiled=True)[0]
-        return lax.psum(part, "rows").astype(F32)
-
-    first = summed([g_up, g_down])
-    second = summed([g_out, g_query, g_kv])
-
-    def split(part, shapes):
-        outs, at = [], 0
-        for shape in shapes:
-            n = shape[0] * shape[1] // 512
-            outs.append(part[at : at + n].reshape(shape))
-            at += n
-        return outs
-
-    sub = width // seq_size
-    hid = up_weight.shape[1]
-    s_up, s_down = split(first, [(sub, hid), (hid // seq_size, width)])
-    s_out, s_query, s_kv = split(second, [(sub, width), (sub, width), (sub, 2 * HD)])
-
-    small = lax.psum(
-        jnp.concatenate([
-            jnp.sum(first_grad * xhat, axis=0), jnp.sum(first_grad, axis=0),
-            jnp.sum(second_grad * xhat, axis=0), jnp.sum(second_grad, axis=0),
-            jnp.sum(dq.astype(F32), axis=0), jnp.sum(d_kv.astype(F32), axis=0),
-            jnp.sum(dy32, axis=0), g_up_bias[0],
-        ]),
-        ("seq", "rows"),
+    seq_bits = lax.axis_size("seq").bit_length() - 1
+    row_bits = lax.axis_size("rows").bit_length() - 1
+    ones = jnp.ones((rows, block, 2 * HD - ROT), F32)
+    zeros = jnp.zeros((rows, block, 8), F32)
+    far = jnp.zeros((rows, block, 2 * HD - ROT), F32)
+    turn = jnp.stack([
+        jnp.concatenate([cos_k, cos_k, ones], axis=-1),
+        jnp.concatenate([sin_k, zeros, far], axis=-1),
+        jnp.concatenate([zeros, -sin_k, far], axis=-1),
+    ]).reshape(3, toks, 2 * HD)
+    vec = jnp.stack([first_gain, second_gain, output_bias + down_bias])
+    layer_output, input_grad, s_up, s_down, s_out, s_query, s_kv, small = tail(
+        (seq_bits, row_bits), hidden.reshape(toks, width), dy, h1, h2,
+        mixed_t.swapaxes(0, 1).reshape(width, toks), mixed.reshape(toks, width), dq.reshape(toks, width),
+        dkv.reshape((2, rows // 2) + (2,) * seq_bits + (block, 2 * HD)), turn, vec, up_bias[None, :],
+        query_weight, keyvalue_weight, output_weight, up_weight, down_weight,
     )
-    sizes = [width] * 5 + [2 * HD, width, hid]
+    sizes = [width] * 5 + [2 * HD, width, up_weight.shape[1]]
+    small = small.reshape(-1)
     pieces, at = [], 0
     for size in sizes:
         pieces.append(small[at : at + size])
         at += size
     s_fg, s_fs, s_sg, s_ss, s_qb, s_kb, s_ob, s_ub = pieces
     return (
-        layer_output, input_grad, s_fg, s_fs, s_sg, s_ss, s_query, s_qb, s_kv, s_kb,
-        s_out, s_ob, s_up, s_ub, s_down, s_ob,
+        layer_output.reshape(hidden.shape), input_grad.reshape(hidden.shape),
+        s_fg, s_fs, s_sg, s_ss, s_query, s_qb, s_kv, s_kb, s_out, s_ob, s_up, s_ub, s_down, s_ob,
     )
 
 

time: 336 us -> 205 us (0.61)
  waiting for transfers between devices: 143 us -> 13.6 us
  Pallas kernels: 27.8 us -> 136 us
  blocking collectives: 42.4 us -> 0 us
  local copies, waits for them, and re-layouts: 58.5 us -> 20.3 us
  other arithmetic: 27.9 us -> 13.5 us
  matrix products: 18.4 us -> 4.51 us
    reduce_scatter x3 -> x0, waiting for transfers between devices: 109 us -> none  [the longest x2 67.1 us: summed(): part = lax.psum_scatter(joined, 'seq', scatter_dimension=0, tiled=True)[0]]
    pallas_call x1, Pallas kernels: 19.4 us -> 127 us  [tail(): pl.pallas_call(functools.partial(tail_kernel, a, b), out_shape=[shape((to...]
    psum x1 -> x0, blocking collectives: 42.4 us -> none  [shards(): lax.psum(jnp.concatenate([jnp.sum(first_grad * xhat, axis=0), jnp.sum(fir...]
    reshape x10 -> x1, local copies, waits for them, and re-layouts: 31.3 us -> 0.96 us  [shards(): mixed_t.swapaxes(0, 1).reshape(width, toks)]
    psum x1 -> x0, waiting for transfers between devices: 23.3 us -> none  [summed(): return lax.psum(part, 'rows').astype(F32)]
    concatenate x2 -> x0, other arithmetic: 10.9 us -> none  [summed(): joined = jnp.concatenate([by_owner(g) for g in parts], axis=1)]
    dot_general x5 -> x0, matrix products: 9.22 us -> none  [the longest x2 4.55 us: dot_tn(): lax.dot_general(a, b, (((0,), (0,)), ((), ())), preferred_element_type=F32)]
    slice x4 -> x0, local copies, waits for them, and re-layouts: 4.64 us -> none  [the longest x3 3.64 us: split(): outs.append(part[at:at + n].reshape(shape))]
  transfers between devices with their start and end apart: 5 -> 1, of which waited for: 4 -> 1; matrix products, arithmetic and copies ran while one was open for 20% -> 6% of each run, Pallas kernels for 6% -> 0%
where the time goes in v2:
time: 205 us; the launch traced here: 202 us
  Pallas kernels  136 us (66%)
  local copies, waits for them, and re-layouts  20.3 us (10%)
  between operations  14.5 us (7%)
  waiting for transfers between devices  13.6 us (7%)
  other arithmetic  13.5 us (7%)
  matrix products  4.51 us (2%)
    pallas_call x1, Pallas kernels, tail(): pl.pallas_call(functools.partial(tail_kernel, a, b), out_shape=[shape((to...  127 us
    all_gather x1, waiting for transfers between devices, shards(): kv_full = lax.all_gather(kv_low, 'seq', axis=1, tiled=True)  13.5 us
    unnamed x82, local copies, waits for them, and re-layouts  9.62 us
    pallas_call x1, Pallas kernels, attention(): pl.pallas_call(attn_kernel, grid_spec=pltpu.PrefetchScalarGridSpec(num_sc...  8.41 us
  transfers between devices with their start and end apart: 1, of which 1 were waited for; matrix products, arithmetic and copies ran while one was open for 6% of the time, Pallas kernels for 0%

profile of v2, /device:TPU:0, one launch (start us, length us, event | category | flops | bytes accessed | tf_op | source)
XLA Modules:
  0.0 202.1 jit_solution(2768803331777524227)
XLA Ops:
  8.6 1.3 slice_reduce_fusion.2
  9.9 1.3 slice_reduce_fusion
  11.2 1.3 convert_reduce_fusion
  12.6 1.5 multiply_reduce_fusion
  14.8 1.4 add_convert_fusion.1
  16.8 1.2 fusion.13
  20.7 0.8 convolution_convert_fusion
  22.7 3.3 %add_bitcast_fusion = f32[4,768,128]{1,2,0:T(8,128)} fusion(bf16[768,768]{1,0:T(8,128)(2,1)} %wq_hbm.1, bf16[4,128,768]{2,1,0:T(8,128)(2,1)S(1)} %copy-done.3, f32[768]{0:T(1024)S(1)} %copy-done.36, f32[768]{0:T(1024)S(1)} %copy-done.31, f32[768]{0:T(1024)S(1)} %copy-done.15, f32[4,128]{1,0:T(4,128)S(1)} %copy-done.32, f32[4,128]{1,0:T(4,128)S(1)} %copy-done.20), kind=kOutput, calls=%fused_computation.2 | convolution fusion | flops 606732288 | bytes 3552256 | tf_op jit(solution)/shard_map/rtd,de->ret/dot_general | solution.py:639
  26.1 1.9 copy.42
  29.1 1.0 multiply_cosine_fusion
  30.2 1.3 maximum_maximum_fusion.turn_ref
  31.6 13.5 %all-gather.2.cloned.1.call-done.kv_ref = bf16[4,1024,128]{2,1,0:T(8,128)(2,1)} async-done(((bf16[4,128,128]{2,1,0:T(8,128)(2,1)}), bf16[4,1024,128]{2,1,0:T(8,128)(2,1)}) %all-gather.2.cloned.1.call-update) | async-done | bytes 1048592 | tf_op jit(solution)/shard_map/all_gather | solution.py:637
  45.2 8.4 %attention.1 = (bf16[4,768,128]{2,1,0:T(8,128)(2,1)S(1)}, bf16[4,128,768]{2,1,0:T(8,128)(2,1)S(1)}, bf16[4,128,768]{2,1,0:T(8,128)(2,1)S(1)}, bf16[4,1024,128]{2,1,0:T(8,128)(2,1)}) custom-call(s32[1]{0:T(128)} %bitcast.5.own_ref, s32[4,4]{1,0:T(4,128)S(1)} %copy-done.2, bf16[4,64,1536]{2,1,0:T(8,128)(2,1)S(1)} %copy_bitcast_fusion.2.q_ref, ...), custom_call_target="tpu_custom_call" | custom-call | flops 4026531840 | bytes 8388608 | tf_op jit(solution)/shard_map/attention/pallas_call | solution.py:130
  53.6 0.9 copy-done
  54.4 0.9 copy-done.1
  55.3 1.0 copy_bitcast_fusion.1.mt_ref
  56.3 127.3 %tail.1 = (bf16[512,768]{1,0:T(8,128)(2,1)}, bf16[512,768]{1,0:T(8,128)(2,1)}, f32[96,3072]{1,0:T(8,128)}, f32[384,768]{1,0:T(8,128)}, f32[96,768]{1,0:T(8,128)}...) custom-call(bf16[512,768]{1,0:T(8,128)(2,1)} %bitcast.89, bf16[512,768]{1,0:T(8,128)(2,1)} %bitcast.96, ...), custom_call_target="tpu_custom_call" | custom-call | tf_op jit(solution)/shard_map/tail/pallas_call | solution.py:584
  183.6 1.3 slice_bitcast_fusion.7
  184.9 1.3 slice_bitcast_fusion
  186.2 1.4 slice_bitcast_fusion.1
  188.2 2.1 %copy.63 = bf16[4,128,768]{2,1,0:T(8,128)(2,1)} copy(bf16[4,128,768]{2,1,0:T(8,128)(2,1)} %bitcast.99) | data formatting | bytes 1572864
  190.3 0.9 copy.64
  193.3 1.0 copy.68
  194.3 1.0 copy.69
  (103 shorter events, 10.3 us)
Async XLA Ops:
  7.2 7.5 %copy-start.3 = (bf16[4,128,768]{2,1,0:T(8,128)(2,1)S(1)}, bf16[4,128,768]{2,1,0:T(8,128)(2,1)}, u32[]{:S(2)}) copy-start(bf16[4,128,768]{2,1,0:T(8,128)(2,1)} %param.17) | copy-start | bytes 2359300
  7.2 7.5 %copy-start.15 = (f32[768]{0:T(1024)S(1)}, f32[768]{0:T(1024)}, u32[]{:S(2)}) copy-start(f32[768]{0:T(1024)} %param.20) | copy-start | bytes 9220
  7.2 7.5 %copy-start.14 = (f32[768]{0:T(1024)S(1)}, f32[768]{0:T(1024)}, u32[]{:S(2)}) copy-start(f32[768]{0:T(1024)} %param.22) | copy-start | bytes 9220
  7.2 7.5 %copy-start.30 = (f32[768]{0:T(1024)S(1)}, f32[768]{0:T(1024)}, u32[]{:S(2)}) copy-start(f32[768]{0:T(1024)} %param.21) | copy-start | bytes 9220
  7.2 7.5 %copy-start.29 = (f32[768]{0:T(1024)S(1)}, f32[768]{0:T(1024)}, u32[]{:S(2)}) copy-start(f32[768]{0:T(1024)} %param.23) | copy-start | bytes 9220
  7.2 37.9 %all-gather.2.cloned.1.call-start = ((), (), s32[]{:S(2)}) async-start(), calls=%async_computation | async-start | bytes 1179648 | tf_op jit(solution)/shard_map/all_gather | solution.py:637
  8.6 8.1 %copy-start.21 = (s32[4]{0:T(128)}, s32[4]{0:T(128)S(1)}, u32[]{:S(2)}) copy-start(s32[4]{0:T(128)S(1)} %slice_reduce_fusion.1) | copy-start | bytes 52
  11.2 5.4 %copy-start.33 = (s32[128]{0:T(128)}, s32[128]{0:T(128)S(1)}, u32[]{:S(2)}) copy-start(s32[128]{0:T(128)S(1)} %iota_add_fusion) | copy-start | bytes 1540
  12.6 3.6 %copy-start.8 = (bf16[768,128]{1,0:T(8,128)(2,1)S(1)}, bf16[768,128]{1,0:T(8,128)(2,1)}, u32[]{:S(2)}) copy-start(bf16[768,128]{1,0:T(8,128)(2,1)} %wkv_hbm.1) | copy-start | bytes 589828
  12.6 3.6 %copy-start.35 = (f32[128]{0:T(128)S(1)}, f32[128]{0:T(128)}, u32[]{:S(2)}) copy-start(f32[128]{0:T(128)} %param.27) | copy-start | bytes 1540
  16.2 5.3 %copy-start.4 = (bf16[512,768]{1,0:T(8,128)(2,1)}, bf16[512,768]{1,0:T(8,128)(2,1)S(1)}, u32[]{:S(2)}) copy-start(bf16[512,768]{1,0:T(8,128)(2,1)S(1)} %get-tuple-element.43.h1_ref) | copy-start | bytes 2359300
  16.2 4.5 %copy-start.5 = (bf16[768,768]{1,0:T(8,128)(2,1)S(1)}, bf16[768,768]{1,0:T(8,128)(2,1)}, u32[]{:S(2)}) copy-start(bf16[768,768]{1,0:T(8,128)(2,1)} %wo_hbm.1) | copy-start | bytes 3538948
  16.2 4.5 %copy-start.9 = (bf16[4,128,768]{2,1,0:T(8,128)(2,1)S(1)}, bf16[4,128,768]{2,1,0:T(8,128)(2,1)}, u32[]{:S(2)}) copy-start(bf16[4,128,768]{2,1,0:T(8,128)(2,1)} %param.19) | copy-start | bytes 2359300
  26.0 2.8 %copy-start.22 = (s32[4]{0:T(128)S(1)}, s32[4]{0:T(128)}, u32[]{:S(2)}) copy-start(s32[4]{0:T(128)} %copy-done.21) | copy-start | bytes 52
  26.0 2.8 %copy-start.24 = (s32[4]{0:T(128)S(1)}, s32[4]{0:T(128)}, u32[]{:S(2)}) copy-start(s32[4]{0:T(128)} %slice_reduce_fusion.2) | copy-start | bytes 52
  26.0 2.8 %copy-start.26 = (s32[4]{0:T(128)S(1)}, s32[4]{0:T(128)}, u32[]{:S(2)}) copy-start(s32[4]{0:T(128)} %slice_reduce_fusion) | copy-start | bytes 52
  26.1 2.8 %copy-start.28 = (f32[8]{0:T(128)S(1)}, f32[8]{0:T(128)}, u32[]{:S(2)}) copy-start(f32[8]{0:T(128)} %multiply_power_fusion) | copy-start | bytes 100
  30.2 15.0 %copy-start.2 = (s32[4,4]{1,0:T(4,128)S(1)}, s32[4,4]{1,0:T(4,128)}, u32[]{:S(2)}) copy-start(s32[4,4]{1,0:T(4,128)} %len_ref.1) | copy-start | bytes 196
  183.6 6.7 %copy-start.10 = (bf16[512,768]{1,0:T(8,128)(2,1)S(1)}, bf16[512,768]{1,0:T(8,128)(2,1)}, u32[]{:S(2)}) copy-start(bf16[512,768]{1,0:T(8,128)(2,1)} %get-tuple-element.33) | copy-start | bytes 2359300
  187.6 3.6 %copy-start.16 = (f32[768]{0:T(1024)}, f32[768]{0:T(1024)S(1)}, u32[]{:S(2)}) copy-start(f32[768]{0:T(1024)S(1)} %get-tuple-element.120) | copy-start | bytes 9220
  188.2 3.0 %copy-start.12 = (f32[96,768]{1,0:T(8,128)S(1)}, f32[96,768]{1,0:T(8,128)}, u32[]{:S(2)}) copy-start(f32[96,768]{1,0:T(8,128)} %get-tuple-element.115) | copy-start | bytes 884740
  188.2 3.7 %copy-start.13 = (f32[96,128]{1,0:T(8,128)S(1)}, f32[96,128]{1,0:T(8,128)}, u32[]{:S(2)}) copy-start(f32[96,128]{1,0:T(8,128)} %get-tuple-element.117) | copy-start | bytes 147460
  188.2 4.4 %copy-start.11 = (f32[96,768]{1,0:T(8,128)S(1)}, f32[96,768]{1,0:T(8,128)}, u32[]{:S(2)}) copy-start(f32[96,768]{1,0:T(8,128)} %get-tuple-element.119) | copy-start | bytes 884740
  190.3 2.9 %copy-start.7 = (f32[96,3072]{1,0:T(8,128)S(1)}, f32[96,3072]{1,0:T(8,128)}, u32[]{:S(2)}) copy-start(f32[96,3072]{1,0:T(8,128)} %get-tuple-element.121) | copy-start | bytes 3538948
  (14 other events, 23.8 us)
Sparse Core Ops, SparseCore 0:
  18.9 26.1 all-gather.1

commit v3 on v1

v3 whole, which is shorter than its diff:
```python
import functools

import jax
import jax.numpy as jnp
from jax import lax
from jax.experimental import pallas as pl
from jax.experimental.pallas import tpu as pltpu
from jax.sharding import PartitionSpec as P

HD = 64
ROT = 16
BLK = 128
NEG = -1e30
EPS = 1e-05
F32 = jnp.float32
BF = jnp.bfloat16
MESH = pl.DeviceIdType.MESH
CHUNK = 512
QUARTER = 128
LAG = 2
SLOTS = LAG + 1
RING = 3 * LAG + 2


def dot(a, b):
    return jnp.dot(a, b, preferred_element_type=F32)


def dot_nt(a, b):
    return lax.dot_general(a, b, (((1,), (1,)), ((), ())), preferred_element_type=F32)


def dot_tn(a, b):
    return lax.dot_general(a, b, (((0,), (0,)), ((), ())), preferred_element_type=F32)


def lanes_mean(v):
    return jnp.mean(v, axis=-1, keepdims=True)


def column_sum(v):
    return jnp.sum(v, axis=0, keepdims=True)


def doc_start(place, cuts):
    begin = jnp.where(place >= cuts[0], cuts[0], 0)
    for cut in cuts[1:]:
        begin = jnp.where(place >= cut, cut, begin)
    return begin


def rotate(values, cosine, sine):
    front, behind = values[:8], values[8:16]
    return jnp.concatenate([front * cosine - behind * sine, behind * cosine + front * sine, values[16:]], axis=0)


def gelu_parts(up):
    cdf = 0.5 + 0.5 * lax.erf(up * 0.7071067811865476)
    pdf = jnp.exp(-0.5 * up * up) * 0.3989422804014327
    return cdf, up * pdf


def bits_of(value, count):
    return [value // 2**i % 2 for i in range(count)]


def remote(src, dst, send_sem, recv_sem, peer):
    return pltpu.make_async_remote_copy(
        src_ref=src, dst_ref=dst, send_sem=send_sem, recv_sem=recv_sem, device_id=peer, device_id_type=MESH
    )


class Net:
    def __init__(self, seq_bits, row_bits):
        self.a, self.b = seq_bits, row_bits
        self.me, self.row = lax.axis_index("seq"), lax.axis_index("rows")
        self.sb, self.rb = bits_of(self.me, seq_bits), bits_of(self.row, row_bits)

    def seq_xor(self, mask):
        out = self.me
        for i in range(self.a):
            if mask >> i & 1:
                out = out + (1 - 2 * self.sb[i]) * 2**i
        return {"seq": out}

    def row_xor(self, mask):
        out = self.row
        for i in range(self.b):
            if mask >> i & 1:
                out = out + (1 - 2 * self.rb[i]) * 2**i
        return {"rows": out}

    def peers(self):
        return [self.seq_xor(m) for m in range(1, 2**self.a)] + [self.row_xor(m) for m in range(1, 2**self.b)]

    def pick(self, left, bit, mine):
        own = self.sb[bit]
        return tuple((own if mine else 1 - own) if i == bit else slice(None) for i in left)


class Ring:
    def __init__(self, net, early, late, grads, recs, recz, fin, send_sem, recv_sem):
        self.net, self.early, self.late = net, early, late
        self.grads, self.recs, self.recz, self.fin = grads, recs, recz, fin
        self.send_sem, self.recv_sem = send_sem, recv_sem
        a, b = net.a, net.b
        self.halves = min(b, 2)
        self.stages = [("first", 0)] + [("seq", k) for k in range(1, a)]
        self.stages += [("split", i) for i in range(self.halves)]
        self.stages += [("whole", i) for i in range(2, b)]
        self.stages += [("back", i) for i in reversed(range(self.halves))]
        self.sem_at, n = [], 0
        for kind, _ in self.stages:
            self.sem_at.append(n)
            n += 2 if kind == "seq" else 1

    def place(self, ch):
        if isinstance(ch, int) and ch in self.late:
            return self.early + self.late.index(ch)
        return ch

    def slot(self, ch):
        if isinstance(ch, int) and ch in self.late:
            return RING + self.late.index(ch)
        return ch % RING

    def moves(self, stage, ch):
        net, a = self.net, self.net.a
        kind, k = self.stages[stage]
        at = (self.slot(ch),)
        if kind == "first":
            left = range(a - 1, -1, -1)
            slot = (ch % SLOTS,)
            return [(self.grads.at[slot + net.pick(left, 0, False)], self.recs[0].at[at], net.seq_xor(1),
                     (self.grads, slot + net.pick(left, 0, True)), (self.recs[0], at))]
        if kind == "seq":
            out = []
            prev, here = self.recs[k - 1], self.recs[k]
            for half in (0, 1):
                if half == 0:
                    bit, left = k, range(a - 1, k - 1, -1)
                else:
                    bit, left = a - k, range(a - k, 0, -1)
                base, tail = (at, (half,)) if k == 1 else (at + (half,), ())
                out.append((prev.at[base + net.pick(left, bit, False) + tail], here.at[at + (half,)],
                            net.seq_xor(1 << bit), (prev, base + net.pick(left, bit, True) + tail), (here, at + (half,))))
            return out
        if kind == "split":
            prev = self.recs[a - 1] if k == 0 else self.recz[k - 1]
            return [(prev.at[at + (1 - net.rb[k],)], self.recz[k].at[at], net.row_xor(1 << k),
                     (prev, at + (net.rb[k],)), (self.recz[k], at))]
        if kind == "whole":
            prev = self.recz[k - 1]
            return [(prev.at[at], self.recz[k].at[at], net.row_xor(1 << k), (prev, at), (self.recz[k], at))]
        at = (self.place(ch),) + tuple(net.rb[: k + 1])
        return [(self.fin.at[at], self.fin.at[at], net.row_xor(1 << k), None, None)]

    def copies(self, stage, ch):
        out = []
        at = self.place(ch)
        for i, (src, dst, peer, _, _) in enumerate(self.moves(stage, ch)):
            sem = self.sem_at[stage] + i
            out.append(remote(src, dst, self.send_sem.at[at, sem], self.recv_sem.at[at, sem], peer))
        return out

    def start(self, stage, ch):
        for copy in self.copies(stage, ch):
            copy.start()

    def finish(self, stage, ch):
        for copy in self.copies(stage, ch):
            copy.wait()
        kind, _ = self.stages[stage]
        if kind != "back":
            last = self.stages[stage + 1][0] == "back"
            for _, _, _, (src, src_at), (dst, dst_at) in self.moves(stage, ch):
                total = src[src_at] + dst[dst_at]
                if last:
                    self.fin[(self.place(ch),) + tuple(self.net.rb[: self.halves])] = total
                else:
                    dst[dst_at] = total
        if stage + 1 < len(self.stages):
            self.start(stage + 1, ch)

    def tick(self, t):
        for stage in reversed(range(len(self.stages))):
            ch = t - LAG * (stage + 1)
            if isinstance(ch, int):
                if 0 <= ch < self.early or ch in self.late:
                    self.finish(stage, ch)
            else:

                @pl.when((ch >= 0) & (ch < self.early))
                def _():
                    self.finish(stage, ch)

    def last_tick(self):
        return max(self.late) + LAG * len(self.stages)


def layer_kernel(
    seq_bits, row_bits, late,
    len_ref, x_ref, dy_ref, fg_ref, fs_ref, sg_ref, ss_ref, bq_ref, bo_ref, bd_ref, bkv_ref, bu_ref, wq_hbm, wkv_hbm, wo_hbm, wu_hbm, wd_hbm,
    lo_ref, ig_ref, fin, small_ref,
    wq, wkv, wo, wu, wd, load_sem, vec_ref, wide_ref,
    h1, h2, act, act_t, dup, gub, q_all, do_all, cs, kv_all, kv_send, kv_recv,
    s_ref, e_ref, qz, dz, m_ref, l_ref, o_ref, dqa, mt, mx, dq, dkv, dkv_in, dkv_sum, dkv_send, dkv_recv,
    grads, *rest,
):
    a, n, count = seq_bits, 2**seq_bits, 2**row_bits
    recs, rest = rest[:a], rest[a:]
    recz, rest = rest[:row_bits], rest[row_bits:]
    send_sem, recv_sem, own_small, seq_small, row_small, m_send, m_recv = rest
    toks, width = x_ref.shape
    hidden = wu.shape[1]
    sub = width // n
    heads = width // HD
    lanes = s_ref.shape[-1]
    groups = heads * BLK // lanes
    near = lanes // BLK
    rows = toks // BLK
    n_up, n_down = hidden // CHUNK, width // QUARTER
    net = Net(seq_bits, row_bits)
    me = net.me
    ring = Ring(net, n_up + n_down, late, grads, recs, recz, fin, send_sem, recv_sem)

    barrier = pltpu.get_barrier_semaphore()
    for peer in net.peers():
        pl.semaphore_signal(barrier, inc=1, device_id=peer, device_id_type=MESH)
    loads = {}
    for i, (name, src, dst) in enumerate(
        (("kv", wkv_hbm, wkv), ("q", wq_hbm, wq), ("o", wo_hbm, wo), ("u", wu_hbm, wu), ("d", wd_hbm, wd))
    ):
        loads[name] = pltpu.make_async_copy(src, dst, load_sem.at[i])
        loads[name].start()

    for i, ref in enumerate((fg_ref, fs_ref, sg_ref, ss_ref, bq_ref)):
        vec_ref[i : i + 1, :] = ref[...].reshape(1, width)
    vec_ref[5:6, :] = (bo_ref[...] + bd_ref[...]).reshape(1, width)
    wide_ref[...] = bu_ref[...].reshape(1, hidden)

    def put_chunk(ch, owner, value, quarters):
        at = (ch % SLOTS,) + tuple(reversed(bits_of(owner, a)))
        for i, q in enumerate(quarters):
            grads[at + (q // 2, q % 2)] = value[:, i * QUARTER : (i + 1) * QUARTER].astype(BF)

    def part(owner):
        return slice(owner * sub, (owner + 1) * sub)

    def row_cuts(r):
        cuts = []
        for i in range(len_ref.shape[1] - 1):
            cuts.append(len_ref[r, i] + (cuts[-1] if cuts else 0))
        return cuts

    place = me * BLK + lax.broadcasted_iota(jnp.int32, (8, BLK), 1)
    which = lax.broadcasted_iota(jnp.int32, (8, BLK), 0)
    freqs = jnp.ones((8, BLK), F32)
    for i in range(1, 8):
        freqs = jnp.where(which == i, 10000.0 ** (-2.0 * i / ROT), freqs)
    for r in range(rows):
        angles = (place - doc_start(place, row_cuts(r))).astype(F32) * freqs
        cs[r, 0] = jnp.cos(angles)
        cs[r, 1] = jnp.sin(angles)

    def row_span(r):
        return pl.ds(pl.multiple_of(r * BLK, BLK), BLK)

    def normalized(r):
        x = x_ref[row_span(r), :].astype(F32)
        centred = x - lanes_mean(x)
        factor = lax.rsqrt(lanes_mean(centred * centred) + EPS)
        return x, centred * factor, factor

    def norms(r, _):
        xhat = normalized(r)[1]
        h1[row_span(r), :] = (xhat * vec_ref[0:1, :] + vec_ref[1:2, :]).astype(BF)
        h2[row_span(r), :] = (xhat * vec_ref[2:3, :] + vec_ref[3:4, :]).astype(BF)
        return 0

    lax.fori_loop(0, rows, norms, 0)

    per_block = lanes // width

    def spare(k, r, cols=None):
        cols = slice(0, width) if cols is None else cols
        at = k % per_block * width
        return k // per_block * rows + r, slice(None), slice(at + cols.start, at + cols.stop)

    def by_rows(k, value):
        for r in range(rows):
            s_ref[spare(k, r)] = value[r * BLK : (r + 1) * BLK]

    loads["kv"].wait()
    kv = dot(h1[...], wkv[...]) + bkv_ref[...].reshape(1, 2 * HD)
    group = rows // 2

    def at_bits(value):
        return tuple(reversed(bits_of(value, a)))

    def kv_at(j, r):
        return at_bits(j) + (r // group, r % group)

    for r in range(rows):
        turned = rotate(kv[r * BLK : (r + 1) * BLK].T, cs[r, 0], cs[r, 1])
        kv_all[kv_at(me, r)] = turned.T.astype(BF)
    pl.semaphore_wait(barrier, n + count - 2)

    def kv_copies(k):
        out = []
        for half in (0, 1):
            order = list(range(1, a)) if half == 0 else list(range(a - 1, 0, -1))
            order.append(0)
            at = tuple(slice(None) if i in order[:k] else net.sb[i] for i in reversed(range(a))) + (half,)
            sem = 2 * k + half
            out.append(remote(kv_all.at[at], kv_all.at[at], kv_send.at[sem], kv_recv.at[sem], net.seq_xor(1 << order[k])))
        return out

    def kv_step(k):
        if k > 0:
            for copy in kv_copies(k - 1):
                copy.wait()
        if k < a:
            for copy in kv_copies(k):
                copy.start()

    kv_step(0)

    loads["q"].wait()
    by_rows(0, dot(h1[...], wq[...]) + vec_ref[4:5, :])
    loads["o"].wait()
    by_rows(1, dot_nt(dy_ref[...], wo[...]))
    kv_step(1)

    def heads_apart(r, _):
        for h in range(0, heads, 2):
            pair = s_ref[spare(0, r, slice(h * HD, (h + 2) * HD))].T
            d_pair = s_ref[spare(1, r, slice(h * HD, (h + 2) * HD))].T.astype(BF)
            for i in (0, 1):
                span = slice((h + i) * BLK, (h + i + 1) * BLK)
                turned = rotate(pair[i * HD : (i + 1) * HD], cs[r, 0], cs[r, 1]).astype(BF).astype(F32)
                q_all[r, :, span] = (turned * 0.125).astype(BF)
                do_all[r, :, span] = d_pair[i * HD : (i + 1) * HD]
        return 0

    lax.fori_loop(0, rows, heads_apart, 0)
    kv_step(2)
    loads["u"].wait()
    loads["d"].wait()

    def feed(f):
        cols = pl.ds(pl.multiple_of(f * CHUNK, CHUNK), CHUNK)
        up = dot(h2[...], wu[:, cols]) + wide_ref[:, cols]
        d_act = dot_nt(dy_ref[...], wd[cols, :])
        cdf, slope = gelu_parts(up)
        low = (up * cdf).astype(BF)
        d_up = (d_act * (cdf + slope)).astype(BF)
        act[:, cols] = low
        act_t[cols, :] = low.T
        dup[:, cols] = d_up
        gub[:, cols] = column_sum(d_up.astype(F32))
        g = dot_tn(h2[...], d_up)
        for owner in range(n):
            put_chunk(f, owner, g[part(owner)], range(4))

    def down(j):
        cols = dy_ref[:, pl.ds(pl.multiple_of(j * QUARTER, QUARTER), QUARTER)]
        for owner in range(n):
            g = dot(act_t[owner * 4 * sub : (owner + 1) * 4 * sub, :], cols).astype(BF)
            at = ((n_up + j) % SLOTS,) + at_bits(owner)
            for i in range(4):
                grads[at + (i // 2, i % 2)] = g[i * sub : (i + 1) * sub]

    n_pre = n_up + n_down - 3 * (rows - 1)

    def feed_step(t, _):
        feed(t)
        ring.start(0, t)
        ring.tick(t)
        return 0

    lax.fori_loop(0, n_pre, feed_step, 0)
    for k in range(3, a + 1):
        kv_step(k)

    key_iota = lax.broadcasted_iota(jnp.int32, (BLK, BLK), 0)
    query_place = me * BLK + lax.broadcasted_iota(jnp.int32, (BLK, BLK), 1)

    def scores_pass(r, g):
        span = slice(g * lanes, (g + 1) * lanes)
        qz[:HD, :] = q_all[r, :, span]
        qz[HD:, :] = jnp.zeros((HD, lanes), BF)
        dz[HD:, :] = do_all[r, :, span]
        dz[:HD, :] = jnp.zeros((HD, lanes), BF)
        m_ref[...] = jnp.full(m_ref.shape, NEG, F32)
        l_ref[...] = jnp.zeros(l_ref.shape, F32)
        o_ref[...] = jnp.zeros(o_ref.shape, F32)
        dqa[...] = jnp.zeros(dqa.shape, F32)
        begin = doc_start(query_place, row_cuts(r))

        def body(j, _):
            keys = j * BLK + key_iota
            bias = jnp.where((keys <= query_place) & (keys >= begin), 0.0, NEG)
            s = dot(kv_all[kv_at(j, r)], qz[...]) + jnp.concatenate([bias] * near, axis=1)
            s_ref[j] = s
            m_ref[...] = jnp.maximum(m_ref[...], jnp.max(s.reshape(BLK // 8, 8, lanes), axis=0))
            return 0

        lax.fori_loop(0, me + 1, body, 0)
        m_ref[0:1, :] = jnp.max(m_ref[...], axis=0, keepdims=True)

    def mix_pass(r, g):
        def body(j, _):
            v_t = kv_all[kv_at(j, r)].T[HD:]
            e = jnp.exp(s_ref[j] - m_ref[0:1, :])
            l_ref[...] += jnp.sum(e.reshape(BLK // 8, 8, lanes), axis=0)
            e_low = e.astype(BF)
            e_ref[j] = e_low
            o_ref[...] += dot(v_t, e_low)
            return 0

        lax.fori_loop(0, me + 1, body, 0)
        inv = 1.0 / jnp.sum(l_ref[...], axis=0, keepdims=True)
        o = o_ref[...] * inv
        l_ref[0:1, :] = inv
        m_ref[0:1, :] = jnp.sum(o * dz[HD:, :].astype(F32), axis=0, keepdims=True)
        span = row_span(r)
        for h in range(0, near, 2):
            pair = jnp.concatenate(
                [o[:, h * BLK : (h + 1) * BLK], o[:, (h + 1) * BLK : (h + 2) * BLK]], axis=0
            )
            at = slice((g * near + h) * HD, (g * near + h + 2) * HD)
            mt[at, span] = pair.astype(BF)
            mx[span, at] = pair.T.astype(BF)

    def back_pass(r, g, start, stop):
        def body(j, _):
            kv = kv_all[kv_at(j, r)]
            k_t = kv.T[:HD]
            dp = dot(kv, dz[...])
            p = e_ref[j].astype(F32) * l_ref[0:1, :]
            ds = (p * (dp - m_ref[0:1, :])).astype(BF)
            total = dot_nt(ds, qz[...]) + dot_nt(p.astype(BF), dz[...])
            if g > 0:
                total = total + dkv[j, r].astype(F32)
            dkv[j, r] = total.astype(BF)
            dqa[...] += dot(k_t, ds)
            return 0

        lax.fori_loop(start, stop, body, 0)

    def dkv_copies(r):
        out = []
        for m in range(1, n):
            peer = net.seq_xor(m)
            out.append((peer["seq"], remote(
                dkv.at[peer["seq"], r], dkv_in.at[m - 1, r], dkv_send.at[m - 1, r], dkv_recv.at[m - 1, r], peer)))
        return out

    def leave_pass(r, g):
        if g == groups - 1:
            for other, copy in dkv_copies(r):

                @pl.when(other < me)
                def _():
                    copy.start()

        cosine, sine = cs[r, 0], cs[r, 1]
        span = row_span(r)
        for h in range(0, near, 2):
            pair = jnp.concatenate(
                [rotate(dqa[:, i * BLK : (i + 1) * BLK], cosine, -sine) for i in (h, h + 1)], axis=0
            )
            dq[span, (g * near + h) * HD : (g * near + h + 2) * HD] = (pair * 0.125).T.astype(BF)

    def first_groups(r):
        for g in range(groups - 1):
            scores_pass(r, g)
            mix_pass(r, g)
            back_pass(r, g, 0, me + 1)
            leave_pass(r, g)

    def chunk_step(t):
        @pl.when(t < n_up)
        def _():
            feed(t)

        @pl.when(t >= n_up)
        def _():
            down(t - n_up)

        ring.start(0, t)
        ring.tick(t)

    def row_step(r, _):
        t = n_pre + 3 * r
        first_groups(r)
        scores_pass(r, groups - 1)
        chunk_step(t)
        mix_pass(r, groups - 1)
        chunk_step(t + 1)
        back_pass(r, groups - 1, 0, me + 1)
        leave_pass(r, groups - 1)
        chunk_step(t + 2)
        return 0

    lax.fori_loop(0, rows - 1, row_step, 0)
    r, t = rows - 1, n_up + n_down
    first_groups(r)
    scores_pass(r, groups - 1)
    ring.tick(t)
    mix_pass(r, groups - 1)
    g = dot(mt[...], dy_ref[:, :CHUNK])
    for owner in range(n):
        put_chunk(late[0], owner, g[part(owner)], range(4))
    ring.start(0, late[0])
    ring.tick(late[0])
    g = dot(mt[...], dy_ref[:, CHUNK:])
    for owner in range(n):
        put_chunk(late[1], owner, g[part(owner)], range(2))
    ring.start(0, late[1])
    ring.tick(late[1])
    back_pass(r, groups - 1, 0, (me + 1) // 2)
    ring.tick(late[1] + 1)
    back_pass(r, groups - 1, (me + 1) // 2, me + 1)
    leave_pass(r, groups - 1)
    ring.tick(late[1] + 2)
    g = dot_tn(h1[...], dq[:, :CHUNK])
    for owner in range(n):
        put_chunk(late[2], owner, g[part(owner)], range(4))
    ring.start(0, late[2])
    ring.tick(late[2])
    g = dot_tn(h1[...], dq[:, CHUNK:])
    for owner in range(n):
        put_chunk(late[3], owner, g[part(owner)], range(2))
    by_rows(0, dot_nt(dup[...], wu[...]))

    dkv_sum[...] = dkv[me].astype(F32)
    for r in range(rows):
        for m, (other, copy) in enumerate(dkv_copies(r)):

            @pl.when(other < me)
            def _():
                copy.wait_send()

            @pl.when(other > me)
            def _():
                copy.wait_recv()
                dkv_sum[r] += dkv_in[m, r].astype(F32)

    d_kv = jnp.concatenate(
        [rotate(dkv_sum[r].T, cs[r, 0], -cs[r, 1]).T.astype(BF) for r in range(rows)], axis=0
    )
    g = dot_tn(h1[...], d_kv)
    for owner in range(n):
        put_chunk(late[3], owner, g[part(owner)], (2,))
        put_chunk(late[3], owner, jnp.zeros((sub, QUARTER), F32), (3,))
    ring.start(0, late[3])
    ring.tick(late[3])

    by_rows(1, dot_nt(dq[...], wq[...]) + dot_nt(d_kv, wkv[...]))
    own_small[...] = jnp.zeros(own_small.shape, F32)
    per = width // 128

    def add_small(at, vector):
        for i in range(vector.shape[1] // 128):
            own_small[at + i : at + i + 1, :] += vector[:, i * 128 : (i + 1) * 128]

    def norms_back(r, _):
        _, xhat, factor = normalized(r)
        dy32 = dy_ref[row_span(r), :].astype(F32)
        result = dy32
        for k, gain in enumerate((vec_ref[0:1, :], vec_ref[2:3, :])):
            grad = s_ref[spare(1 - k, r)]
            add_small(2 * k * per, column_sum(grad * xhat))
            add_small((2 * k + 1) * per, column_sum(grad))
            g = grad * gain
            result = result + factor * (g - lanes_mean(g) - xhat * lanes_mean(g * xhat))
        h2[row_span(r), :] = result.astype(BF)
        add_small(4 * per, column_sum(dq[row_span(r), :].astype(F32)))
        add_small(5 * per + 1, column_sum(dy32))
        return 0

    lax.fori_loop(0, rows, norms_back, 0)
    ig_copy = pltpu.make_async_copy(h2, ig_ref, load_sem.at[5])
    ig_copy.start()
    add_small(5 * per, column_sum(d_kv.astype(F32)))
    add_small(6 * per + 1, gub[...])

    def narrow(step):
        if step == 0:
            return [
                remote(own_small, seq_small.at[me], m_send.at[m - 1], m_recv.at[m - 1], net.seq_xor(m)) for m in range(1, n)
            ]
        spot = row_small.at[net.row]
        return [
            remote(spot, spot, m_send.at[n + m - 2], m_recv.at[n + m - 2], net.row_xor(m)) for m in range(1, count)
        ]

    for copy in narrow(0):
        copy.start()
    ring.tick(late[3] + 1)
    by_rows(2, dot(act[...], wd[...]) + vec_ref[5:6, :])
    ring.tick(late[3] + 2)
    for copy in narrow(0):
        copy.wait()
    seq_small[me] = own_small[...]
    sums = seq_small[0]
    for i in range(1, n):
        sums = sums + seq_small[i]
    row_small[net.row] = sums
    for copy in narrow(1):
        copy.start()
    ring.tick(late[3] + 3)
    by_rows(3, dot(mx[...], wo[...]))

    def layer_out(r, _):
        total = x_ref[row_span(r), :].astype(F32) + s_ref[spare(2, r)] + s_ref[spare(3, r)]
        h1[row_span(r), :] = total.astype(BF)
        return 0

    lax.fori_loop(0, rows, layer_out, 0)
    lo_copy = pltpu.make_async_copy(h1, lo_ref, load_sem.at[6])
    lo_copy.start()
    for t in range(late[3] + 4, ring.last_tick() + 1):
        ring.tick(t)
    for copy in narrow(1):
        copy.wait()
    sums = row_small[0]
    for i in range(1, count):
        sums = sums + row_small[i]
    small_ref[...] = sums
    ig_copy.wait()
    lo_copy.wait()


def layer(net_bits, lengths, x, dy, vectors, wq, wkv, wo, wu, wd):
    a, b = net_bits
    n, count = 2**a, 2**b
    toks, width = x.shape
    hidden = wu.shape[1]
    sub = width // n
    rows = toks // BLK
    all_lanes = width // HD * BLK
    lanes = all_lanes // max(1, n // 8)
    n_up, n_down = hidden // CHUNK, width // QUARTER
    last_row = n_up + n_down
    late = [last_row + 1, last_row + 2, last_row + 5, last_row + 6]
    total = n_up + n_down + len(late)
    slots = RING + len(late)
    two = (2,)
    vm = pltpu.VMEM
    dma = pltpu.SemaphoreType.DMA
    n_sems = 1 + 2 * (a - 1) + b + min(b, 2)
    scratch = [
        vm(wq.shape, BF), vm(wkv.shape, BF), vm(wo.shape, BF), vm(wu.shape, BF), vm(wd.shape, BF), dma((7,)),
        vm((8, width), F32), vm((1, hidden), F32),
        vm((toks, width), BF), vm((toks, width), BF),
        vm((toks, hidden), BF), vm((hidden, toks), BF), vm((toks, hidden), BF), vm((1, hidden), F32),
        vm((rows, HD, all_lanes), BF), vm((rows, HD, all_lanes), BF), vm((rows, 2, 8, BLK), F32),
        vm(two * a + (2, rows // 2, BLK, 2 * HD), BF), dma((2 * a,)), dma((2 * a,)),
        vm((n, BLK, lanes), F32), vm((n, BLK, lanes), BF), vm((2 * HD, lanes), BF), vm((2 * HD, lanes), BF),
        vm((8, lanes), F32), vm((8, lanes), F32), vm((HD, lanes), F32), vm((HD, lanes), F32),
        vm((width, toks), BF), vm((toks, width), BF), vm((toks, width), BF),
        vm((n, rows, BLK, 2 * HD), BF), vm((n - 1, rows, BLK, 2 * HD), BF), vm((rows, BLK, 2 * HD), F32),
        dma((n - 1, rows)), dma((n - 1, rows)),
        vm((SLOTS,) + two * a + (2, 2, sub, 128), BF),
        vm((slots,) + two * (a - 1) + (2, 2, sub, 128), BF),
    ]
    scratch += [vm((slots, 2) + two * (a - 1 - k) + (2, sub, 128), BF) for k in range(1, a)]
    scratch += [vm((slots, 2, sub, 128), BF)] + [vm((slots, sub, 128), BF) for _ in range(1, b)]
    scratch += [
        dma((total, n_sems)), dma((total, n_sems)),
        vm((64, 128), F32), vm((n, 64, 128), F32), vm((count, 64, 128), F32),
        dma((n + count,)), dma((n + count,)),
    ]
    vmem = pl.BlockSpec(memory_space=pltpu.VMEM)
    hbm = pl.BlockSpec(memory_space=pl.ANY)
    shape = jax.ShapeDtypeStruct
    return pl.pallas_call(
        functools.partial(layer_kernel, a, b, late),
        out_shape=[
            shape((toks, width), BF), shape((toks, width), BF),
            shape((total, 2, 2, sub, 128), BF), shape((64, 128), F32),
        ],
        in_specs=[pl.BlockSpec(memory_space=pltpu.SMEM)] + [vmem] * (2 + len(vectors)) + [hbm] * 5,
        out_specs=[hbm, hbm, vmem, vmem],
        scratch_shapes=scratch,
        compiler_params=pltpu.CompilerParams(collective_id=0, has_side_effects=True, vmem_limit_bytes=64 * 2**20),
        name="layer",
    )(lengths, x, dy, *vectors, wq, wkv, wo, wu, wd)


def finish_kernel(n_up, sizes, lo_in, ig_in, fin_in, small_in, lo, ig, gup, gdown, gout, gq, gkv, *rest):
    vectors, (fin, small, vlo, vig, vup, vdown, vout, vq, vkv, sem) = rest[: len(sizes)], rest[len(sizes) :]
    sub, width = gout.shape
    n_down = width // QUARTER
    late = n_up + n_down

    def move(i, src, dst):
        copy = pltpu.make_async_copy(src, dst, sem.at[i])
        copy.start()
        return copy

    loads = [move(0, fin_in, fin), move(1, small_in, small)]
    loads += [move(2, lo_in, vlo), move(3, ig_in, vig)]
    for load in loads:
        load.wait()
    moves = [move(9, vlo, lo), move(10, vig, ig)]

    def piece(ch, q):
        return fin[ch, q // 2, q % 2].astype(F32)

    def span(at, q):
        return slice(at + q * QUARTER, at + (q + 1) * QUARTER)

    for q in range(4):
        for f in range(n_up):
            vup[:, span(f * CHUNK, q)] = piece(f, q)
    moves.append(move(4, vup, gup))
    for q in range(4):
        for j in range(n_down):
            vdown[q * sub : (q + 1) * sub, j * QUARTER : (j + 1) * QUARTER] = piece(n_up + j, q)
    moves.append(move(5, vdown, gdown))
    for q in range(4):
        vout[:, span(0, q)] = piece(late, q)
        vq[:, span(0, q)] = piece(late + 2, q)
        if q < 2:
            vout[:, span(CHUNK, q)] = piece(late + 1, q)
            vq[:, span(CHUNK, q)] = piece(late + 3, q)
    vkv[...] = piece(late + 3, 2)
    moves += [move(6, vout, gout), move(7, vq, gq), move(8, vkv, gkv)]
    at = 0
    for size, ref in zip(sizes[:-1], vectors):
        for i in range(size // 128):
            ref[i * 128 : (i + 1) * 128] = small[at + i, :]
        at += size // 128
    vectors[-1][...] = vectors[-3][...]
    for copy in moves:
        copy.wait()


def finish(lo, ig, fin, small, sub, width, hidden):
    sizes = [width] * 5 + [2 * HD, width, hidden, width]
    shape = jax.ShapeDtypeStruct
    hbm = pl.BlockSpec(memory_space=pl.ANY)
    grads = [(sub, hidden), (4 * sub, width), (sub, width), (sub, width), (sub, 2 * HD)]
    return pl.pallas_call(
        functools.partial(finish_kernel, hidden // CHUNK, sizes),
        out_shape=[shape(lo.shape, BF), shape(ig.shape, BF)]
        + [shape(g, F32) for g in grads] + [shape((size,), F32) for size in sizes],
        in_specs=[hbm] * 4,
        out_specs=[hbm] * 7 + [pl.BlockSpec(memory_space=pltpu.VMEM)] * len(sizes),
        scratch_shapes=[pltpu.VMEM(fin.shape, BF), pltpu.VMEM(small.shape, F32), pltpu.VMEM(lo.shape, BF), pltpu.VMEM(ig.shape, BF)]
        + [pltpu.VMEM(g, F32) for g in grads] + [pltpu.SemaphoreType.DMA((11,))],
        compiler_params=pltpu.CompilerParams(vmem_limit_bytes=64 * 2**20),
        name="finish",
    )(lo, ig, fin, small)


def shards(
    hidden, lengths, cotangent, first_gain, first_shift, second_gain, second_shift,
    query_weight, query_bias, keyvalue_weight, keyvalue_bias, output_weight, output_bias,
    up_weight, up_bias, down_weight, down_bias,
):
    rows, block, width = hidden.shape
    toks = rows * block
    n, count = lax.axis_size("seq"), lax.axis_size("rows")
    vectors = (
        first_gain, first_shift, second_gain, second_shift, query_bias, output_bias, down_bias, keyvalue_bias, up_bias,
    )
    lo, ig, fin, small = layer(
        (n.bit_length() - 1, count.bit_length() - 1), lengths,
        hidden.reshape(toks, width), cotangent.reshape(toks, width), vectors,
        query_weight, keyvalue_weight, output_weight, up_weight, down_weight,
    )
    lo, ig, g_up, g_down, g_out, g_q, g_kv, *sums = finish(lo, ig, fin, small, width // n, width, up_weight.shape[1])
    s_fg, s_fs, s_sg, s_ss, s_qb, s_kb, s_ob, s_ub, s_db = sums
    return (
        lo.reshape(hidden.shape), ig.reshape(hidden.shape),
        s_fg, s_fs, s_sg, s_ss, g_q, s_qb, g_kv, s_kb, g_out, s_ob, g_up, s_ub, g_down, s_db,
    )


def solution(mesh):
    tokens = P("rows", "seq", None)
    weight = P("seq", None)
    return jax.shard_map(
        shards,
        mesh=mesh,
        in_specs=(tokens, P("rows", None), tokens) + (P(),) * 14,
        out_specs=(
            tokens, tokens, P(), P(), P(), P(), weight, P(), weight, P(), weight, P(), weight, P(), weight, P(),
        ),
        check_vma=False,
    )
```

time: 336 us -> 126 us (0.38)
  waiting for transfers between devices: 143 us -> 0 us
  Pallas kernels: 27.8 us -> 125 us
  local copies, waits for them, and re-layouts: 58.5 us -> 0 us
  blocking collectives: 42.4 us -> 0 us
  other arithmetic: 27.9 us -> 0 us
  matrix products: 18.4 us -> 0 us
  between operations: 14.4 us -> 0.84 us
    reduce_scatter x3 -> x0, waiting for transfers between devices: 109 us -> none  [the longest x2 67.1 us: summed(): part = lax.psum_scatter(joined, 'seq', scatter_dimension=0, tiled=True)[0]]
    pallas_call x2, Pallas kernels: 27.8 us -> 125 us  [the longest x1 120 us: layer(): pl.pallas_call(functools.partial(layer_kernel, a, b, late), out_shape=[sh...]
    psum x1 -> x0, blocking collectives: 42.4 us -> none  [shards(): lax.psum(jnp.concatenate([jnp.sum(first_grad * xhat, axis=0), jnp.sum(fir...]
    reshape x12 -> x0, local copies, waits for them, and re-layouts: 34.5 us -> none  [the longest x5 25 us: by_owner(): return g.astype(BF).reshape(seq_size, -1, 512)]
    psum x1 -> x0, waiting for transfers between devices: 23.3 us -> none  [summed(): return lax.psum(part, 'rows').astype(F32)]
    dot_general x9 -> x0, matrix products: 18.4 us -> none  [the longest x2 4.55 us: dot_tn(): lax.dot_general(a, b, (((0,), (0,)), ((), ())), preferred_element_type=F32)]
    unnamed x102 -> x0, local copies, waits for them, and re-layouts: 12 us -> none
    concatenate x3 -> x0, other arithmetic: 11.7 us -> none  [the longest x2 10.9 us: summed(): joined = jnp.concatenate([by_owner(g) for g in parts], axis=1)]
  transfers between devices with their start and end apart: 5 -> 0, of which waited for: 4 -> 0; matrix products, arithmetic and copies ran while one was open for 20% -> 0% of each run, Pallas kernels for 6% -> 0%
where the time goes in v3:
time: 126 us; the launch traced here: 125 us
  Pallas kernels  125 us (99%)
    pallas_call x1, Pallas kernels, layer(): pl.pallas_call(functools.partial(layer_kernel, a, b, late), out_shape=[sh...  120 us
    pallas_call x1, Pallas kernels, finish(): pl.pallas_call(functools.partial(finish_kernel, hidden // CHUNK, sizes),...  4.68 us

profile of v3, /device:TPU:0, one launch (start us, length us, event | category | flops | bytes accessed | tf_op | source)
XLA Modules:
  0.0 125.4 jit_solution(5586138948807732878)
XLA Ops:
  0.7 119.9 %layer.1 = (bf16[512,768]{1,0:T(8,128)(2,1)}, bf16[512,768]{1,0:T(8,128)(2,1)}, bf16[16,2,2,96,128]{4,3,2,1,0:T(8,128)(2,1)}, f32[64,128]{1,0:T(8,128)}) custom-call(s32[4,4]{1,0:T(4,128)} %len_ref.1, bf16[512,768]{1,0:T(8,128)(2,1)} %bitcast.4, bf16[512,768]{1,0:T(8,128)(2,1)} %bitcast.5, f32[768]{0:T(1024)} %fg_ref.1, f32[768]{0:T(1024)} %fs_ref.1, ...), custom_call_target="tpu_custom_call" | custom-call | tf_op jit(solution)/shard_map/layer/pallas_call | solution.py:680
  120.5 4.7 %finish.1 = (bf16[512,768]{1,0:T(8,128)(2,1)}, bf16[512,768]{1,0:T(8,128)(2,1)}, f32[96,3072]{1,0:T(8,128)}, f32[384,768]{1,0:T(8,128)}, f32[96,768]{1,0:T(8,128...) custom-call(bf16[512,768]{1,0:T(8,128)(2,1)} %get-tuple-element.36.l, ...), custom_call_target="tpu_custom_call" | custom-call | tf_op jit(solution)/shard_map/finish/pallas_call | solution.py:748

commit v4 on v3

--- a/solution.py
+++ b/solution.py
@@ -8,6 +8,7 @@
 from jax.sharding import PartitionSpec as P
 
 HD = 64
+PAIR = 4
 ROT = 16
 BLK = 128
 NEG = -1e30
@@ -99,8 +100,8 @@
 
 
 class Ring:
-    def __init__(self, net, early, late, grads, recs, recz, fin, send_sem, recv_sem):
-        self.net, self.early, self.late = net, early, late
+    def __init__(self, net, early, grads, recs, recz, fin, send_sem, recv_sem):
+        self.net, self.early = net, early
         self.grads, self.recs, self.recz, self.fin = grads, recs, recz, fin
         self.send_sem, self.recv_sem = send_sem, recv_sem
         a, b = net.a, net.b
@@ -114,20 +115,10 @@
             self.sem_at.append(n)
             n += 2 if kind == "seq" else 1
 
-    def place(self, ch):
-        if isinstance(ch, int) and ch in self.late:
-            return self.early + self.late.index(ch)
-        return ch
-
-    def slot(self, ch):
-        if isinstance(ch, int) and ch in self.late:
-            return RING + self.late.index(ch)
-        return ch % RING
-
     def moves(self, stage, ch):
         net, a = self.net, self.net.a
         kind, k = self.stages[stage]
-        at = (self.slot(ch),)
+        at = (ch % RING,)
         if kind == "first":
             left = range(a - 1, -1, -1)
             slot = (ch % SLOTS,)
@@ -152,15 +143,14 @@
         if kind == "whole":
             prev = self.recz[k - 1]
             return [(prev.at[at], self.recz[k].at[at], net.row_xor(1 << k), (prev, at), (self.recz[k], at))]
-        at = (self.place(ch),) + tuple(net.rb[: k + 1])
+        at = (ch,) + tuple(net.rb[: k + 1])
         return [(self.fin.at[at], self.fin.at[at], net.row_xor(1 << k), None, None)]
 
     def copies(self, stage, ch):
         out = []
-        at = self.place(ch)
         for i, (src, dst, peer, _, _) in enumerate(self.moves(stage, ch)):
             sem = self.sem_at[stage] + i
-            out.append(remote(src, dst, self.send_sem.at[at, sem], self.recv_sem.at[at, sem], peer))
+            out.append(remote(src, dst, self.send_sem.at[ch, sem], self.recv_sem.at[ch, sem], peer))
         return out
 
     def start(self, stage, ch):
@@ -176,7 +166,7 @@
             for _, _, _, (src, src_at), (dst, dst_at) in self.moves(stage, ch):
                 total = src[src_at] + dst[dst_at]
                 if last:
-                    self.fin[(self.place(ch),) + tuple(self.net.rb[: self.halves])] = total
+                    self.fin[(ch,) + tuple(self.net.rb[: self.halves])] = total
                 else:
                     dst[dst_at] = total
         if stage + 1 < len(self.stages):
@@ -186,7 +176,7 @@
         for stage in reversed(range(len(self.stages))):
             ch = t - LAG * (stage + 1)
             if isinstance(ch, int):
-                if 0 <= ch < self.early or ch in self.late:
+                if 0 <= ch < self.early:
                     self.finish(stage, ch)
             else:
 
@@ -195,22 +185,96 @@
                     self.finish(stage, ch)
 
     def last_tick(self):
-        return max(self.late) + LAG * len(self.stages)
+        return self.early - 1 + LAG * len(self.stages)
+
+
+class Late:
+    def __init__(self, net, first, grads, pair, wide, part, quarter, cross, fin, send_sem, recv_sem):
+        self.net, self.first, self.fin = net, first, fin
+        self.grads, self.pair, self.wide, self.part = grads, pair, wide, part
+        self.quarter, self.cross = quarter, cross
+        self.send_sem, self.recv_sem = send_sem, recv_sem
+        self.low = min(net.b, 2)
+        self.stages = ["core", "chips", "split"] + (["cross"] if net.b > 2 else []) + ["back"]
+
+    def copies(self, c, kind):
+        net, a = self.net, self.net.a
+        mine = tuple(net.rb[: self.low])
+        moves = []
+        if kind == "core":
+            left = range(a - 1, -1, -1)
+            moves.append((self.grads.at[(c % 2,) + net.pick(left, 0, False)], self.pair.at[c], net.seq_xor(1)))
+        elif kind == "chips":
+            for m in range(1, 2 ** (a - 1)):
+                spot = tuple((1 - net.sb[i] if m >> (i - 1) & 1 else net.sb[i]) for i in range(a - 1, 0, -1))
+                moves.append((self.pair.at[(c,) + spot], self.wide.at[c, m - 1], net.seq_xor(2 * m)))
+        elif kind == "split":
+            for m in range(1, 2**self.low):
+                spot = tuple((1 - net.rb[i] if m >> i & 1 else net.rb[i]) for i in range(self.low))
+                moves.append((self.part.at[(c,) + spot], self.quarter.at[c, m - 1], net.row_xor(m)))
+        elif kind == "cross":
+            spot = self.cross.at[c, net.row // 4]
+            for m in range(1, 2 ** (net.b - 2)):
+                moves.append((spot, spot, net.row_xor(4 * m)))
+        else:
+            spot = self.fin.at[(self.first + c,) + mine]
+            for m in range(1, 2**self.low):
+                moves.append((spot, spot, net.row_xor(m)))
+        base = sum(len(self.copies(c, k)) for k in self.stages[: self.stages.index(kind)])
+        return [
+            remote(src, dst, self.send_sem.at[c, base + i], self.recv_sem.at[c, base + i], peer)
+            for i, (src, dst, peer) in enumerate(moves)
+        ]
+
+    def start(self, c, kind="core"):
+        for copy in self.copies(c, kind):
+            copy.start()
+
+    def finish(self, c, kind):
+        net, a = self.net, self.net.a
+        for copy in self.copies(c, kind):
+            copy.wait()
+        mine = tuple(net.rb[: self.low])
+        at = self.stages.index(kind)
+        if kind == "core":
+            self.pair[c] = self.pair[c] + self.grads[(c % 2,) + net.pick(range(a - 1, -1, -1), 0, True)]
+        elif kind == "chips":
+            total = self.pair[(c,) + tuple(net.sb[i] for i in range(a - 1, 0, -1))].astype(F32)
+            for m in range(1, 2 ** (a - 1)):
+                total = total + self.wide[c, m - 1].astype(F32)
+            self.part[c] = total.astype(BF)
+        elif kind == "split":
+            total = self.part[(c,) + mine].astype(F32)
+            for m in range(1, 2**self.low):
+                total = total + self.quarter[c, m - 1].astype(F32)
+            if net.b > 2:
+                self.cross[c, net.row // 4] = total.astype(BF)
+            else:
+                self.fin[(self.first + c,) + mine] = total.astype(BF)
+        elif kind == "cross":
+            total = self.cross[c, 0].astype(F32)
+            for i in range(1, 2 ** (net.b - 2)):
+                total = total + self.cross[c, i].astype(F32)
+            self.fin[(self.first + c,) + mine] = total.astype(BF)
+        if at + 1 < len(self.stages):
+            self.start(c, self.stages[at + 1])
 
 
 def layer_kernel(
-    seq_bits, row_bits, late,
+    seq_bits, row_bits,
     len_ref, x_ref, dy_ref, fg_ref, fs_ref, sg_ref, ss_ref, bq_ref, bo_ref, bd_ref, bkv_ref, bu_ref, wq_hbm, wkv_hbm, wo_hbm, wu_hbm, wd_hbm,
-    lo_ref, ig_ref, fin, small_ref,
+    lo_ref, ig_ref, fin, small_ref, gkv_ref,
     wq, wkv, wo, wu, wd, load_sem, vec_ref, wide_ref,
     h1, h2, act, act_t, dup, gub, q_all, do_all, cs, kv_all, kv_send, kv_recv,
-    s_ref, e_ref, qz, dz, m_ref, l_ref, o_ref, dqa, mt, mx, dq, dkv, dkv_in, dkv_sum, dkv_send, dkv_recv,
+    s_ref, e_ref, qz, dz, m_ref, l_ref, o_ref, dqa, mt, dq, dkv, dkv_in, dkv_core, dkv_chip, dkv_sum, dkv_send, dkv_recv,
     grads, *rest,
 ):
     a, n, count = seq_bits, 2**seq_bits, 2**row_bits
     recs, rest = rest[:a], rest[a:]
     recz, rest = rest[:row_bits], rest[row_bits:]
-    send_sem, recv_sem, own_small, seq_small, row_small, m_send, m_recv = rest
+    send_sem, recv_sem, rest = rest[0], rest[1], rest[2:]
+    late_refs, rest = rest[:8], rest[8:]
+    own_small, seq_small, row_small, own_kv, seq_kv, row_kv, m_send, m_recv = rest
     toks, width = x_ref.shape
     hidden = wu.shape[1]
     sub = width // n
@@ -222,15 +286,19 @@
     n_up, n_down = hidden // CHUNK, width // QUARTER
     net = Net(seq_bits, row_bits)
     me = net.me
-    ring = Ring(net, n_up + n_down, late, grads, recs, recz, fin, send_sem, recv_sem)
+    n_early = n_up + n_down
+    ring = Ring(net, n_early, grads, recs, recz, fin, send_sem, recv_sem)
+    late = Late(net, n_early, *late_refs[:6], fin, *late_refs[6:])
 
     barrier = pltpu.get_barrier_semaphore()
     for peer in net.peers():
         pl.semaphore_signal(barrier, inc=1, device_id=peer, device_id_type=MESH)
     loads = {}
-    for i, (name, src, dst) in enumerate(
-        (("kv", wkv_hbm, wkv), ("q", wq_hbm, wq), ("o", wo_hbm, wo), ("u", wu_hbm, wu), ("d", wd_hbm, wd))
-    ):
+    head, tail = slice(0, CHUNK), slice(CHUNK, hidden)
+    for i, (name, src, dst) in enumerate((
+        ("kv", wkv_hbm, wkv), ("u0", wu_hbm.at[:, head], wu.at[:, head]), ("d0", wd_hbm.at[head], wd.at[head]),
+        ("q", wq_hbm, wq), ("o", wo_hbm, wo), ("u", wu_hbm.at[:, tail], wu.at[:, tail]), ("d", wd_hbm.at[tail], wd.at[tail]),
+    )):
         loads[name] = pltpu.make_async_copy(src, dst, load_sem.at[i])
         loads[name].start()
 
@@ -239,13 +307,12 @@
     vec_ref[5:6, :] = (bo_ref[...] + bd_ref[...]).reshape(1, width)
     wide_ref[...] = bu_ref[...].reshape(1, hidden)
 
-    def put_chunk(ch, owner, value, quarters):
-        at = (ch % SLOTS,) + tuple(reversed(bits_of(owner, a)))
-        for i, q in enumerate(quarters):
-            grads[at + (q // 2, q % 2)] = value[:, i * QUARTER : (i + 1) * QUARTER].astype(BF)
-
-    def part(owner):
-        return slice(owner * sub, (owner + 1) * sub)
+    def put_chunk(ref, ch, value, quarters=range(4)):
+        for owner in range(n):
+            at = (ch,) + tuple(reversed(bits_of(owner, a)))
+            for i, q in enumerate(quarters):
+                piece = value[owner * sub : (owner + 1) * sub, i * QUARTER : (i + 1) * QUARTER]
+                ref[at + (q // 2, q % 2)] = piece.astype(BF)
 
     def row_cuts(r):
         cuts = []
@@ -325,28 +392,6 @@
                 copy.start()
 
     kv_step(0)
-
-    loads["q"].wait()
-    by_rows(0, dot(h1[...], wq[...]) + vec_ref[4:5, :])
-    loads["o"].wait()
-    by_rows(1, dot_nt(dy_ref[...], wo[...]))
-    kv_step(1)
-
-    def heads_apart(r, _):
-        for h in range(0, heads, 2):
-            pair = s_ref[spare(0, r, slice(h * HD, (h + 2) * HD))].T
-            d_pair = s_ref[spare(1, r, slice(h * HD, (h + 2) * HD))].T.astype(BF)
-            for i in (0, 1):
-                span = slice((h + i) * BLK, (h + i + 1) * BLK)
-                turned = rotate(pair[i * HD : (i + 1) * HD], cs[r, 0], cs[r, 1]).astype(BF).astype(F32)
-                q_all[r, :, span] = (turned * 0.125).astype(BF)
-                do_all[r, :, span] = d_pair[i * HD : (i + 1) * HD]
-        return 0
-
-    lax.fori_loop(0, rows, heads_apart, 0)
-    kv_step(2)
-    loads["u"].wait()
-    loads["d"].wait()
 
     def feed(f):
         cols = pl.ds(pl.multiple_of(f * CHUNK, CHUNK), CHUNK)
@@ -360,8 +405,7 @@
         dup[:, cols] = d_up
         gub[:, cols] = column_sum(d_up.astype(F32))
         g = dot_tn(h2[...], d_up)
-        for owner in range(n):
-            put_chunk(f, owner, g[part(owner)], range(4))
+        put_chunk(grads, f % SLOTS, g)
 
     def down(j):
         cols = dy_ref[:, pl.ds(pl.multiple_of(j * QUARTER, QUARTER), QUARTER)]
@@ -371,7 +415,8 @@
             for i in range(4):
                 grads[at + (i // 2, i % 2)] = g[i * sub : (i + 1) * sub]
 
-    n_pre = n_up + n_down - 3 * (rows - 1)
+    n_pre = 3
+    dkv[...] = jnp.zeros(dkv.shape, BF)
 
     def feed_step(t, _):
         feed(t)
@@ -379,12 +424,43 @@
         ring.tick(t)
         return 0
 
-    lax.fori_loop(0, n_pre, feed_step, 0)
+    loads["u0"].wait()
+    loads["d0"].wait()
+    feed_step(0, 0)
+
+    loads["q"].wait()
+    by_rows(0, dot(h1[...], wq[...]) + vec_ref[4:5, :])
+    loads["o"].wait()
+    by_rows(1, dot_nt(dy_ref[...], wo[...]))
+    kv_step(1)
+
+    def heads_apart(r, _):
+        for h in range(0, heads, 2):
+            pair = s_ref[spare(0, r, slice(h * HD, (h + 2) * HD))].T
+            d_pair = s_ref[spare(1, r, slice(h * HD, (h + 2) * HD))].T.astype(BF)
+            for i in (0, 1):
+                span = slice((h + i) * BLK, (h + i + 1) * BLK)
+                turned = rotate(pair[i * HD : (i + 1) * HD], cs[r, 0], cs[r, 1]).astype(BF).astype(F32)
+                q_all[r, :, span] = (turned * 0.125).astype(BF)
+                do_all[r, :, span] = d_pair[i * HD : (i + 1) * HD]
+        return 0
+
+    lax.fori_loop(0, rows, heads_apart, 0)
+    kv_step(2)
+
+    loads["u"].wait()
+    loads["d"].wait()
+    lax.fori_loop(1, n_pre, feed_step, 0)
     for k in range(3, a + 1):
         kv_step(k)
 
-    key_iota = lax.broadcasted_iota(jnp.int32, (BLK, BLK), 0)
-    query_place = me * BLK + lax.broadcasted_iota(jnp.int32, (BLK, BLK), 1)
+    keys_at_once = PAIR * BLK
+    steps = me // PAIR + 1
+    key_iota = lax.broadcasted_iota(jnp.int32, (keys_at_once, BLK), 0)
+    query_place = me * BLK + lax.broadcasted_iota(jnp.int32, (keys_at_once, BLK), 1)
+
+    def kv_blocks(i, r):
+        return jnp.concatenate([kv_all[kv_at(PAIR * i + k, r)] for k in range(PAIR)], axis=0)
 
     def scores_pass(r, g):
         span = slice(g * lanes, (g + 1) * lanes)
@@ -398,28 +474,28 @@
         dqa[...] = jnp.zeros(dqa.shape, F32)
         begin = doc_start(query_place, row_cuts(r))
 
-        def body(j, _):
-            keys = j * BLK + key_iota
+        def body(i, _):
+            keys = i * keys_at_once + key_iota
             bias = jnp.where((keys <= query_place) & (keys >= begin), 0.0, NEG)
-            s = dot(kv_all[kv_at(j, r)], qz[...]) + jnp.concatenate([bias] * near, axis=1)
-            s_ref[j] = s
-            m_ref[...] = jnp.maximum(m_ref[...], jnp.max(s.reshape(BLK // 8, 8, lanes), axis=0))
+            s = dot(kv_blocks(i, r), qz[...]) + jnp.concatenate([bias] * near, axis=1)
+            s_ref[pl.ds(PAIR * i, PAIR)] = s.reshape(PAIR, BLK, lanes)
+            m_ref[...] = jnp.maximum(m_ref[...], jnp.max(s.reshape(keys_at_once // 8, 8, lanes), axis=0))
             return 0
 
-        lax.fori_loop(0, me + 1, body, 0)
+        lax.fori_loop(0, steps, body, 0)
         m_ref[0:1, :] = jnp.max(m_ref[...], axis=0, keepdims=True)
 
     def mix_pass(r, g):
-        def body(j, _):
-            v_t = kv_all[kv_at(j, r)].T[HD:]
-            e = jnp.exp(s_ref[j] - m_ref[0:1, :])
-            l_ref[...] += jnp.sum(e.reshape(BLK // 8, 8, lanes), axis=0)
+        def body(i, _):
+            v_t = kv_blocks(i, r).T[HD:]
+            e = jnp.exp(s_ref[pl.ds(PAIR * i, PAIR)].reshape(keys_at_once, lanes) - m_ref[0:1, :])
+            l_ref[...] += jnp.sum(e.reshape(keys_at_once // 8, 8, lanes), axis=0)
             e_low = e.astype(BF)
-            e_ref[j] = e_low
+            e_ref[pl.ds(PAIR * i, PAIR)] = e_low.reshape(PAIR, BLK, lanes)
             o_ref[...] += dot(v_t, e_low)
             return 0
 
-        lax.fori_loop(0, me + 1, body, 0)
+        lax.fori_loop(0, steps, body, 0)
         inv = 1.0 / jnp.sum(l_ref[...], axis=0, keepdims=True)
         o = o_ref[...] * inv
         l_ref[0:1, :] = inv
@@ -431,39 +507,70 @@
             )
             at = slice((g * near + h) * HD, (g * near + h + 2) * HD)
             mt[at, span] = pair.astype(BF)
-            mx[span, at] = pair.T.astype(BF)
 
     def back_pass(r, g, start, stop):
-        def body(j, _):
-            kv = kv_all[kv_at(j, r)]
+        def body(i, _):
+            kv = kv_blocks(i, r)
             k_t = kv.T[:HD]
             dp = dot(kv, dz[...])
-            p = e_ref[j].astype(F32) * l_ref[0:1, :]
+            p = e_ref[pl.ds(PAIR * i, PAIR)].reshape(keys_at_once, lanes).astype(F32) * l_ref[0:1, :]
             ds = (p * (dp - m_ref[0:1, :])).astype(BF)
             total = dot_nt(ds, qz[...]) + dot_nt(p.astype(BF), dz[...])
-            if g > 0:
-                total = total + dkv[j, r].astype(F32)
-            dkv[j, r] = total.astype(BF)
+            for k in range(PAIR):
+                block = total[k * BLK : (k + 1) * BLK]
+                if g > 0:
+                    block = block + dkv[at_bits(PAIR * i + k) + (r,)].astype(F32)
+                dkv[at_bits(PAIR * i + k) + (r,)] = block.astype(BF)
             dqa[...] += dot(k_t, ds)
             return 0
 
         lax.fori_loop(start, stop, body, 0)
 
-    def dkv_copies(r):
+    upper = range(a - 1, 0, -1)
+
+    def dkv_pair(r):
+        src = dkv.at[net.pick(range(a - 1, -1, -1), 0, False) + (r,)]
+        return remote(src, dkv_core.at[r], dkv_send.at[r, 0], dkv_recv.at[r, 0], net.seq_xor(1))
+
+    def dkv_chips(r):
+        out = []
+        for m in range(1, 2 ** (a - 1)):
+            spot = tuple((1 - net.sb[i] if m >> (i - 1) & 1 else net.sb[i]) for i in upper)
+            out.append(remote(dkv_core.at[(r,) + spot], dkv_chip.at[m - 1, r], dkv_send.at[r, m], dkv_recv.at[r, m],
+                              net.seq_xor(2 * m)))
+        return out
+
+    def dkv_on(r):
+        dkv_pair(r).wait()
+        dkv_core[r] = dkv_core[r] + dkv[net.pick(range(a - 1, -1, -1), 0, True) + (r,)]
+        for copy in dkv_chips(r):
+            copy.start()
+
+    def dkv_straight():
         out = []
         for m in range(1, n):
             peer = net.seq_xor(m)
             out.append((peer["seq"], remote(
-                dkv.at[peer["seq"], r], dkv_in.at[m - 1, r], dkv_send.at[m - 1, r], dkv_recv.at[m - 1, r], peer)))
+                dkv.at[at_bits(peer["seq"]) + (rows - 1,)], dkv_in.at[m - 1],
+                dkv_send.at[rows - 1, m - 1], dkv_recv.at[rows - 1, m - 1], peer)))
         return out
 
     def leave_pass(r, g):
         if g == groups - 1:
-            for other, copy in dkv_copies(r):
-
-                @pl.when(other < me)
+            if isinstance(r, int):
+                for other, copy in dkv_straight():
+
+                    @pl.when(other < me)
+                    def _():
+                        copy.start()
+
+                dkv_on(r - 1)
+            else:
+                dkv_pair(r).start()
+
+                @pl.when(r > 0)
                 def _():
-                    copy.start()
+                    dkv_on(r - 1)
 
         cosine, sine = cs[r, 0], cs[r, 1]
         span = row_span(r)
@@ -477,10 +584,16 @@
         for g in range(groups - 1):
             scores_pass(r, g)
             mix_pass(r, g)
-            back_pass(r, g, 0, me + 1)
+            back_pass(r, g, 0, steps)
             leave_pass(r, g)
 
     def chunk_step(t):
+        if isinstance(t, int):
+            down(t - n_up)
+            ring.start(0, t)
+            ring.tick(t)
+            return
+
         @pl.when(t < n_up)
         def _():
             feed(t)
@@ -499,64 +612,98 @@
         chunk_step(t)
         mix_pass(r, groups - 1)
         chunk_step(t + 1)
-        back_pass(r, groups - 1, 0, me + 1)
+        back_pass(r, groups - 1, 0, steps)
         leave_pass(r, groups - 1)
         chunk_step(t + 2)
         return 0
 
     lax.fori_loop(0, rows - 1, row_step, 0)
     r, t = rows - 1, n_up + n_down
+    now = [t]
+
+    def advance(count):
+        for _ in range(count):
+            if now[0] <= ring.last_tick():
+                ring.tick(now[0])
+                now[0] += 1
+
     first_groups(r)
     scores_pass(r, groups - 1)
-    ring.tick(t)
+    advance(1)
     mix_pass(r, groups - 1)
-    g = dot(mt[...], dy_ref[:, :CHUNK])
-    for owner in range(n):
-        put_chunk(late[0], owner, g[part(owner)], range(4))
-    ring.start(0, late[0])
-    ring.tick(late[0])
-    g = dot(mt[...], dy_ref[:, CHUNK:])
-    for owner in range(n):
-        put_chunk(late[1], owner, g[part(owner)], range(2))
-    ring.start(0, late[1])
-    ring.tick(late[1])
-    back_pass(r, groups - 1, 0, (me + 1) // 2)
-    ring.tick(late[1] + 1)
-    back_pass(r, groups - 1, (me + 1) // 2, me + 1)
+    put_chunk(late.grads, 0, dot(mt[...], dy_ref[:, :CHUNK]))
+    late.start(0)
+    advance(2)
+    back_pass(r, groups - 1, 0, steps // 2)
+    late.finish(0, "core")
+    put_chunk(late.grads, 0, dot(mt[...], dy_ref[:, CHUNK:]), (0, 1))
+    advance(2)
+    back_pass(r, groups - 1, steps // 2, steps)
     leave_pass(r, groups - 1)
-    ring.tick(late[1] + 2)
-    g = dot_tn(h1[...], dq[:, :CHUNK])
-    for owner in range(n):
-        put_chunk(late[2], owner, g[part(owner)], range(4))
-    ring.start(0, late[2])
-    ring.tick(late[2])
-    g = dot_tn(h1[...], dq[:, CHUNK:])
-    for owner in range(n):
-        put_chunk(late[3], owner, g[part(owner)], range(2))
+    advance(2)
+    put_chunk(late.grads, 1, dot_tn(h1[...], dq[:, :CHUNK]))
+    late.start(1)
+    late.finish(0, "chips")
+    put_chunk(late.grads, 0, dot_tn(h1[...], dq[:, CHUNK:]), (2, 3))
+    late.start(2)
+    advance(2)
+    late.finish(1, "core")
     by_rows(0, dot_nt(dup[...], wu[...]))
-
-    dkv_sum[...] = dkv[me].astype(F32)
-    for r in range(rows):
-        for m, (other, copy) in enumerate(dkv_copies(r)):
-
-            @pl.when(other < me)
-            def _():
-                copy.wait_send()
-
-            @pl.when(other > me)
-            def _():
-                copy.wait_recv()
-                dkv_sum[r] += dkv_in[m, r].astype(F32)
+    late.finish(2, "core")
+    advance(2)
+    for kind in late.stages[2:-1]:
+        late.finish(0, kind)
+
+    def narrow(step):
+        if step == 0:
+            return [
+                remote(own_small, seq_small.at[me], m_send.at[m - 1], m_recv.at[m - 1], net.seq_xor(m)) for m in range(1, n)
+            ]
+        spot, base = row_small.at[net.row], n - 2
+        return [
+            remote(spot, spot, m_send.at[base + m], m_recv.at[base + m], net.row_xor(m)) for m in range(1, count)
+        ]
+
+    def narrow_kv(step):
+        base = n + count - 2
+        if step == 0:
+            out = []
+            for m in range(1, n):
+                peer = net.seq_xor(m)
+                out.append(remote(own_kv.at[peer["seq"]], seq_kv.at[m - 1],
+                                  m_send.at[base + m - 1], m_recv.at[base + m - 1], peer))
+            return out
+        spot, base = row_kv.at[net.row], base + n - 2
+        return [
+            remote(spot, spot, m_send.at[base + m], m_recv.at[base + m], net.row_xor(m)) for m in range(1, count)
+        ]
+
+    dkv_sum[rows - 1] = dkv[at_bits(me) + (rows - 1,)].astype(F32)
+    for r in range(rows - 1):
+        total = dkv_core[(r,) + tuple(net.sb[i] for i in upper)].astype(F32)
+        for m, copy in enumerate(dkv_chips(r)):
+            copy.wait()
+            total = total + dkv_chip[m, r].astype(F32)
+        dkv_sum[r] = total
+    for m, (other, copy) in enumerate(dkv_straight()):
+
+        @pl.when(other < me)
+        def _():
+            copy.wait_send()
+
+        @pl.when(other > me)
+        def _():
+            copy.wait_recv()
+            dkv_sum[rows - 1] += dkv_in[m].astype(F32)
 
     d_kv = jnp.concatenate(
         [rotate(dkv_sum[r].T, cs[r, 0], -cs[r, 1]).T.astype(BF) for r in range(rows)], axis=0
     )
     g = dot_tn(h1[...], d_kv)
     for owner in range(n):
-        put_chunk(late[3], owner, g[part(owner)], (2,))
-        put_chunk(late[3], owner, jnp.zeros((sub, QUARTER), F32), (3,))
-    ring.start(0, late[3])
-    ring.tick(late[3])
+        own_kv[owner] = g[owner * sub : (owner + 1) * sub].astype(BF)
+    for copy in narrow_kv(0):
+        copy.start()
 
     by_rows(1, dot_nt(dq[...], wq[...]) + dot_nt(d_kv, wkv[...]))
     own_small[...] = jnp.zeros(own_small.shape, F32)
@@ -582,26 +729,25 @@
         return 0
 
     lax.fori_loop(0, rows, norms_back, 0)
-    ig_copy = pltpu.make_async_copy(h2, ig_ref, load_sem.at[5])
+    ig_copy = pltpu.make_async_copy(h2, ig_ref, load_sem.at[7])
     ig_copy.start()
     add_small(5 * per, column_sum(d_kv.astype(F32)))
     add_small(6 * per + 1, gub[...])
 
-    def narrow(step):
-        if step == 0:
-            return [
-                remote(own_small, seq_small.at[me], m_send.at[m - 1], m_recv.at[m - 1], net.seq_xor(m)) for m in range(1, n)
-            ]
-        spot = row_small.at[net.row]
-        return [
-            remote(spot, spot, m_send.at[n + m - 2], m_recv.at[n + m - 2], net.row_xor(m)) for m in range(1, count)
-        ]
-
     for copy in narrow(0):
         copy.start()
-    ring.tick(late[3] + 1)
+    late.finish(1, "chips")
+    late.finish(2, "chips")
+    advance(2)
     by_rows(2, dot(act[...], wd[...]) + vec_ref[5:6, :])
-    ring.tick(late[3] + 2)
+    for copy in narrow_kv(0):
+        copy.wait()
+    sums = own_kv[me].astype(F32)
+    for m in range(1, n):
+        sums = sums + seq_kv[m - 1].astype(F32)
+    row_kv[net.row] = sums.astype(BF)
+    for copy in narrow_kv(1):
+        copy.start()
     for copy in narrow(0):
         copy.wait()
     seq_small[me] = own_small[...]
@@ -611,8 +757,10 @@
     row_small[net.row] = sums
     for copy in narrow(1):
         copy.start()
-    ring.tick(late[3] + 3)
-    by_rows(3, dot(mx[...], wo[...]))
+    for c in (1, 2):
+        for kind in late.stages[2:-1]:
+            late.finish(c, kind)
+    by_rows(3, dot_tn(mt[...], wo[...]))
 
     def layer_out(r, _):
         total = x_ref[row_span(r), :].astype(F32) + s_ref[spare(2, r)] + s_ref[spare(3, r)]
@@ -620,16 +768,23 @@
         return 0
 
     lax.fori_loop(0, rows, layer_out, 0)
-    lo_copy = pltpu.make_async_copy(h1, lo_ref, load_sem.at[6])
+    lo_copy = pltpu.make_async_copy(h1, lo_ref, load_sem.at[8])
     lo_copy.start()
-    for t in range(late[3] + 4, ring.last_tick() + 1):
-        ring.tick(t)
+    advance(99)
+    for c in range(3):
+        late.finish(c, "back")
     for copy in narrow(1):
         copy.wait()
     sums = row_small[0]
     for i in range(1, count):
         sums = sums + row_small[i]
     small_ref[...] = sums
+    for copy in narrow_kv(1):
+        copy.wait()
+    sums = row_kv[0].astype(F32)
+    for i in range(1, count):
+        sums = sums + row_kv[i].astype(F32)
+    gkv_ref[...] = sums
     ig_copy.wait()
     lo_copy.wait()
 
@@ -644,16 +799,16 @@
     all_lanes = width // HD * BLK
     lanes = all_lanes // max(1, n // 8)
     n_up, n_down = hidden // CHUNK, width // QUARTER
-    last_row = n_up + n_down
-    late = [last_row + 1, last_row + 2, last_row + 5, last_row + 6]
-    total = n_up + n_down + len(late)
-    slots = RING + len(late)
+    early, late = n_up + n_down, 3
+    total = early + late
+    slots = RING
+    low = min(b, 2)
     two = (2,)
     vm = pltpu.VMEM
     dma = pltpu.SemaphoreType.DMA
     n_sems = 1 + 2 * (a - 1) + b + min(b, 2)
     scratch = [
-        vm(wq.shape, BF), vm(wkv.shape, BF), vm(wo.shape, BF), vm(wu.shape, BF), vm(wd.shape, BF), dma((7,)),
+        vm(wq.shape, BF), vm(wkv.shape, BF), vm(wo.shape, BF), vm(wu.shape, BF), vm(wd.shape, BF), dma((9,)),
         vm((8, width), F32), vm((1, hidden), F32),
         vm((toks, width), BF), vm((toks, width), BF),
         vm((toks, hidden), BF), vm((hidden, toks), BF), vm((toks, hidden), BF), vm((1, hidden), F32),
@@ -661,37 +816,46 @@
         vm(two * a + (2, rows // 2, BLK, 2 * HD), BF), dma((2 * a,)), dma((2 * a,)),
         vm((n, BLK, lanes), F32), vm((n, BLK, lanes), BF), vm((2 * HD, lanes), BF), vm((2 * HD, lanes), BF),
         vm((8, lanes), F32), vm((8, lanes), F32), vm((HD, lanes), F32), vm((HD, lanes), F32),
-        vm((width, toks), BF), vm((toks, width), BF), vm((toks, width), BF),
-        vm((n, rows, BLK, 2 * HD), BF), vm((n - 1, rows, BLK, 2 * HD), BF), vm((rows, BLK, 2 * HD), F32),
-        dma((n - 1, rows)), dma((n - 1, rows)),
+        vm((width, toks), BF), vm((toks, width), BF),
+        vm(two * a + (rows, BLK, 2 * HD), BF), vm((n - 1, BLK, 2 * HD), BF),
+        vm((rows - 1,) + two * (a - 1) + (BLK, 2 * HD), BF), vm((n // 2 - 1, rows - 1, BLK, 2 * HD), BF),
+        vm((rows, BLK, 2 * HD), F32), dma((rows, n - 1)), dma((rows, n - 1)),
         vm((SLOTS,) + two * a + (2, 2, sub, 128), BF),
         vm((slots,) + two * (a - 1) + (2, 2, sub, 128), BF),
     ]
     scratch += [vm((slots, 2) + two * (a - 1 - k) + (2, sub, 128), BF) for k in range(1, a)]
     scratch += [vm((slots, 2, sub, 128), BF)] + [vm((slots, sub, 128), BF) for _ in range(1, b)]
     scratch += [
-        dma((total, n_sems)), dma((total, n_sems)),
+        dma((early, n_sems)), dma((early, n_sems)),
+        vm((2,) + two * a + (2, 2, sub, 128), BF),
+        vm((late,) + two * (a - 1) + (2, 2, sub, 128), BF),
+        vm((late, n // 2 - 1, 2, 2, sub, 128), BF),
+        vm((late, 2, 2, sub, 128), BF),
+        vm((late, 2**low - 1, sub, 128), BF),
+        vm((late, max(count // 4, 1), sub, 128), BF),
+        dma((late, n // 2 + count + 2)), dma((late, n // 2 + count + 2)),
         vm((64, 128), F32), vm((n, 64, 128), F32), vm((count, 64, 128), F32),
-        dma((n + count,)), dma((n + count,)),
+        vm((n, sub, 2 * HD), BF), vm((n - 1, sub, 2 * HD), BF), vm((count, sub, 2 * HD), BF),
+        dma((2 * (n + count),)), dma((2 * (n + count),)),
     ]
     vmem = pl.BlockSpec(memory_space=pltpu.VMEM)
     hbm = pl.BlockSpec(memory_space=pl.ANY)
     shape = jax.ShapeDtypeStruct
     return pl.pallas_call(
-        functools.partial(layer_kernel, a, b, late),
+        functools.partial(layer_kernel, a, b),
         out_shape=[
             shape((toks, width), BF), shape((toks, width), BF),
-            shape((total, 2, 2, sub, 128), BF), shape((64, 128), F32),
+            shape((total, 2, 2, sub, 128), BF), shape((64, 128), F32), shape((sub, 2 * HD), F32),
         ],
         in_specs=[pl.BlockSpec(memory_space=pltpu.SMEM)] + [vmem] * (2 + len(vectors)) + [hbm] * 5,
-        out_specs=[hbm, hbm, vmem, vmem],
+        out_specs=[hbm, hbm, vmem, vmem, vmem],
         scratch_shapes=scratch,
         compiler_params=pltpu.CompilerParams(collective_id=0, has_side_effects=True, vmem_limit_bytes=64 * 2**20),
         name="layer",
     )(lengths, x, dy, *vectors, wq, wkv, wo, wu, wd)
 
 
-def finish_kernel(n_up, sizes, lo_in, ig_in, fin_in, small_in, lo, ig, gup, gdown, gout, gq, gkv, *rest):
+def finish_kernel(n_up, sizes, lo_in, ig_in, fin_in, small_in, gkv_in, lo, ig, gup, gdown, gout, gq, gkv, *rest):
     vectors, (fin, small, vlo, vig, vup, vdown, vout, vq, vkv, sem) = rest[: len(sizes)], rest[len(sizes) :]
     sub, width = gout.shape
     n_down = width // QUARTER
@@ -702,7 +866,7 @@
         copy.start()
         return copy
 
-    loads = [move(0, fin_in, fin), move(1, small_in, small)]
+    loads = [move(0, fin_in, fin), move(1, small_in, small), move(8, gkv_in, vkv)]
     loads += [move(2, lo_in, vlo), move(3, ig_in, vig)]
     for load in loads:
         load.wait()
@@ -724,12 +888,11 @@
     moves.append(move(5, vdown, gdown))
     for q in range(4):
         vout[:, span(0, q)] = piece(late, q)
-        vq[:, span(0, q)] = piece(late + 2, q)
+        vq[:, span(0, q)] = piece(late + 1, q)
         if q < 2:
-            vout[:, span(CHUNK, q)] = piece(late + 1, q)
-            vq[:, span(CHUNK, q)] = piece(late + 3, q)
-    vkv[...] = piece(late + 3, 2)
-    moves += [move(6, vout, gout), move(7, vq, gq), move(8, vkv, gkv)]
+            vout[:, span(CHUNK, q)] = piece(late + 2, q)
+            vq[:, span(CHUNK, q)] = piece(late + 2, q + 2)
+    moves += [move(6, vout, gout), move(7, vq, gq), move(11, vkv, gkv)]
     at = 0
     for size, ref in zip(sizes[:-1], vectors):
         for i in range(size // 128):
@@ -740,7 +903,7 @@
         copy.wait()
 
 
-def finish(lo, ig, fin, small, sub, width, hidden):
+def finish(lo, ig, fin, small, gkv, sub, width, hidden):
     sizes = [width] * 5 + [2 * HD, width, hidden, width]
     shape = jax.ShapeDtypeStruct
     hbm = pl.BlockSpec(memory_space=pl.ANY)
@@ -749,13 +912,13 @@
         functools.partial(finish_kernel, hidden // CHUNK, sizes),
         out_shape=[shape(lo.shape, BF), shape(ig.shape, BF)]
         + [shape(g, F32) for g in grads] + [shape((size,), F32) for size in sizes],
-        in_specs=[hbm] * 4,
+        in_specs=[hbm] * 5,
         out_specs=[hbm] * 7 + [pl.BlockSpec(memory_space=pltpu.VMEM)] * len(sizes),
         scratch_shapes=[pltpu.VMEM(fin.shape, BF), pltpu.VMEM(small.shape, F32), pltpu.VMEM(lo.shape, BF), pltpu.VMEM(ig.shape, BF)]
-        + [pltpu.VMEM(g, F32) for g in grads] + [pltpu.SemaphoreType.DMA((11,))],
+        + [pltpu.VMEM(g, F32) for g in grads] + [pltpu.SemaphoreType.DMA((12,))],
         compiler_params=pltpu.CompilerParams(vmem_limit_bytes=64 * 2**20),
         name="finish",
-    )(lo, ig, fin, small)
+    )(lo, ig, fin, small, gkv)
 
 
 def shards(
@@ -769,12 +932,14 @@
     vectors = (
         first_gain, first_shift, second_gain, second_shift, query_bias, output_bias, down_bias, keyvalue_bias, up_bias,
     )
-    lo, ig, fin, small = layer(
+    lo, ig, fin, small, g_kv = layer(
         (n.bit_length() - 1, count.bit_length() - 1), lengths,
         hidden.reshape(toks, width), cotangent.reshape(toks, width), vectors,
         query_weight, keyvalue_weight, output_weight, up_weight, down_weight,
     )
-    lo, ig, g_up, g_down, g_out, g_q, g_kv, *sums = finish(lo, ig, fin, small, width // n, width, up_weight.shape[1])
+    lo, ig, g_up, g_down, g_out, g_q, g_kv, *sums = finish(
+        lo, ig, fin, small, g_kv, width // n, width, up_weight.shape[1]
+    )
     s_fg, s_fs, s_sg, s_ss, s_qb, s_kb, s_ob, s_ub, s_db = sums
     return (
         lo.reshape(hidden.shape), ig.reshape(hidden.shape),

time: 126 us -> 113 us (0.90)
  Pallas kernels: 125 us -> 111 us
    pallas_call x1, Pallas kernels: 120 us -> 107 us  [layer(): pl.pallas_call(functools.partial(layer_kernel, a, b), out_shape=[shape((t...]
where the time goes in v4:
time: 113 us; the launch traced here: 112 us
  Pallas kernels  111 us (98%)
    pallas_call x1, Pallas kernels, layer(): pl.pallas_call(functools.partial(layer_kernel, a, b), out_shape=[shape((t...  107 us
    pallas_call x1, Pallas kernels, finish(): pl.pallas_call(functools.partial(finish_kernel, hidden // CHUNK, sizes),...  4.68 us

profile of v4, /device:TPU:0, one launch (start us, length us, event | category | flops | bytes accessed | tf_op | source)
XLA Modules:
  0.0 112.3 jit_solution(3851342517085605504)
XLA Ops:
  0.7 106.8 %layer.1 = (bf16[512,768]{1,0:T(8,128)(2,1)}, bf16[512,768]{1,0:T(8,128)(2,1)}, bf16[15,2,2,96,128]{4,3,2,1,0:T(8,128)(2,1)}, f32[64,128]{1,0:T(8,128)}, f32[96,128]{1,0:T(8,128)}) custom-call(s32[4,4]{1,0:T(4,128)} %len_ref.1, bf16[512,768]{1,0:T(8,128)(2,1)} %bitcast.4, bf16[512,768]{1,0:T(8,128)(2,1)} %bitcast.5, f32[768]{0:T(1024)} %fg_ref.1, ...), custom_call_target="tpu_custom_call" | custom-call | tf_op jit(solution)/shard_map/layer/pallas_call | solution.py:844
  107.5 4.7 %finish.1 = (bf16[512,768]{1,0:T(8,128)(2,1)}, bf16[512,768]{1,0:T(8,128)(2,1)}, f32[96,3072]{1,0:T(8,128)}, f32[384,768]{1,0:T(8,128)}, f32[96,768]{1,0:T(8,128...) custom-call(bf16[512,768]{1,0:T(8,128)(2,1)} %get-tuple-element.37.l, ...), custom_call_target="tpu_custom_call" | custom-call | tf_op jit(solution)/shard_map/finish/pallas_call | solution.py:911

commit v5 on v4

--- a/solution.py
+++ b/solution.py
@@ -18,9 +18,9 @@
 MESH = pl.DeviceIdType.MESH
 CHUNK = 512
 QUARTER = 128
-LAG = 2
-SLOTS = LAG + 1
-RING = 3 * LAG + 2
+SLOTS = 3
+RING = 8
+WAITS = {"first": 1, "seq": 2}
 
 
 def dot(a, b):
@@ -111,9 +111,12 @@
         self.stages += [("whole", i) for i in range(2, b)]
         self.stages += [("back", i) for i in reversed(range(self.halves))]
         self.sem_at, n = [], 0
+        self.ticks_to, ticks = [], 0
         for kind, _ in self.stages:
             self.sem_at.append(n)
             n += 2 if kind == "seq" else 1
+            ticks += WAITS.get(kind, 2)
+            self.ticks_to.append(ticks)
 
     def moves(self, stage, ch):
         net, a = self.net, self.net.a
@@ -174,7 +177,7 @@
 
     def tick(self, t):
         for stage in reversed(range(len(self.stages))):
-            ch = t - LAG * (stage + 1)
+            ch = t - self.ticks_to[stage]
             if isinstance(ch, int):
                 if 0 <= ch < self.early:
                     self.finish(stage, ch)
@@ -185,7 +188,7 @@
                     self.finish(stage, ch)
 
     def last_tick(self):
-        return self.early - 1 + LAG * len(self.stages)
+        return self.early - 1 + self.ticks_to[-1]
 
 
 class Late:
@@ -508,23 +511,25 @@
             at = slice((g * near + h) * HD, (g * near + h + 2) * HD)
             mt[at, span] = pair.astype(BF)
 
-    def back_pass(r, g, start, stop):
+    def back_pass(r, g, cols=slice(0, lanes), more=False):
+        wide = cols.stop - cols.start
+
         def body(i, _):
             kv = kv_blocks(i, r)
             k_t = kv.T[:HD]
-            dp = dot(kv, dz[...])
-            p = e_ref[pl.ds(PAIR * i, PAIR)].reshape(keys_at_once, lanes).astype(F32) * l_ref[0:1, :]
-            ds = (p * (dp - m_ref[0:1, :])).astype(BF)
-            total = dot_nt(ds, qz[...]) + dot_nt(p.astype(BF), dz[...])
+            dp = dot(kv, dz[:, cols])
+            p = e_ref[pl.ds(PAIR * i, PAIR), :, cols].reshape(keys_at_once, wide).astype(F32) * l_ref[0:1, cols]
+            ds = (p * (dp - m_ref[0:1, cols])).astype(BF)
+            total = dot_nt(ds, qz[:, cols]) + dot_nt(p.astype(BF), dz[:, cols])
             for k in range(PAIR):
                 block = total[k * BLK : (k + 1) * BLK]
-                if g > 0:
+                if g > 0 or more:
                     block = block + dkv[at_bits(PAIR * i + k) + (r,)].astype(F32)
                 dkv[at_bits(PAIR * i + k) + (r,)] = block.astype(BF)
-            dqa[...] += dot(k_t, ds)
+            dqa[:, cols] += dot(k_t, ds)
             return 0
 
-        lax.fori_loop(start, stop, body, 0)
+        lax.fori_loop(0, steps, body, 0)
 
     upper = range(a - 1, 0, -1)
 
@@ -555,36 +560,41 @@
                 dkv_send.at[rows - 1, m - 1], dkv_recv.at[rows - 1, m - 1], peer)))
         return out
 
-    def leave_pass(r, g):
-        if g == groups - 1:
-            if isinstance(r, int):
-                for other, copy in dkv_straight():
-
-                    @pl.when(other < me)
-                    def _():
-                        copy.start()
-
+    def dkv_leave(r):
+        if isinstance(r, int):
+            for other, copy in dkv_straight():
+
+                @pl.when(other < me)
+                def _():
+                    copy.start()
+
+            dkv_on(r - 1)
+        else:
+            dkv_pair(r).start()
+
+            @pl.when(r > 0)
+            def _():
                 dkv_on(r - 1)
-            else:
-                dkv_pair(r).start()
-
-                @pl.when(r > 0)
-                def _():
-                    dkv_on(r - 1)
-
+
+    def dq_leave(r, g, first=0, stop=near):
         cosine, sine = cs[r, 0], cs[r, 1]
         span = row_span(r)
-        for h in range(0, near, 2):
+        for h in range(first, stop, 2):
             pair = jnp.concatenate(
                 [rotate(dqa[:, i * BLK : (i + 1) * BLK], cosine, -sine) for i in (h, h + 1)], axis=0
             )
             dq[span, (g * near + h) * HD : (g * near + h + 2) * HD] = (pair * 0.125).T.astype(BF)
 
+    def leave_pass(r, g):
+        if g == groups - 1:
+            dkv_leave(r)
+        dq_leave(r, g)
+
     def first_groups(r):
         for g in range(groups - 1):
             scores_pass(r, g)
             mix_pass(r, g)
-            back_pass(r, g, 0, steps)
+            back_pass(r, g)
             leave_pass(r, g)
 
     def chunk_step(t):
@@ -612,7 +622,7 @@
         chunk_step(t)
         mix_pass(r, groups - 1)
         chunk_step(t + 1)
-        back_pass(r, groups - 1, 0, steps)
+        back_pass(r, groups - 1)
         leave_pass(r, groups - 1)
         chunk_step(t + 2)
         return 0
@@ -633,26 +643,35 @@
     mix_pass(r, groups - 1)
     put_chunk(late.grads, 0, dot(mt[...], dy_ref[:, :CHUNK]))
     late.start(0)
+    put_chunk(late.grads, 1, dot(mt[...], dy_ref[:, CHUNK : CHUNK + QUARTER]), (3,))
     advance(2)
-    back_pass(r, groups - 1, 0, steps // 2)
+    near_cols = slice(0, lanes // 2)
+    if groups == 1:
+        back_pass(r, 0, near_cols)
+        dq_leave(r, 0, 0, near // 2)
     late.finish(0, "core")
-    put_chunk(late.grads, 0, dot(mt[...], dy_ref[:, CHUNK:]), (0, 1))
+    put_chunk(late.grads, 1, dot_tn(h1[...], dq[:, : width // 2]), (0, 1, 2))
+    late.start(1)
+    put_chunk(late.grads, 0, dot(mt[...], dy_ref[:, CHUNK + QUARTER :]), (3,))
     advance(2)
-    back_pass(r, groups - 1, steps // 2, steps)
-    leave_pass(r, groups - 1)
-    advance(2)
-    put_chunk(late.grads, 1, dot_tn(h1[...], dq[:, :CHUNK]))
-    late.start(1)
-    late.finish(0, "chips")
-    put_chunk(late.grads, 0, dot_tn(h1[...], dq[:, CHUNK:]), (2, 3))
+    if groups == 1:
+        back_pass(r, 0, slice(lanes // 2, lanes), True)
+        dkv_leave(r)
+        dq_leave(r, 0, near // 2)
+    else:
+        back_pass(r, groups - 1)
+        leave_pass(r, groups - 1)
+    late.finish(1, "core")
+    put_chunk(late.grads, 0, dot_tn(h1[...], dq[:, width // 2 :]), (0, 1, 2))
     late.start(2)
-    advance(2)
-    late.finish(1, "core")
-    by_rows(0, dot_nt(dup[...], wu[...]))
     late.finish(2, "core")
     advance(2)
+    late.finish(0, "chips")
+    by_rows(0, dot_nt(dup[...], wu[...]))
+    late.finish(1, "chips")
     for kind in late.stages[2:-1]:
         late.finish(0, kind)
+    advance(2)
 
     def narrow(step):
         if step == 0:
@@ -706,6 +725,7 @@
         copy.start()
 
     by_rows(1, dot_nt(dq[...], wq[...]) + dot_nt(d_kv, wkv[...]))
+    late.finish(2, "chips")
     own_small[...] = jnp.zeros(own_small.shape, F32)
     per = width // 128
 
@@ -736,10 +756,12 @@
 
     for copy in narrow(0):
         copy.start()
-    late.finish(1, "chips")
-    late.finish(2, "chips")
+    for kind in late.stages[2:-1]:
+        late.finish(1, kind)
     advance(2)
     by_rows(2, dot(act[...], wd[...]) + vec_ref[5:6, :])
+    for kind in late.stages[2:-1]:
+        late.finish(2, kind)
     for copy in narrow_kv(0):
         copy.wait()
     sums = own_kv[me].astype(F32)
@@ -757,9 +779,6 @@
     row_small[net.row] = sums
     for copy in narrow(1):
         copy.start()
-    for c in (1, 2):
-        for kind in late.stages[2:-1]:
-            late.finish(c, kind)
     by_rows(3, dot_tn(mt[...], wo[...]))
 
     def layer_out(r, _):
@@ -868,9 +887,8 @@
 
     loads = [move(0, fin_in, fin), move(1, small_in, small), move(8, gkv_in, vkv)]
     loads += [move(2, lo_in, vlo), move(3, ig_in, vig)]
-    for load in loads:
-        load.wait()
-    moves = [move(9, vlo, lo), move(10, vig, ig)]
+    loads[0].wait()
+    moves = []
 
     def piece(ch, q):
         return fin[ch, q // 2, q % 2].astype(F32)
@@ -886,12 +904,17 @@
         for j in range(n_down):
             vdown[q * sub : (q + 1) * sub, j * QUARTER : (j + 1) * QUARTER] = piece(n_up + j, q)
     moves.append(move(5, vdown, gdown))
+    for load in loads[1:]:
+        load.wait()
+    moves += [move(9, vlo, lo), move(10, vig, ig)]
     for q in range(4):
         vout[:, span(0, q)] = piece(late, q)
-        vq[:, span(0, q)] = piece(late + 1, q)
-        if q < 2:
-            vout[:, span(CHUNK, q)] = piece(late + 2, q)
-            vq[:, span(CHUNK, q)] = piece(late + 2, q + 2)
+        if q < 3:
+            vq[:, span(0, q)] = piece(late + 1, q)
+            vq[:, span(3 * QUARTER, q)] = piece(late + 2, q)
+        else:
+            vout[:, span(CHUNK, 0)] = piece(late + 1, q)
+            vout[:, span(CHUNK, 1)] = piece(late + 2, q)
     moves += [move(6, vout, gout), move(7, vq, gq), move(11, vkv, gkv)]
     at = 0
     for size, ref in zip(sizes[:-1], vectors):

time: 113 us -> 107 us (0.947)
  Pallas kernels: 111 us -> 106 us
    pallas_call x1, Pallas kernels: 107 us -> 102 us  [layer(): pl.pallas_call(functools.partial(layer_kernel, a, b), out_shape=[shape((t...]
where the time goes in v5:
time: 107 us
  Pallas kernels  106 us (99%)
    pallas_call x1, Pallas kernels, layer(): pl.pallas_call(functools.partial(layer_kernel, a, b), out_shape=[shape((t...  102 us
    pallas_call x1, Pallas kernels, finish(): pl.pallas_call(functools.partial(finish_kernel, hidden // CHUNK, sizes),...  4.36 us

profile of v5, /device:TPU:0, one launch (start us, length us, event | category | flops | bytes accessed | tf_op | source)
XLA Modules:
  0.0 107.1 jit_solution(18250513583282121238)
XLA Ops:
  0.7 101.9 %layer.1 = (bf16[512,768]{1,0:T(8,128)(2,1)}, bf16[512,768]{1,0:T(8,128)(2,1)}, bf16[15,2,2,96,128]{4,3,2,1,0:T(8,128)(2,1)}, f32[64,128]{1,0:T(8,128)}, f32[96,128]{1,0:T(8,128)}) custom-call(s32[4,4]{1,0:T(4,128)} %len_ref.1, bf16[512,768]{1,0:T(8,128)(2,1)} %bitcast.4, bf16[512,768]{1,0:T(8,128)(2,1)} %bitcast.5, f32[768]{0:T(1024)} %fg_ref.1, ...), custom_call_target="tpu_custom_call" | custom-call | tf_op jit(solution)/shard_map/layer/pallas_call | solution.py:863
  102.6 4.4 %finish.1 = (bf16[512,768]{1,0:T(8,128)(2,1)}, bf16[512,768]{1,0:T(8,128)(2,1)}, f32[96,3072]{1,0:T(8,128)}, f32[384,768]{1,0:T(8,128)}, f32[96,768]{1,0:T(8,128...) custom-call(bf16[512,768]{1,0:T(8,128)(2,1)} %get-tuple-element.37.l, ...), custom_call_target="tpu_custom_call" | custom-call | tf_op jit(solution)/shard_map/finish/pallas_call | solution.py:934

commit v6 on v5

--- a/solution.py
+++ b/solution.py
@@ -875,7 +875,8 @@
 
 
 def finish_kernel(n_up, sizes, lo_in, ig_in, fin_in, small_in, gkv_in, lo, ig, gup, gdown, gout, gq, gkv, *rest):
-    vectors, (fin, small, vlo, vig, vup, vdown, vout, vq, vkv, sem) = rest[: len(sizes)], rest[len(sizes) :]
+    k = len(sizes)
+    vectors, held, (fin, small, vlo, vig, vup, vdown, vout, vq, vkv, sem) = rest[:k], rest[k : 2 * k], rest[2 * k :]
     sub, width = gout.shape
     n_down = width // QUARTER
     late = n_up + n_down
@@ -885,10 +886,17 @@
         copy.start()
         return copy
 
-    loads = [move(0, fin_in, fin), move(1, small_in, small), move(8, gkv_in, vkv)]
+    loads = [move(1, small_in, small), move(0, fin_in, fin), move(8, gkv_in, vkv)]
     loads += [move(2, lo_in, vlo), move(3, ig_in, vig)]
     loads[0].wait()
-    moves = []
+    at = 0
+    for size, ref in zip(sizes[:-1], held):
+        for i in range(size // 128):
+            ref[i * 128 : (i + 1) * 128] = small[at + i, :]
+        at += size // 128
+    held[-1][...] = held[-3][...]
+    moves = [move(12 + i, src, dst) for i, (src, dst) in enumerate(zip(held, vectors))]
+    loads[1].wait()
 
     def piece(ch, q):
         return fin[ch, q // 2, q % 2].astype(F32)
@@ -904,7 +912,7 @@
         for j in range(n_down):
             vdown[q * sub : (q + 1) * sub, j * QUARTER : (j + 1) * QUARTER] = piece(n_up + j, q)
     moves.append(move(5, vdown, gdown))
-    for load in loads[1:]:
+    for load in loads[2:]:
         load.wait()
     moves += [move(9, vlo, lo), move(10, vig, ig)]
     for q in range(4):
@@ -916,12 +924,6 @@
             vout[:, span(CHUNK, 0)] = piece(late + 1, q)
             vout[:, span(CHUNK, 1)] = piece(late + 2, q)
     moves += [move(6, vout, gout), move(7, vq, gq), move(11, vkv, gkv)]
-    at = 0
-    for size, ref in zip(sizes[:-1], vectors):
-        for i in range(size // 128):
-            ref[i * 128 : (i + 1) * 128] = small[at + i, :]
-        at += size // 128
-    vectors[-1][...] = vectors[-3][...]
     for copy in moves:
         copy.wait()
 
@@ -936,9 +938,10 @@
         out_shape=[shape(lo.shape, BF), shape(ig.shape, BF)]
         + [shape(g, F32) for g in grads] + [shape((size,), F32) for size in sizes],
         in_specs=[hbm] * 5,
-        out_specs=[hbm] * 7 + [pl.BlockSpec(memory_space=pltpu.VMEM)] * len(sizes),
-        scratch_shapes=[pltpu.VMEM(fin.shape, BF), pltpu.VMEM(small.shape, F32), pltpu.VMEM(lo.shape, BF), pltpu.VMEM(ig.shape, BF)]
-        + [pltpu.VMEM(g, F32) for g in grads] + [pltpu.SemaphoreType.DMA((12,))],
+        out_specs=[hbm] * (7 + len(sizes)),
+        scratch_shapes=[pltpu.VMEM((size,), F32) for size in sizes]
+        + [pltpu.VMEM(fin.shape, BF), pltpu.VMEM(small.shape, F32), pltpu.VMEM(lo.shape, BF), pltpu.VMEM(ig.shape, BF)]
+        + [pltpu.VMEM(g, F32) for g in grads] + [pltpu.SemaphoreType.DMA((12 + len(sizes),))],
         compiler_params=pltpu.CompilerParams(vmem_limit_bytes=64 * 2**20),
         name="finish",
     )(lo, ig, fin, small, gkv)

time: 107 us -> 107 us (level)
  no operation moved by 1% of the time
where the time goes in v6:
time: 107 us
  Pallas kernels  106 us (99%)
    pallas_call x1, Pallas kernels, layer(): pl.pallas_call(functools.partial(layer_kernel, a, b), out_shape=[shape((t...  102 us
    pallas_call x1, Pallas kernels, finish(): pl.pallas_call(functools.partial(finish_kernel, hidden // CHUNK, sizes),...  3.85 us

profile of v6, /device:TPU:0, one launch (start us, length us, event | category | flops | bytes accessed | tf_op | source)
XLA Modules:
  0.0 106.6 jit_solution(3559181850104179888)
XLA Ops:
  0.7 101.9 %layer.1 = (bf16[512,768]{1,0:T(8,128)(2,1)}, bf16[512,768]{1,0:T(8,128)(2,1)}, bf16[15,2,2,96,128]{4,3,2,1,0:T(8,128)(2,1)}, f32[64,128]{1,0:T(8,128)}, f32[96,128]{1,0:T(8,128)}) custom-call(s32[4,4]{1,0:T(4,128)} %len_ref.1, bf16[512,768]{1,0:T(8,128)(2,1)} %bitcast.4, bf16[512,768]{1,0:T(8,128)(2,1)} %bitcast.5, f32[768]{0:T(1024)} %fg_ref.1, ...), custom_call_target="tpu_custom_call" | custom-call | tf_op jit(solution)/shard_map/layer/pallas_call | solution.py:863
  102.6 3.8 %finish.1 = (bf16[512,768]{1,0:T(8,128)(2,1)}, bf16[512,768]{1,0:T(8,128)(2,1)}, f32[96,3072]{1,0:T(8,128)}, f32[384,768]{1,0:T(8,128)}, f32[96,768]{1,0:T(8,128...) custom-call(bf16[512,768]{1,0:T(8,128)(2,1)} %get-tuple-element.37.l, ...), custom_call_target="tpu_custom_call" | custom-call | tf_op jit(solution)/shard_map/finish/pallas_call | solution.py:936
